TPU v7x, 32 devices: a whole 2x2x4 slice. The times are simulated.
32 devices in a mesh: grp: 1, gx: 32 (over z, y, x, core).
Axes of the slice: x: 2, y: 2, z: 4, core: 2. Of those that a mesh axis runs over, the one named last changes fastest.
Arguments:
- field: bfloat16 [256, 32, 2, 32, 256], P(('grp', 'gx')), may hold values from -6 to 6
- cotangent: bfloat16 [256, 32, 2, 32, 256], P(('grp', 'gx')), may hold values from -6 to 6
- spectral_weight: bfloat16 [2, 32, 32, 768, 24], P(None, None, None, 'gx'), may hold values from -4 to 4
- local_weight: bfloat16 [32, 32], replicated, may hold values from -1 to 1
Outputs:
- output: bfloat16 [256, 32, 2, 32, 256], P(('grp', 'gx'))
- grad_field: bfloat16 [256, 32, 2, 32, 256], P(('grp', 'gx'))
- grad_spectral: float32 [2, 32, 32, 768, 24], P(None, None, None, ('grp', 'gx'))
- grad_local: float32 [32, 32], P('grp')
All inputs are finite; a program needn't handle non-finite values.
Results may differ from a plain program's by a relative error of at most 0.0065.
Values sent between devices are 32-bit elements; how exact they have to be, the bound alone decides.
No kernel may reach another device: no remote copies, remote signals or barrier semaphores. Data moves between devices by JAX's collectives and lax.ppermute only.
A program may use at most 256 MiB of HBM per device.

v0:
```python
import math

import jax
import jax.numpy as jnp
from jax import lax
from jax.sharding import PartitionSpec as P

NX = 256
NY = 256
KY = 24
PAIRS = 32


def phases(length, kept):
    rows_idx = jnp.arange(length, dtype=jnp.int32)[:, None]
    cols_idx = jnp.arange(kept, dtype=jnp.int32)[None, :]
    freqs = jnp.where(cols_idx < kept // 2, cols_idx, cols_idx - kept)
    angles = (rows_idx * freqs % length).astype(jnp.float32) * (2.0 * math.pi / length)
    factor = 1.0 / math.sqrt(length)
    return (jnp.cos(angles) * factor, -jnp.sin(angles) * factor)


def spectral_rows(source, cosines, sines):
    real_part = source[:, :, 0]
    imag_part = source[:, :, 1]

    def product(operand, matrix):
        return jnp.einsum("xpcn,nk->xckp", operand, matrix, preferred_element_type=jnp.float32)

    out_re = product(real_part, cosines) - product(imag_part, sines)
    out_im = product(real_part, sines) + product(imag_part, cosines)
    stacked = jnp.stack([out_re, out_im], axis=1)
    return stacked.reshape(
        stacked.shape[0], 2, stacked.shape[2], stacked.shape[3] * stacked.shape[4]
    )


def modes_x(block, cosines, sines):

    def product(operand, matrix):
        return jnp.einsum("ncm,nk->cmk", operand, matrix, precision=lax.Precision.HIGHEST)

    out_re = product(block[:, 0], cosines) - product(block[:, 1], sines)
    out_im = product(block[:, 0], sines) + product(block[:, 1], cosines)
    return jnp.stack([out_re, out_im]).astype(jnp.bfloat16)


def spectral_mix(coeffs, grads, weights):

    def product(form, left_op, right_op):
        return jnp.einsum(form, left_op, right_op, preferred_element_type=jnp.float32)

    forward_form = "cmk,cdmk->dmk"
    adjoint_form = "dmk,cdmk->cmk"
    outer_form = "cmk,dmk->cdmk"
    mixed_re = product(forward_form, coeffs[0], weights[0]) - product(
        forward_form, coeffs[1], weights[1]
    )
    mixed_im = product(forward_form, coeffs[0], weights[1]) + product(
        forward_form, coeffs[1], weights[0]
    )
    back_re = product(adjoint_form, grads[0], weights[0]) + product(
        adjoint_form, grads[1], weights[1]
    )
    back_im = product(adjoint_form, grads[1], weights[0]) - product(
        adjoint_form, grads[0], weights[1]
    )
    grad_re = product(outer_form, coeffs[0], grads[0]) + product(outer_form, coeffs[1], grads[1])
    grad_im = product(outer_form, coeffs[0], grads[1]) - product(outer_form, coeffs[1], grads[0])
    mixed = jnp.stack([mixed_re, mixed_im]).astype(jnp.bfloat16)
    back = jnp.stack([back_re, back_im]).astype(jnp.bfloat16)
    return (mixed, back, jnp.stack([grad_re, grad_im]))


def spatial_x(coeffs, cosines, sines):
    real_part = coeffs[0].astype(jnp.float32)
    imag_part = coeffs[1].astype(jnp.float32)

    def product(operand, matrix):
        return jnp.einsum("cmk,nk->ncm", operand, matrix, precision=lax.Precision.HIGHEST)

    out_re = product(real_part, cosines) + product(imag_part, sines)
    out_im = product(imag_part, cosines) - product(real_part, sines)
    return jnp.stack([out_re, out_im], axis=1)


def spatial_y(block, cosines, sines, kept):
    shaped = block.reshape(block.shape[0], 2, block.shape[2], kept, block.shape[3] // kept)

    def product(operand, matrix):
        return jnp.einsum("xckp,nk->xpcn", operand, matrix, precision=lax.Precision.HIGHEST)

    out_re = product(shaped[:, 0], cosines) + product(shaped[:, 1], sines)
    out_im = product(shaped[:, 1], cosines) - product(shaped[:, 0], sines)
    return jnp.stack([out_re, out_im], axis=2)


def local(field, cotangent, spectral_weight, local_weight):
    cosines_y, sines_y = phases(field.shape[4], KY)
    low_cosines = cosines_y.astype(jnp.bfloat16)
    low_sines = sines_y.astype(jnp.bfloat16)
    field_rows = spectral_rows(field, low_cosines, low_sines)
    cot_rows = spectral_rows(cotangent, low_cosines, low_sines)
    field_cols = lax.all_to_all(field_rows, "gx", split_axis=3, concat_axis=0, tiled=True)
    cot_cols = lax.all_to_all(cot_rows, "gx", split_axis=3, concat_axis=0, tiled=True)
    cosines_x, sines_x = phases(field_cols.shape[0], spectral_weight.shape[4])
    field_hat = modes_x(field_cols, cosines_x, sines_x)
    cot_hat = modes_x(cot_cols, cosines_x, sines_x)
    mixed, back, grad_spectral = spectral_mix(field_hat, cot_hat, spectral_weight)
    mixed_cols = spatial_x(mixed, cosines_x, sines_x)
    back_cols = spatial_x(back, cosines_x, sines_x)
    mixed_rows = lax.all_to_all(mixed_cols, "gx", split_axis=0, concat_axis=3, tiled=True)
    back_rows = lax.all_to_all(back_cols, "gx", split_axis=0, concat_axis=3, tiled=True)
    local_term = jnp.einsum(
        "xprcn,cd->xprdn", field, local_weight, preferred_element_type=jnp.float32
    )
    output = (spatial_y(mixed_rows, cosines_y, sines_y, KY) + local_term).astype(jnp.bfloat16)
    local_back = jnp.einsum(
        "xprdn,cd->xprcn", cotangent, local_weight, preferred_element_type=jnp.float32
    )
    grad_field = (spatial_y(back_rows, cosines_y, sines_y, KY) + local_back).astype(jnp.bfloat16)
    partial_grad = jnp.einsum(
        "xprcn,xprdn->cd", field, cotangent, preferred_element_type=jnp.float32
    )
    norm_factor = 1.0 / math.sqrt(NX * NY * PAIRS * 2.0)
    grad_local = lax.psum(partial_grad, "gx") * norm_factor
    return (output, grad_field, grad_spectral, grad_local)


def solution(mesh):
    return jax.shard_map(
        local,
        mesh=mesh,
        in_specs=(
            P(("grp", "gx"), None, None, None, None),
            P(("grp", "gx"), None, None, None, None),
            P(None, None, None, "gx", None),
            P(),
        ),
        out_specs=(
            P(("grp", "gx"), None, None, None, None),
            P(("grp", "gx"), None, None, None, None),
            P(None, None, None, ("grp", "gx"), None),
            P("grp", None),
        ),
        check_vma=False,
    )
```

profile of v0, /device:TPU:0, one launch (start us, length us, event | category | flops | bytes accessed | tf_op | source)
XLA Modules:
  0.0 508.0 jit_solution(18115583021307054824)
XLA Ops:
  6.0 6.9 %fusion.19 = f32[24,8,32,32]{3,0,2,1:T(8,128)} fusion(bf16[8,32,2,32,256]{4,3,2,1,0:T(8,128)(2,1)} %param.4, s32[24]{0:T(128)S(1)} %compare_select_fusion), kind=kOutput, calls=%fused_computation.32 | convolution fusion | flops 100767744 | bytes 4980832 | tf_op jit(solution)/shard_map/xpcn,nk->xckp/dot_general | solution.py:28
  21.4 6.2 %subtract_bitcast_fusion.4 = f32[8,32,24,32]{1,2,3,0:T(8,128)S(1)} fusion(f32[24,8,32,32]{3,0,2,1:T(8,128)} %fusion.19, bf16[8,32,2,32,256]{4,3,2,1,0:T(8,128)(2,1)} %param.4, s32[24]{0:T(128)S(1)} %compare_select_fusion), kind=kOutput, calls=%fused_computation.71 | convolution fusion | flops 100958208 | bytes 8126560 | tf_op jit(solution)/shard_map/xpcn,nk->xckp/dot_general | solution.py:28
  38.6 6.0 %reshape.72 = f32[32,1,12288]{2,1,0:T(1,128)} reshape(f32[768,2,8,32]{3,2,1,0:T(8,128)} %bitcast.328) | data formatting | bytes 3145728
  44.6 7.6 %all-to-all-start = ((f32[32,1,12288]{2,1,0:T(1,128)}), f32[32,1,12288]{2,1,0:T(1,128)}, u32[]{:S(2)}, u32[]{:S(2)}) async-start(f32[32,1,12288]{2,1,0:T(1,128)} %reshape.72), calls=%async_computation | async-start | bytes 3145728 | tf_op jit(solution)/shard_map/all_to_all | solution.py:104
  57.5 6.9 %fusion.11 = f32[24,8,32,32]{3,0,2,1:T(8,128)} fusion(bf16[8,32,2,32,256]{4,3,2,1,0:T(8,128)(2,1)} %param.5, s32[24]{0:T(128)S(1)} %compare_select_fusion), kind=kOutput, calls=%fused_computation.24 | convolution fusion | flops 100767744 | bytes 4980832 | tf_op jit(solution)/shard_map/xpcn,nk->xckp/dot_general | solution.py:28
  75.0 6.2 %subtract_bitcast_fusion.3 = f32[8,32,24,32]{1,2,3,0:T(8,128)S(1)} fusion(f32[24,8,32,32]{3,0,2,1:T(8,128)} %fusion.11, bf16[8,32,2,32,256]{4,3,2,1,0:T(8,128)(2,1)} %param.5, s32[24]{0:T(128)S(1)} %compare_select_fusion), kind=kOutput, calls=%fused_computation.69 | convolution fusion | flops 100958208 | bytes 8126560 | tf_op jit(solution)/shard_map/xpcn,nk->xckp/dot_general | solution.py:28
  98.3 8.0 %fusion.69 = f32[32,32]{1,0:T(8,128)S(1)} fusion(bf16[8,32,2,32,256]{4,3,2,1,0:T(8,128)(2,1)} %param.5, bf16[8,32,2,32,256]{4,3,2,1,0:T(8,128)(2,1)} %param.4), kind=kOutput, calls=%fused_computation.92 | convolution fusion | flops 268435456 | bytes 16781312 | tf_op jit(solution)/shard_map/xprcn,xprdn->cd/dot_general | solution.py:122
  106.3 41.1 %psum.7 = f32[32,32]{1,0:T(8,128)S(1)} all-reduce(f32[32,32]{1,0:T(8,128)S(1)} %fusion.69), channel_id=1, replica_groups=mesh['grp'=1,'gx'=32] {'gx'}, use_global_device_ids=true, to_apply=%region_0.1 | all-reduce | flops 1024 | bytes 8192 | tf_op jit(solution)/shard_map/psum | solution.py:126
  147.4 9.3 %slice_bitcast_fusion.1 = (bf16[32,32,24,24]{1,3,2,0:T(8,128)(2,1)}, bf16[32,32,24,24]{1,3,2,0:T(8,128)(2,1)}) fusion(bf16[2,32,32,24,24]{2,4,3,1,0:T(8,128)(2,1)} %param.6), kind=kLoop, calls=%fused_computation.55 | loop fusion | bytes 4718592 | tf_op jit(solution)/shard_map/squeeze | solution.py:56
  156.7 11.6 %fusion.144 = f32[32,8,32,2,256]{4,0,3,2,1:T(8,128)} fusion(bf16[8,32,2,32,256]{4,3,2,1,0:T(8,128)(2,1)} %param.4, bf16[32,32]{1,0:T(8,128)(2,1)S(1)} %copy-done), kind=kOutput, calls=%fused_computation.170 | convolution fusion | flops 268435456 | bytes 25167872 | tf_op jit(solution)/shard_map/xprcn,cd->xprdn/dot_general | solution.py:114
  168.3 8.0 %fusion.142 = f32[32,8,32,2,256]{4,0,3,2,1:T(8,128)} fusion(bf16[8,32,2,32,256]{4,3,2,1,0:T(8,128)(2,1)S(1)} %bitcast.315, bf16[32,32]{1,0:T(8,128)(2,1)S(1)} %copy-done), kind=kOutput, calls=%fused_computation.168 | convolution fusion | flops 268435456 | bytes 25167872 | tf_op jit(solution)/shard_map/xprdn,cd->xprcn/dot_general | solution.py:118
  212.5 6.1 %fusion.25 = f32[24,24,1,32]{3,2,1,0:T(1,128)} fusion(bf16[32,24,24,1]{0,3,2,1:T(2,128)(2,1)S(1)} %copy.93, bf16[32,32,24,24]{1,3,2,0:T(8,128)(2,1)} %get-tuple-element.23), kind=kOutput, calls=%fused_computation.38 | convolution fusion | flops 1179648 | bytes 1290240 | tf_op jit(solution)/shard_map/cmk,cdmk->dmk/dot_general | solution.py:51
  218.6 6.1 %fusion.31 = f32[24,24,1,32]{3,2,1,0:T(1,128)} fusion(bf16[32,24,24,1]{0,3,2,1:T(2,128)(2,1)S(1)} %copy.93, bf16[32,32,24,24]{1,3,2,0:T(8,128)(2,1)} %get-tuple-element.22), kind=kOutput, calls=%fused_computation.44 | convolution fusion | flops 1179648 | bytes 1290240 | tf_op jit(solution)/shard_map/cmk,cdmk->dmk/dot_general | solution.py:51
  232.5 6.0 %reduce.10 = f32[32,12288]{1,0:T(8,128)S(1)} reduce(f32[32,1,12288]{2,1,0:T(1,128)} %all-to-all-done.2, f32[]{:T(128)} %broadcast.373), dimensions={1}, to_apply=%all_to_all.55.reduce_sub_computation | reduce | bytes 3145732 | tf_op jit(solution)/shard_map/all_to_all | solution.py:105
  264.5 6.0 %copy.65 = f32[256,2,32,24]{2,3,1,0:T(8,128)} copy(f32[256,2,32,24]{0,2,3,1:T(8,128)} %pad_maximum_fusion.2) | data formatting | bytes 3145728 | tf_op jit(solution)/shard_map/stack | solution.py:84
  276.5 6.3 %all-to-all-start.1 = ((f32[32,1,12288]{2,1,0:T(1,128)}), f32[32,1,12288]{2,1,0:T(1,128)}, u32[]{:S(2)}, u32[]{:S(2)}) async-start(f32[32,1,12288]{2,1,0:T(1,128)} %reshape.74), calls=%async_computation.1 | async-start | bytes 3145728 | tf_op jit(solution)/shard_map/all_to_all | solution.py:112
  290.1 12.1 %fusion.4 = (f32[24,24,32]{1,0,2:T(8,128)S(1)}, f32[24,24,32]{1,0,2:T(8,128)S(1)}, f32[24,24,32]{1,0,2:T(8,128)S(1)}, f32[24,24,32]{1,0,2:T(8,128)S(1)}) fusion(f32[24,24,32]{2,1,0:T(8,128)S(1)} %copy.156, bf16[2,32,32,24,24]{2,4,3,1,0:T(8,128)(2,1)} %param.6, f32[24,24,32]{2,1,0:T(8,128)} %copy.155), kind=kLoop, calls=%fused_computation.11 | loop fusion | flops 5824512 | bytes 2801664
  322.9 7.0 %pad_maximum_fusion = f32[2,32,32,24,24]{2,4,3,1,0:T(8,128)} fusion(f32[1,32,32,24,24]{2,4,3,1,0:T(8,128)S(1)} %get-tuple-element.33, f32[1,32,32,24,24]{2,4,3,1,0:T(8,128)S(1)} %get-tuple-element.32), kind=kLoop, calls=%fused_computation | loop fusion | flops 1179648 | bytes 9437184 | tf_op jit(solution)/shard_map/stack | solution.py:72
  329.9 6.1 %all-to-all-start.3 = ((f32[32,1,12288]{2,1,0:T(1,128)}), f32[32,1,12288]{2,1,0:T(1,128)}, u32[]{:S(2)}, u32[]{:S(2)}) async-start(f32[32,1,12288]{2,1,0:T(1,128)} %reshape.78), calls=%async_computation.3 | async-start | bytes 3145728 | tf_op jit(solution)/shard_map/all_to_all | solution.py:113
  336.0 6.0 %reduce.9 = f32[32,12288]{1,0:T(8,128)S(1)} reduce(f32[32,1,12288]{2,1,0:T(1,128)} %all-to-all-done.1, f32[]{:T(128)} %broadcast.373), dimensions={1}, to_apply=%all_to_all.52.reduce_sub_computation | reduce | bytes 3145732 | tf_op jit(solution)/shard_map/all_to_all | solution.py:112
  358.8 7.2 %fusion.47 = f32[256,8,32,32]{0,3,2,1:T(8,128)S(1)} fusion(f32[8,1,32,24,32]{4,3,2,0,1:T(8,128)S(1)} %copy.148, s32[24]{0:T(128)S(1)} %compare_select_fusion), kind=kOutput, calls=%fused_computation.62 | convolution fusion | flops 604071936 | bytes 9175136 | tf_op jit(solution)/shard_map/xckp,nk->xpcn/dot_general | solution.py:91
  366.0 9.8 %fusion.51 = f32[256,8,32,32]{0,3,2,1:T(8,128)} fusion(f32[8,1,32,24,32]{4,3,2,0,1:T(8,128)S(1)} %copy-done.4, s32[24]{0:T(128)S(1)} %compare_select_fusion), kind=kOutput, calls=%fused_computation.66 | convolution fusion | flops 604071936 | bytes 9175136 | tf_op jit(solution)/shard_map/xckp,nk->xpcn/dot_general | solution.py:91
  375.8 7.2 %subtract_bitcast_fusion.2 = f32[8,32,1,32,256]{4,1,3,0,2:T(8,128)S(1)} fusion(f32[256,8,32,32]{0,3,2,1:T(8,128)S(1)} %fusion.47, f32[8,1,32,24,32]{4,3,2,0,1:T(8,128)S(1)} %copy-done.4, s32[24]{0:T(128)S(1)} %compare_select_fusion), kind=kOutput, calls=%fused_computation.20 | convolution fusion | flops 606175232 | bytes 17563744 | tf_op jit(solution)/shard_map/xckp,nk->xpcn/dot_general | solution.py:91
  383.0 12.0 %add_bitcast_fusion.2 = f32[8,32,1,32,256]{4,1,3,0,2:T(8,128)} fusion(f32[256,8,32,32]{0,3,2,1:T(8,128)} %fusion.51, f32[8,1,32,24,32]{4,3,2,0,1:T(8,128)S(1)} %copy.148, s32[24]{0:T(128)S(1)} %compare_select_fusion), kind=kOutput, calls=%fused_computation.21 | convolution fusion | flops 606175232 | bytes 17563744 | tf_op jit(solution)/shard_map/xckp,nk->xpcn/dot_general | solution.py:91
  395.0 13.0 %fusion = bf16[8,32,2,32,256]{4,1,3,0,2:T(8,128)(2,1)} fusion(f32[8,32,1,32,256]{4,1,3,0,2:T(8,128)S(1)} %subtract_bitcast_fusion.2, f32[8,32,1,32,256]{4,1,3,0,2:T(8,128)} %add_bitcast_fusion.2, f32[32,8,32,2,256]{4,0,3,2,1:T(8,128)S(1)} %bitcast.319), kind=kLoop, calls=%fused_computation.2 | loop fusion | flops 12582912 | bytes 41943040 | tf_op jit(solution)/shard_map/convert_element_type | solution.py:117
  408.0 11.9 %copy.89 = bf16[8,32,2,32,256]{4,3,2,1,0:T(8,128)(2,1)} copy(bf16[8,32,2,32,256]{4,1,3,0,2:T(8,128)(2,1)} %fusion) | data formatting | bytes 16777216
  439.2 9.6 %fusion.41 = f32[256,8,32,32]{0,3,2,1:T(8,128)} fusion(f32[8,1,32,24,32]{4,3,2,0,1:T(8,128)S(1)} %copy.154, s32[24]{0:T(128)S(1)} %compare_select_fusion), kind=kOutput, calls=%fused_computation.56 | convolution fusion | flops 604071936 | bytes 9175136 | tf_op jit(solution)/shard_map/xckp,nk->xpcn/dot_general | solution.py:91
  452.3 11.2 %fusion.45 = f32[256,8,32,32]{0,3,2,1:T(8,128)} fusion(f32[8,1,32,24,32]{4,3,2,0,1:T(8,128)} %copy.153, s32[24]{0:T(128)S(1)} %compare_select_fusion), kind=kOutput, calls=%fused_computation.60 | convolution fusion | flops 604071936 | bytes 9175136 | tf_op jit(solution)/shard_map/xckp,nk->xpcn/dot_general | solution.py:91
  463.5 7.2 %subtract_bitcast_fusion.1 = f32[8,32,1,32,256]{4,1,3,0,2:T(8,128)S(1)} fusion(f32[256,8,32,32]{0,3,2,1:T(8,128)S(1)} %copy-done.3, f32[8,1,32,24,32]{4,3,2,0,1:T(8,128)S(1)} %copy-done.5, s32[24]{0:T(128)S(1)} %compare_select_fusion), kind=kOutput, calls=%fused_computation.18 | convolution fusion | flops 606175232 | bytes 17563744 | tf_op jit(solution)/shard_map/xckp,nk->xpcn/dot_general | solution.py:91
  470.8 12.0 %add_bitcast_fusion.1 = f32[8,32,1,32,256]{4,1,3,0,2:T(8,128)} fusion(f32[256,8,32,32]{0,3,2,1:T(8,128)} %fusion.45, f32[8,1,32,24,32]{4,3,2,0,1:T(8,128)S(1)} %copy.154, s32[24]{0:T(128)S(1)} %compare_select_fusion), kind=kOutput, calls=%fused_computation.19 | convolution fusion | flops 606175232 | bytes 17563744 | tf_op jit(solution)/shard_map/xckp,nk->xpcn/dot_general | solution.py:91
  482.8 12.8 %fusion.1 = bf16[8,32,2,32,256]{4,1,3,0,2:T(8,128)(2,1)} fusion(f32[8,32,1,32,256]{4,1,3,0,2:T(8,128)S(1)} %subtract_bitcast_fusion.1, f32[8,32,1,32,256]{4,1,3,0,2:T(8,128)} %add_bitcast_fusion.1, f32[32,8,32,2,256]{4,0,3,2,1:T(8,128)S(1)} %bitcast.317), kind=kLoop, calls=%fused_computation.4 | loop fusion | flops 12582912 | bytes 41943040 | tf_op jit(solution)/shard_map/convert_element_type | solution.py:121
  495.6 11.9 %copy.90 = bf16[8,32,2,32,256]{4,3,2,1,0:T(8,128)(2,1)} copy(bf16[8,32,2,32,256]{4,1,3,0,2:T(8,128)(2,1)} %fusion.1) | data formatting | bytes 16777216
  (133 shorter events, 201.1 us)
Async XLA Ops:
  0.6 156.0 %copy-start = (bf16[32,32]{1,0:T(8,128)(2,1)S(1)}, bf16[32,32]{1,0:T(8,128)(2,1)}, u32[]{:S(2)}) copy-start(bf16[32,32]{1,0:T(8,128)(2,1)} %param.7) | copy-start | bytes 6148
  0.7 12.3 %copy-start.2 = (bf16[8,32,2,32,256]{4,3,2,1,0:T(8,128)(2,1)S(1)}, bf16[8,32,2,32,256]{4,3,2,1,0:T(8,128)(2,1)}, u32[]{:S(2)}) copy-start(bf16[8,32,2,32,256]{4,3,2,1,0:T(8,128)(2,1)} %param.4) | copy-start | bytes 25165828
  44.6 131.7 %all-to-all-start = ((f32[32,1,12288]{2,1,0:T(1,128)}), f32[32,1,12288]{2,1,0:T(1,128)}, u32[]{:S(2)}, u32[]{:S(2)}) async-start(f32[32,1,12288]{2,1,0:T(1,128)} %reshape.72), calls=%async_computation | async-start | bytes 3145728 | tf_op jit(solution)/shard_map/all_to_all | solution.py:104
  147.4 20.9 %slice-start = ((s8[8388608]{0:T(1024)(128)(4,1)}), s8[4194304]{0:T(1024)(128)(4,1)S(1)}, s32[]{:S(2)}) async-start(s8[8388608]{0:T(1024)(128)(4,1)} %bitcast.314), calls=%async_computation.4 | async-start | bytes 8388608
  156.7 11.6 %slice-start.1 = ((s8[8388608]{0:T(1024)(128)(4,1)}), s8[4194304]{0:T(1024)(128)(4,1)S(1)}, s32[]{:S(2)}) async-start(s8[8388608]{0:T(1024)(128)(4,1)} %bitcast.314), calls=%async_computation.5 | async-start | bytes 8388608
  176.4 56.1 %all-to-all-start.2 = ((f32[32,1,12288]{2,1,0:T(1,128)}), f32[32,1,12288]{2,1,0:T(1,128)}, u32[]{:S(2)}, u32[]{:S(2)}) async-start(f32[32,1,12288]{2,1,0:T(1,128)} %reshape.76), calls=%async_computation.2 | async-start | bytes 3145728 | tf_op jit(solution)/shard_map/all_to_all | solution.py:105
  204.7 6.5 %copy-start.6 = (f32[256,1,32,24]{0,3,2,1:T(8,128)S(1)}, f32[256,1,32,24]{0,3,2,1:T(8,128)}, u32[]{:S(2)}) copy-start(f32[256,1,32,24]{0,3,2,1:T(8,128)} %copy.146) | copy-start | bytes 2359300
  212.2 12.5 %slice-start.12 = ((s8[4718592]{0:T(1024)(128)(4,1)}), s8[524288]{0:T(1024)(128)(4,1)S(1)}, s32[]{:S(2)}) async-start(s8[4718592]{0:T(1024)(128)(4,1)} %bitcast.334), calls=%async_computation.16 | async-start | bytes 1048576
  212.5 12.3 %slice-start.13 = ((s8[4718592]{0:T(1024)(128)(4,1)}), s8[4194304]{0:T(1024)(128)(4,1)S(1)}, s32[]{:S(2)}) async-start(s8[4718592]{0:T(1024)(128)(4,1)} %bitcast.334), calls=%async_computation.17 | async-start | bytes 8388608
  218.6 10.2 %slice-start.10 = ((s8[4718592]{0:T(1024)(128)(4,1)}), s8[4194304]{0:T(1024)(128)(4,1)S(1)}, s32[]{:S(2)}) async-start(s8[4718592]{0:T(1024)(128)(4,1)} %bitcast.332), calls=%async_computation.14 | async-start | bytes 8388608
  218.6 10.2 %slice-start.11 = ((s8[4718592]{0:T(1024)(128)(4,1)}), s8[524288]{0:T(1024)(128)(4,1)S(1)}, s32[]{:S(2)}) async-start(s8[4718592]{0:T(1024)(128)(4,1)} %bitcast.332), calls=%async_computation.15 | async-start | bytes 1048576
  276.5 53.4 %all-to-all-start.1 = ((f32[32,1,12288]{2,1,0:T(1,128)}), f32[32,1,12288]{2,1,0:T(1,128)}, u32[]{:S(2)}, u32[]{:S(2)}) async-start(f32[32,1,12288]{2,1,0:T(1,128)} %reshape.74), calls=%async_computation.1 | async-start | bytes 3145728 | tf_op jit(solution)/shard_map/all_to_all | solution.py:112
  329.9 90.0 %all-to-all-start.3 = ((f32[32,1,12288]{2,1,0:T(1,128)}), f32[32,1,12288]{2,1,0:T(1,128)}, u32[]{:S(2)}, u32[]{:S(2)}) async-start(f32[32,1,12288]{2,1,0:T(1,128)} %reshape.78), calls=%async_computation.3 | async-start | bytes 3145728 | tf_op jit(solution)/shard_map/all_to_all | solution.py:113
  358.8 7.2 %copy-start.4 = (f32[8,1,32,24,32]{4,3,2,0,1:T(8,128)S(1)}, f32[8,1,32,24,32]{4,3,2,0,1:T(8,128)}, u32[]{:S(2)}) copy-start(f32[8,1,32,24,32]{4,3,2,0,1:T(8,128)} %copy.147) | copy-start | bytes 2359300
  375.8 19.2 %slice-start.6 = ((s8[16777216]{0:T(1024)(128)(4,1)}), s8[4194304]{0:T(1024)(128)(4,1)S(1)}, s32[]{:S(2)}) async-start(s8[16777216]{0:T(1024)(128)(4,1)} %bitcast.318), calls=%async_computation.10 | async-start | bytes 8388608
  375.8 19.2 %slice-start.7 = ((s8[16777216]{0:T(1024)(128)(4,1)}), s8[4194304]{0:T(1024)(128)(4,1)S(1)}, s32[]{:S(2)}) async-start(s8[16777216]{0:T(1024)(128)(4,1)} %bitcast.318), calls=%async_computation.11 | async-start | bytes 8388608
  383.0 12.0 %slice-start.8 = ((s8[16777216]{0:T(1024)(128)(4,1)}), s8[4194304]{0:T(1024)(128)(4,1)S(1)}, s32[]{:S(2)}) async-start(s8[16777216]{0:T(1024)(128)(4,1)} %bitcast.318), calls=%async_computation.12 | async-start | bytes 8388608
  383.0 12.0 %slice-start.9 = ((s8[16777216]{0:T(1024)(128)(4,1)}), s8[4194304]{0:T(1024)(128)(4,1)S(1)}, s32[]{:S(2)}) async-start(s8[16777216]{0:T(1024)(128)(4,1)} %bitcast.318), calls=%async_computation.13 | async-start | bytes 8388608
  452.3 11.2 %copy-start.3 = (f32[256,8,32,32]{0,3,2,1:T(8,128)S(1)}, f32[256,8,32,32]{0,3,2,1:T(8,128)}, u32[]{:S(2)}) copy-start(f32[256,8,32,32]{0,3,2,1:T(8,128)} %fusion.41) | copy-start | bytes 25165828
  452.3 11.2 %copy-start.5 = (f32[8,1,32,24,32]{4,3,2,0,1:T(8,128)S(1)}, f32[8,1,32,24,32]{4,3,2,0,1:T(8,128)}, u32[]{:S(2)}) copy-start(f32[8,1,32,24,32]{4,3,2,0,1:T(8,128)} %copy.153) | copy-start | bytes 2359300
  463.5 19.2 %slice-start.2 = ((s8[16777216]{0:T(1024)(128)(4,1)}), s8[4194304]{0:T(1024)(128)(4,1)S(1)}, s32[]{:S(2)}) async-start(s8[16777216]{0:T(1024)(128)(4,1)} %bitcast.316), calls=%async_computation.6 | async-start | bytes 8388608
  463.5 19.2 %slice-start.3 = ((s8[16777216]{0:T(1024)(128)(4,1)}), s8[4194304]{0:T(1024)(128)(4,1)S(1)}, s32[]{:S(2)}) async-start(s8[16777216]{0:T(1024)(128)(4,1)} %bitcast.316), calls=%async_computation.7 | async-start | bytes 8388608
  470.8 12.0 %slice-start.4 = ((s8[16777216]{0:T(1024)(128)(4,1)}), s8[4194304]{0:T(1024)(128)(4,1)S(1)}, s32[]{:S(2)}) async-start(s8[16777216]{0:T(1024)(128)(4,1)} %bitcast.316), calls=%async_computation.8 | async-start | bytes 8388608
  470.8 12.0 %slice-start.5 = ((s8[16777216]{0:T(1024)(128)(4,1)}), s8[4194304]{0:T(1024)(128)(4,1)S(1)}, s32[]{:S(2)}) async-start(s8[16777216]{0:T(1024)(128)(4,1)} %bitcast.316), calls=%async_computation.9 | async-start | bytes 8388608
  482.8 24.8 %copy-start.1 = (bf16[32,32]{1,0:T(8,128)(2,1)S(1)}, bf16[32,32]{1,0:T(8,128)(2,1)}, u32[]{:S(2)}) copy-start(bf16[32,32]{1,0:T(8,128)(2,1)} %param.7) | copy-start | bytes 6148
where the time goes:
time: 517 us; the launch traced here: 508 us
  matrix products  191 us (37%)
  local copies, waits for them, and re-layouts  168 us (32%)
  other arithmetic  81.5 us (16%)
  blocking collectives  41.1 us (8%)
  starting transfers between devices  24.8 us (5%)
    unnamed x62, local copies, waits for them, and re-layouts  86.6 us
    dot_general x8, matrix products, product(): jnp.einsum('xckp,nk->xpcn', operand, matrix, precision=lax.Precision.HIGH...  76.1 us
    dot_general x8, matrix products, product(): jnp.einsum('xpcn,nk->xckp', operand, matrix, preferred_element_type=jnp.f...  44.9 us
    psum x1, blocking collectives, local(): grad_local = lax.psum(partial_grad, 'gx') * norm_factor  41.1 us
    another operation x6, local copies, waits for them, and re-layouts, spectral_rows(): stacked = jnp.stack([out_re, out_im], axis=1)  20.8 us
    dot_general x4, matrix products, product(): jnp.einsum(form, left_op, right_op, preferred_element_type=jnp.float32)  19.9 us
    dot_general x8, matrix products, product(): jnp.einsum('ncm,nk->cmk', operand, matrix, precision=lax.Precision.HIGHEST)  17.1 us
    convert_element_type x1, other arithmetic, local(): (spatial_y(mixed_rows, cosines_y, sines_y, KY) + local_term).astype(jnp.b...  13 us
  transfers between devices with their start and end apart: 4, of which 0 were waited for; matrix products, arithmetic and copies ran while one was open for 52% of the time, Pallas kernels for 0%

commit v1 on v0

--- a/solution.py
+++ b/solution.py
@@ -1,14 +1,22 @@
+import functools
 import math
+
+import numpy as np
 
 import jax
 import jax.numpy as jnp
 from jax import lax
+from jax.experimental import pallas as pl
+from jax.experimental.pallas import tpu as pltpu
 from jax.sharding import PartitionSpec as P
 
 NX = 256
 NY = 256
 KY = 24
 PAIRS = 32
+
+F32 = jnp.float32
+BF16 = jnp.bfloat16
 
 
 def phases(length, kept):
@@ -95,7 +103,7 @@
     return jnp.stack([out_re, out_im], axis=2)
 
 
-def local(field, cotangent, spectral_weight, local_weight):
+def local_plain(field, cotangent, spectral_weight, local_weight):
     cosines_y, sines_y = phases(field.shape[4], KY)
     low_cosines = cosines_y.astype(jnp.bfloat16)
     low_sines = sines_y.astype(jnp.bfloat16)
@@ -127,7 +135,552 @@
     return (output, grad_field, grad_spectral, grad_local)
 
 
+LANES = 256
+PER = 8
+SLOTS = 3
+GA = 8
+K2 = 48
+
+
+class Plane:
+    @staticmethod
+    def a(me, m, sign, n):
+        return me ^ m
+
+    @staticmethod
+    def b(me, s, sign, n):
+        return lax.rem(me + (GA * s * sign + n), n) if not isinstance(me, int) else (me + GA * s * sign) % n
+
+
+def np_tables(length, kept):
+    rows = np.arange(length)[:, None]
+    cols = np.arange(kept)[None, :]
+    freqs = np.where(cols < kept // 2, cols, cols - kept)
+    angles = ((rows * freqs) % length) * (2.0 * np.pi / length)
+    return (
+        (np.cos(angles) / np.sqrt(length)).astype(np.float32),
+        (-np.sin(angles) / np.sqrt(length)).astype(np.float32),
+    )
+
+
+def complex_rows(cos, sin):
+    return np.concatenate(
+        [
+            np.concatenate([cos.T, -sin.T], axis=1),
+            np.concatenate([sin.T, cos.T], axis=1),
+        ],
+        axis=0,
+    )
+
+
+def high_low(array):
+    high = array.astype(jnp.bfloat16)
+    low = (array - high.astype(np.float32)).astype(jnp.bfloat16)
+    return high, low
+
+
+def x_tables(route, n, cells):
+    cos, sin = np_tables(n * cells, 24)
+    forward, backward = [], []
+    for me in range(n):
+        blocks = []
+        for m in range(GA):
+            source = route.a(me, m, -1, n)
+            at = slice(source * cells, (source + 1) * cells)
+            blocks.append(complex_rows(cos[at], sin[at]))
+        table = np.concatenate(blocks, axis=1)
+        high, low = high_low(table)
+        forward.append(np.concatenate([high, low, high], axis=1))
+        backward.append(np.concatenate([high.T, low.T], axis=1))
+    return np.stack(forward), np.stack(backward)
+
+
+def nt(a, b):
+    return lax.dot_general(a, b, (((1,), (1,)), ((), ())), preferred_element_type=F32)
+
+
+def tn(a, b):
+    return lax.dot_general(a, b, (((0,), (0,)), ((), ())), preferred_element_type=F32)
+
+
+def nn(a, b):
+    return lax.dot_general(a, b, (((1,), (0,)), ((), ())), preferred_element_type=F32)
+
+
+def nn_full(a, b):
+    return lax.dot_general(
+        a, b, (((1,), (0,)), ((), ())), precision=lax.Precision.HIGHEST, preferred_element_type=F32
+    )
+
+
+def piece_place(route, me, m, s, slot, n):
+    owner = route.b(route.a(me, m, 1, n), s, 1, n)
+    q = owner * SLOTS + slot
+    return q // 4, lax.rem(q, 4)
+
+
+def rows_kernel(route, n, cells, gb, me_ref, src_ref, tab_ref, *rest):
+    outs, hold = rest[:GA], rest[GA]
+    x = pl.program_id(0)
+    groups = src_ref.shape[1] // PER
+    for g in range(groups):
+        total = None
+        for r in range(2):
+            tile = src_ref[0, g * PER : (g + 1) * PER, r].reshape(LANES, src_ref.shape[4])
+            part = nt(tab_ref[r], tile)
+            total = part if total is None else total + part
+        at = pl.ds(pl.multiple_of(x * K2, 8), K2)
+        hold[2 * g, at, :] = total[:, :128]
+        hold[2 * g + 1, at, :] = total[:, 128:]
+
+    @pl.when(x == cells - 1)
+    def _():
+        me = me_ref[0]
+        for m in range(GA):
+            for s in range(gb):
+                for slot in range(SLOTS):
+                    k, g = piece_place(route, me, m, s, slot, n)
+                    for r in range(2):
+                        at = (s * SLOTS + slot) * 2 * cells + r * cells
+                        for half in range(2):
+                            lanes = slice(half * 128, (half + 1) * 128)
+                            outs[m][at : at + cells, lanes] = hold[
+                                2 * g + half, pl.ds(k + r * KY, cells, stride=K2), :
+                            ]
+
+
+def rows_call(route, n, cells, gb, me, src, tab):
+    shape = src.shape
+    rows = gb * SLOTS * 2 * cells
+    return pl.pallas_call(
+        functools.partial(rows_kernel, route, n, cells, gb),
+        grid_spec=pltpu.PrefetchScalarGridSpec(
+            num_scalar_prefetch=1,
+            grid=(cells,),
+            in_specs=[
+                pl.BlockSpec((1,) + shape[1:], lambda i, me: (i, 0, 0, 0, 0)),
+                pl.BlockSpec(tab.shape, lambda i, me: (0, 0, 0)),
+            ],
+            out_specs=[pl.BlockSpec((rows, LANES), lambda i, me: (0, 0))] * GA,
+            scratch_shapes=[pltpu.VMEM((shape[1] // PER * 2, cells * K2, 128), F32)],
+        ),
+        out_shape=[jax.ShapeDtypeStruct((rows, LANES), F32)] * GA,
+        compiler_params=pltpu.CompilerParams(vmem_limit_bytes=24 * 2**20),
+        cost_estimate=pl.CostEstimate(flops=int(2e9), bytes_accessed=12 * 2**20, transcendentals=0),
+        name="rows",
+    )(me, src, tab)
+
+
+def partial_kernel(cells, gb, me_ref, tab_ref, *rest):
+    ins, outs = rest[:GA], rest[GA:]
+    table = tab_ref[0]
+    step = 2 * cells
+    for s in range(gb):
+        for slot in range(SLOTS):
+            at = (s * SLOTS + slot) * step
+            data = jnp.concatenate([ref[at : at + step, :] for ref in ins], axis=0)
+            high = data.astype(BF16)
+            low = (data - high.astype(F32)).astype(BF16)
+            outs[s][slot * K2 : (slot + 1) * K2, :] = nn(
+                table, jnp.concatenate([high, high, low], axis=0)
+            )
+
+
+def partial_call(cells, gb, me, tab, messages):
+    rows = gb * SLOTS * 2 * cells
+    spec = pl.BlockSpec((rows, LANES), lambda i, me: (0, 0))
+    out = pl.BlockSpec((SLOTS * K2, LANES), lambda i, me: (0, 0))
+    return pl.pallas_call(
+        functools.partial(partial_kernel, cells, gb),
+        grid_spec=pltpu.PrefetchScalarGridSpec(
+            num_scalar_prefetch=1,
+            grid=(1,),
+            in_specs=[pl.BlockSpec((1,) + tab.shape[1:], lambda i, me: (me[0], 0, 0))] + [spec] * GA,
+            out_specs=[out] * gb,
+        ),
+        out_shape=[jax.ShapeDtypeStruct((SLOTS * K2, LANES), F32)] * gb,
+        compiler_params=pltpu.CompilerParams(vmem_limit_bytes=24 * 2**20),
+        cost_estimate=pl.CostEstimate(flops=int(1e9), bytes_accessed=4 * 2**20, transcendentals=0),
+        name="partial_modes",
+    )(me, tab, *messages)
+
+
+def load_hat(parts, hat_ref, channels):
+    for slot in range(SLOTS):
+        at = slice(slot * K2, (slot + 1) * K2)
+        total = parts[0][at, :]
+        for part in parts[1:]:
+            total = total + part[at, :]
+        total = total.astype(BF16).astype(F32)
+        for p in range(PER):
+            hat_ref[slot * PER + p] = total[:, p * channels : (p + 1) * channels]
+
+
+def store_modes(hold, out_ref, channels):
+    for slot in range(SLOTS):
+        out_ref[slot * K2 : (slot + 1) * K2, :] = jnp.concatenate(
+            [hold[slot * PER + p] for p in range(PER)], axis=1
+        )
+
+
+def mix_kernel(gb, block, channels, kx, w_ref, extra_ref, *rest):
+    parts, (out_ref, hat_ref, hold) = rest[:gb], rest[gb:]
+    i = pl.program_id(0)
+
+    @pl.when(i == 0)
+    def _():
+        load_hat(parts, hat_ref, channels)
+
+    def body(j, carry):
+        mode = i * block + j
+        hat_re = hat_ref[mode, 0:kx, :]
+        hat_im = hat_ref[mode, kx : 2 * kx, :]
+        acc_re = jnp.zeros((kx, channels), F32)
+        acc_im = jnp.zeros((kx, channels), F32)
+        for c in range(channels):
+            w_re = w_ref[0, c, j].astype(F32)
+            w_im = w_ref[1, c, j].astype(F32)
+            f_re = hat_re[:, c : c + 1]
+            f_im = hat_im[:, c : c + 1]
+            acc_re += f_re * w_re - f_im * w_im
+            acc_im += f_re * w_im + f_im * w_re
+        hold[mode, 0:kx, :] = acc_re.astype(BF16).astype(F32)
+        hold[mode, kx : 2 * kx, :] = acc_im.astype(BF16).astype(F32)
+        return carry
+
+    lax.fori_loop(0, block, body, 0)
+
+    @pl.when(i == pl.num_programs(0) - 1)
+    def _():
+        store_modes(hold, out_ref, channels)
+        out_ref[SLOTS * K2 :, :] = extra_ref[...]
+
+
+def adjoint_kernel(gb, block, channels, kx, w_ref, *rest):
+    parts, (out_ref, hat_ref, hold) = rest[:gb], rest[gb:]
+    i = pl.program_id(0)
+
+    @pl.when(i == 0)
+    def _():
+        load_hat(parts, hat_ref, channels)
+
+    lane = lax.broadcasted_iota(jnp.int32, (kx, channels), 1)
+
+    def body(j, carry):
+        mode = i * block + j
+        hat_re = hat_ref[mode, 0:kx, :]
+        hat_im = hat_ref[mode, kx : 2 * kx, :]
+        acc_re = jnp.zeros((kx, channels), F32)
+        acc_im = jnp.zeros((kx, channels), F32)
+        for c in range(channels):
+            w_re = w_ref[0, c, j].astype(F32)
+            w_im = w_ref[1, c, j].astype(F32)
+            sum_re = jnp.sum(w_re * hat_re + w_im * hat_im, axis=1, keepdims=True)
+            sum_im = jnp.sum(w_re * hat_im - w_im * hat_re, axis=1, keepdims=True)
+            acc_re = jnp.where(lane == c, sum_re, acc_re)
+            acc_im = jnp.where(lane == c, sum_im, acc_im)
+        hold[mode, 0:kx, :] = acc_re.astype(BF16).astype(F32)
+        hold[mode, kx : 2 * kx, :] = acc_im.astype(BF16).astype(F32)
+        return carry
+
+    lax.fori_loop(0, block, body, 0)
+
+    @pl.when(i == pl.num_programs(0) - 1)
+    def _():
+        store_modes(hold, out_ref, channels)
+
+
+def mode_call(kernel, name, gb, weight, extra, parts):
+    _, channels, modes, kx, _ = weight.shape
+    block = 4
+    whole = lambda a: pl.BlockSpec(a.shape, lambda i: (0,) * a.ndim)
+    more = [extra] if extra is not None else []
+    rows = SLOTS * K2 + (extra.shape[0] if extra is not None else 0)
+    return pl.pallas_call(
+        functools.partial(kernel, gb, block, channels, kx),
+        grid=(modes // block,),
+        in_specs=[pl.BlockSpec((2, channels, block, kx, channels), lambda i: (0, 0, i, 0, 0))]
+        + [whole(a) for a in more]
+        + [whole(a) for a in parts],
+        out_specs=[
+            pl.BlockSpec((rows, LANES), lambda i: (0, 0)),
+            pl.BlockSpec((modes, 2 * kx, channels), lambda i: (0, 0, 0)),
+        ],
+        out_shape=[
+            jax.ShapeDtypeStruct((rows, LANES), F32),
+            jax.ShapeDtypeStruct((modes, 2 * kx, channels), F32),
+        ],
+        scratch_shapes=[pltpu.VMEM((modes, 2 * kx, channels), F32)],
+        compiler_params=pltpu.CompilerParams(vmem_limit_bytes=32 * 2**20),
+        cost_estimate=pl.CostEstimate(flops=int(5e9), bytes_accessed=12 * 2**20, transcendentals=0),
+        name=name,
+    )(weight, *more, *parts)
+
+
+def outer_kernel(block, channels, kx, f_ref, g_ref, out_ref):
+    def body(j, carry):
+        f_re = f_ref[j, 0:kx, :]
+        f_im = f_ref[j, kx : 2 * kx, :]
+        g_re = g_ref[j, 0:kx, :]
+        g_im = g_ref[j, kx : 2 * kx, :]
+        for c in range(channels):
+            a = f_re[:, c : c + 1]
+            b = f_im[:, c : c + 1]
+            out_ref[0, c, j] = a * g_re + b * g_im
+            out_ref[1, c, j] = a * g_im - b * g_re
+        return carry
+
+    lax.fori_loop(0, block, body, 0)
+
+
+def outer_call(f_hat, g_hat):
+    modes, two_kx, channels = f_hat.shape
+    kx = two_kx // 2
+    block = 4
+    spec = pl.BlockSpec((block, two_kx, channels), lambda i: (i, 0, 0))
+    return pl.pallas_call(
+        functools.partial(outer_kernel, block, channels, kx),
+        grid=(modes // block,),
+        in_specs=[spec, spec],
+        out_specs=pl.BlockSpec((2, channels, block, kx, channels), lambda i: (0, 0, i, 0, 0)),
+        out_shape=jax.ShapeDtypeStruct((2, channels, modes, kx, channels), F32),
+        compiler_params=pltpu.CompilerParams(vmem_limit_bytes=32 * 2**20),
+        cost_estimate=pl.CostEstimate(flops=int(5e9), bytes_accessed=20 * 2**20, transcendentals=0),
+        name="grad_modes",
+    )(f_hat, g_hat)
+
+
+def expand_kernel(cells, gb, extra, me_ref, tab_ref, *rest):
+    ins, outs = rest[:gb], rest[gb:]
+    table = tab_ref[0]
+    step = 2 * cells
+    for s in range(gb):
+        for slot in range(SLOTS):
+            data = ins[s][slot * K2 : (slot + 1) * K2, :].astype(BF16)
+            full = nn(table, jnp.concatenate([data, data], axis=0))
+            at = (s * SLOTS + slot) * step
+            for m in range(GA):
+                outs[m][at : at + step, :] = full[m * step : (m + 1) * step]
+    if extra:
+        total = ins[0][SLOTS * K2 :, :]
+        for s in range(1, gb):
+            total = total + ins[s][SLOTS * K2 :, :]
+        for m in range(GA):
+            outs[m][gb * SLOTS * step :, :] = total
+
+
+def expand_call(cells, gb, me, tab, parts):
+    extra = parts[0].shape[0] - SLOTS * K2
+    rows = gb * SLOTS * 2 * cells + extra
+    spec = pl.BlockSpec(parts[0].shape, lambda i, me: (0, 0))
+    out = pl.BlockSpec((rows, LANES), lambda i, me: (0, 0))
+    return pl.pallas_call(
+        functools.partial(expand_kernel, cells, gb, extra),
+        grid_spec=pltpu.PrefetchScalarGridSpec(
+            num_scalar_prefetch=1,
+            grid=(1,),
+            in_specs=[pl.BlockSpec((1,) + tab.shape[1:], lambda i, me: (me[0], 0, 0))] + [spec] * gb,
+            out_specs=[out] * GA,
+        ),
+        out_shape=[jax.ShapeDtypeStruct((rows, LANES), F32)] * GA,
+        compiler_params=pltpu.CompilerParams(vmem_limit_bytes=24 * 2**20),
+        cost_estimate=pl.CostEstimate(flops=int(1e9), bytes_accessed=4 * 2**20, transcendentals=0),
+        name="expand_cells",
+    )(me, tab, *parts)
+
+
+def cells_kernel(route, n, cells, gb, extra, me_ref, src_ref, tab_ref, w_ref, *rest):
+    ins = rest[:GA]
+    out_ref = rest[GA]
+    hold = rest[-1]
+    x = pl.program_id(0)
+
+    @pl.when(x == 0)
+    def _():
+        me = me_ref[0]
+        for m in range(GA):
+            for s in range(gb):
+                for slot in range(SLOTS):
+                    k, g = piece_place(route, me, m, s, slot, n)
+                    for r in range(2):
+                        at = (s * SLOTS + slot) * 2 * cells + r * cells
+                        for half in range(2):
+                            lanes = slice(half * 128, (half + 1) * 128)
+                            hold[2 * g + half, pl.ds(k + r * KY, cells, stride=K2), :] = ins[m][
+                                at : at + cells, lanes
+                            ]
+        if extra:
+            total = ins[0][gb * SLOTS * 2 * cells :, :]
+            for m in range(1, GA):
+                total = total + ins[m][gb * SLOTS * 2 * cells :, :]
+            rest[GA + 1][...] = total
+
+    for g in range(src_ref.shape[1] // PER):
+        at = pl.ds(pl.multiple_of(x * K2, 8), K2)
+        data = jnp.concatenate([hold[2 * g, at, :], hold[2 * g + 1, at, :]], axis=1)
+        high = data.astype(BF16)
+        low = (data - high.astype(F32)).astype(BF16)
+        stack = jnp.concatenate([high, high, low], axis=0)
+        for r in range(2):
+            tile = src_ref[0, g * PER : (g + 1) * PER, r].reshape(LANES, src_ref.shape[4])
+            total = tn(stack, tab_ref[r]) + nn(w_ref[...], tile)
+            out_ref[0, g * PER : (g + 1) * PER, r] = total.astype(BF16).reshape(
+                PER, LANES // PER, src_ref.shape[4]
+            )
+
+
+def cells_call(route, n, cells, gb, me, src, tab, mixer, messages):
+    shape = src.shape
+    extra = messages[0].shape[0] - gb * SLOTS * 2 * cells
+    big = pl.BlockSpec((1,) + shape[1:], lambda i, me: (i, 0, 0, 0, 0))
+    whole = lambda a: pl.BlockSpec(a.shape, lambda i, me: (0,) * a.ndim)
+    out_specs, out_shape = [big], [jax.ShapeDtypeStruct(shape, BF16)]
+    if extra:
+        out_specs.append(pl.BlockSpec((extra, LANES), lambda i, me: (0, 0)))
+        out_shape.append(jax.ShapeDtypeStruct((extra, LANES), F32))
+    return pl.pallas_call(
+        functools.partial(cells_kernel, route, n, cells, gb, extra),
+        grid_spec=pltpu.PrefetchScalarGridSpec(
+            num_scalar_prefetch=1,
+            grid=(cells,),
+            in_specs=[big, whole(tab), whole(mixer)] + [whole(a) for a in messages],
+            out_specs=out_specs,
+            scratch_shapes=[pltpu.VMEM((shape[1] // PER * 2, cells * K2, 128), F32)],
+        ),
+        out_shape=out_shape,
+        compiler_params=pltpu.CompilerParams(vmem_limit_bytes=32 * 2**20),
+        cost_estimate=pl.CostEstimate(flops=int(4e9), bytes_accessed=20 * 2**20, transcendentals=0),
+        name="cells",
+    )(me, src, tab, mixer, *messages)
+
+
+def pointwise_kernel(cells, channels, norm, f_ref, g_ref, out_ref, hold):
+    x = pl.program_id(0)
+    total = jnp.zeros((LANES, LANES), F32)
+    for g in range(f_ref.shape[1] // PER):
+        for r in range(2):
+            at = slice(g * PER, (g + 1) * PER)
+            left = f_ref[0, at, r].reshape(LANES, f_ref.shape[4])
+            right = g_ref[0, at, r].reshape(LANES, f_ref.shape[4])
+            total = total + nt(left, right)
+
+    @pl.when(x == 0)
+    def _():
+        hold[...] = total
+
+    @pl.when(x > 0)
+    def _():
+        hold[...] += total
+
+    @pl.when(x == cells - 1)
+    def _():
+        iota = lambda shape, dim: lax.broadcasted_iota(jnp.int32, shape, dim)
+        square = (LANES, LANES)
+        same = iota(square, 0) // channels == iota(square, 1) // channels
+        diagonal = jnp.where(same, hold[...], 0.0)
+        fold = (iota((channels, LANES), 1) % channels == iota((channels, LANES), 0)).astype(F32)
+        rows = nn_full(fold, diagonal)
+        spread = (iota(square, 0) % channels == iota(square, 1) % channels).astype(F32)
+        full = nn_full(rows, spread)
+        keep = iota((channels, LANES), 0) % PER == iota((channels, LANES), 1) // channels
+        full = jnp.where(keep, full, 0.0)
+        pick = (iota((8, channels), 1) // PER == iota((8, channels), 0)).astype(F32)
+        out_ref[...] = nn_full(pick, full) * norm
+
+
+def pointwise_call(cells, field, cotangent, norm):
+    shape = field.shape
+    big = pl.BlockSpec((1,) + shape[1:], lambda i: (i, 0, 0, 0, 0))
+    return pl.pallas_call(
+        functools.partial(pointwise_kernel, cells, shape[3], norm),
+        grid=(cells,),
+        in_specs=[big, big],
+        out_specs=pl.BlockSpec((8, LANES), lambda i: (0, 0)),
+        out_shape=jax.ShapeDtypeStruct((8, LANES), F32),
+        scratch_shapes=[pltpu.VMEM((LANES, LANES), F32)],
+        compiler_params=pltpu.CompilerParams(vmem_limit_bytes=24 * 2**20),
+        cost_estimate=pl.CostEstimate(flops=int(4e9), bytes_accessed=17 * 2**20, transcendentals=0),
+        name="pointwise",
+    )(field, cotangent)
+
+
+def local_kernels(n, field, cotangent, spectral_weight, local_weight):
+    cells = field.shape[0]
+    channels = field.shape[3]
+    gb = n // GA
+    me = lax.axis_index("gx").astype(jnp.int32)[None]
+    route_f = Plane
+    route_g = Plane
+
+    def send(route, kind, step, sign, array):
+        hop = route.a if kind == "a" else route.b
+        return lax.ppermute(array, "gx", [(i, hop(i, step, sign, n)) for i in range(n)])
+
+    cos_y, sin_y = np_tables(field.shape[4], KY)
+    table_y = complex_rows(cos_y, sin_y)
+    split_y = np.stack(np.split(table_y, 2, axis=1))
+    rows_table = jnp.asarray(split_y.astype(BF16))
+    high, low = high_low(split_y)
+    cells_table = jnp.asarray(
+        np.concatenate(
+            [np.swapaxes(high, 1, 2), np.swapaxes(low, 1, 2), np.swapaxes(high, 1, 2)], axis=2
+        ).swapaxes(1, 2)
+    )
+    forward_f, backward_f = x_tables(route_f, n, cells)
+    forward_g, backward_g = (forward_f, backward_f) if route_g is route_f else x_tables(route_g, n, cells)
+    eye = jnp.eye(PER, dtype=BF16)
+    mixer_g = jnp.kron(eye, local_weight)
+    mixer_f = jnp.kron(eye, local_weight.T)
+    weight = jnp.transpose(spectral_weight, (0, 1, 3, 4, 2))
+
+    def exchange(route, messages):
+        return [messages[0]] + [send(route, "a", m, 1, messages[m]) for m in range(1, GA)]
+
+    def gather(route, parts):
+        return [parts[0]] + [send(route, "b", s, 1, parts[s]) for s in range(1, gb)]
+
+    field_rows = exchange(route_f, rows_call(route_f, n, cells, gb, me, field, rows_table))
+    cot_rows = exchange(route_g, rows_call(route_g, n, cells, gb, me, cotangent, rows_table))
+    norm = 1.0 / math.sqrt(NX * NY * PAIRS * 2.0)
+    grad_part = pointwise_call(cells, field, cotangent, norm)
+
+    field_parts = gather(route_f, partial_call(cells, gb, me, jnp.asarray(forward_f), field_rows))
+    mixed, field_hat = mode_call(mix_kernel, "mix", gb, weight, grad_part, field_parts)
+    cot_parts = gather(route_g, partial_call(cells, gb, me, jnp.asarray(forward_g), cot_rows))
+    back, cot_hat = mode_call(adjoint_kernel, "adjoint", gb, weight, None, cot_parts)
+
+    mixed_all = [mixed] + [send(route_f, "b", s, -1, mixed) for s in range(1, gb)]
+    back_all = [back] + [send(route_g, "b", s, -1, back) for s in range(1, gb)]
+    grad_spectral = jnp.transpose(outer_call(field_hat, cot_hat), (0, 1, 4, 2, 3))
+
+    def exchange_back(route, messages):
+        return [messages[0]] + [send(route, "a", m, -1, messages[m]) for m in range(1, GA)]
+
+    mixed_rows = exchange_back(route_f, expand_call(cells, gb, me, jnp.asarray(backward_f), mixed_all))
+    back_rows = exchange_back(route_g, expand_call(cells, gb, me, jnp.asarray(backward_g), back_all))
+    output, grad_rows = cells_call(
+        route_f, n, cells, gb, me, field, cells_table, mixer_f, mixed_rows
+    )
+    (grad_field,) = cells_call(
+        route_g, n, cells, gb, me, cotangent, cells_table, mixer_g, back_rows
+    )
+    grad_local = grad_rows[: channels // PER].reshape(channels, channels)
+    return (output, grad_field, grad_spectral, grad_local)
+
+
 def solution(mesh):
+    n = mesh.shape["gx"]
+
+    def local(field, cotangent, spectral_weight, local_weight):
+        tiled = (
+            n == 32
+            and field.shape == (8, PAIRS, 2, 32, NY)
+            and spectral_weight.shape == (2, 32, 32, SLOTS * PER, 24)
+        )
+        if tiled:
+            return local_kernels(n, field, cotangent, spectral_weight, local_weight)
+        return local_plain(field, cotangent, spectral_weight, local_weight)
+
     return jax.shard_map(
         local,
         mesh=mesh,

time: 517 us -> 169 us (0.33); the launches traced: 508 us -> 169 us
  matrix products: 191 us -> 0 us
  local copies, waits for them, and re-layouts: 168 us -> 27 us
  other arithmetic: 81.5 us -> 1.11 us
  Pallas kernels: 0 us -> 62.4 us
  blocking collectives: 41.1 us -> 0 us
  waiting for transfers between devices: 0.01 us -> 30.2 us
  starting transfers between devices: 24.8 us -> 47.4 us
    dot_general x39 -> x0, matrix products: 191 us -> none  [the longest x8 76.1 us: product(): jnp.einsum('xckp,nk->xpcn', operand, matrix, precision=lax.Precision.HIGH...]
    unnamed x62 -> x44, local copies, waits for them, and re-layouts: 86.6 us -> 23.3 us
    pallas_call x0 -> x12, Pallas kernels: none -> 62.4 us  [the longest x2 17.8 us: mode_call(): pl.pallas_call(functools.partial(kernel, gb, block, channels, kx), grid=(...]
    ppermute x0 -> x40, starting transfers between devices: none -> 47.4 us  [send(): lax.ppermute(array, 'gx', [(i, hop(i, step, sign, n)) for i in range(n)])]
    psum x1 -> x0, blocking collectives: 41.1 us -> none  [local(): grad_local = lax.psum(partial_grad, 'gx') * norm_factor]
    another operation x10 -> x0, local copies, waits for them, and re-layouts: 32.2 us -> none  [the longest x6 20.8 us: spectral_rows(): stacked = jnp.stack([out_re, out_im], axis=1)]
    ppermute x0 -> x40, waiting for transfers between devices: none -> 30.2 us  [send(): lax.ppermute(array, 'gx', [(i, hop(i, step, sign, n)) for i in range(n)])]
    convert_element_type x2 -> x1, other arithmetic: 25.8 us -> 0.01 us  [local_kernels(): eye = jnp.eye(PER, dtype=BF16)]
  transfers between devices with their start and end apart: 4 -> 40, of which waited for: 0 -> 8; matrix products, arithmetic and copies ran while one was open for 52% -> 2% of each run, Pallas kernels for 0% -> 29%
where the time goes in v1:
time: 169 us
  Pallas kernels  62.4 us (37%)
  starting transfers between devices  47.4 us (28%)
  waiting for transfers between devices  30.2 us (18%)
  local copies, waits for them, and re-layouts  27 us (16%)
    ppermute x40, starting transfers between devices, send(): lax.ppermute(array, 'gx', [(i, hop(i, step, sign, n)) for i in range(n)])  47.4 us
    ppermute x40, waiting for transfers between devices, send(): lax.ppermute(array, 'gx', [(i, hop(i, step, sign, n)) for i in range(n)])  30.2 us
    unnamed x44, local copies, waits for them, and re-layouts  23.3 us
    pallas_call x2, Pallas kernels, mode_call(): pl.pallas_call(functools.partial(kernel, gb, block, channels, kx), grid=(...  17.8 us
    pallas_call x2, Pallas kernels, cells_call(): pl.pallas_call(functools.partial(cells_kernel, route, n, cells, gb, extra...  17.2 us
    pallas_call x1, Pallas kernels, outer_call(): pl.pallas_call(functools.partial(outer_kernel, block, channels, kx), grid...  10.4 us
    pallas_call x2, Pallas kernels, rows_call(): pl.pallas_call(functools.partial(rows_kernel, route, n, cells, gb), grid_...  8.6 us
    pallas_call x1, Pallas kernels, pointwise_call(): pl.pallas_call(functools.partial(pointwise_kernel, cells, shape[3], norm)...  4.76 us
  transfers between devices with their start and end apart: 40, of which 8 were waited for; matrix products, arithmetic and copies ran while one was open for 2% of the time, Pallas kernels for 29%

profile of v1, /device:TPU:0, one launch (start us, length us, event | category | flops | bytes accessed | tf_op | source)
XLA Modules:
  0.0 168.9 jit_solution(13069853775361977808)
XLA Ops:
  0.6 3.4 %copy-done = bf16[8,32,2,32,256]{4,3,2,1,0:T(8,128)(2,1)S(1)} copy-done((bf16[8,32,2,32,256]{4,3,2,1,0:T(8,128)(2,1)S(1)}, bf16[8,32,2,32,256]{4,3,2,1,0:T(8,128)(2,1)}, u32[]{:S(2)}) %copy-start) | copy-done | bytes 8388632
  4.8 4.3 %rows.3 = (f32[192,256]{1,0:T(8,128)S(1)}, f32[192,256]{1,0:T(8,128)S(1)}, f32[192,256]{1,0:T(8,128)S(1)}, f32[192,256]{1,0:T(8,128)S(1)}, f32[192,256]{1,0:T(8,...) custom-call(s32[1]{0:T(128)} %bitcast.me_ref, ...), custom_call_target="tpu_custom_call" | custom-call | flops 2000000000 | bytes 12582912 | tf_op jit(solution)/shard_map/rows/pallas_call | solution.py:255
  9.6 2.6 %collective-permute-start.21 = (f32[192,256]{1,0:T(8,128)S(1)}, f32[192,256]{1,0:T(8,128)S(1)}, u32[]{:S(2)}, u32[]{:S(2)}) collective-permute-start(f32[192,256]{1,0:T(8,128)S(1)} %get-tuple-element.74), channel_id=1, source_target_pairs={{0,2},{1,3},{2,0},{3,1},{4,6},{5,7},{6,4},{7,5},{8,10},{9,11},{10,... | collective-permute-start | bytes 589832 | tf_op jit(solution)/shard_map/ppermute | solution.py:617
  12.3 1.8 %collective-permute-start.23 = (f32[192,256]{1,0:T(8,128)S(1)}, f32[192,256]{1,0:T(8,128)S(1)}, u32[]{:S(2)}, u32[]{:S(2)}) collective-permute-start(f32[192,256]{1,0:T(8,128)S(1)} %get-tuple-element.76), channel_id=1, source_target_pairs={{0,4},{1,5},{2,6},{3,7},{4,0},{5,1},{6,2},{7,3},{8,12},{9,13},{10,... | collective-permute-start | bytes 589832 | tf_op jit(solution)/shard_map/ppermute | solution.py:617
  14.1 2.6 %collective-permute-start.25 = (f32[192,256]{1,0:T(8,128)S(1)}, f32[192,256]{1,0:T(8,128)S(1)}, u32[]{:S(2)}, u32[]{:S(2)}) collective-permute-start(f32[192,256]{1,0:T(8,128)S(1)} %get-tuple-element.78), channel_id=1, source_target_pairs={{0,6},{1,7},{2,4},{3,5},{4,2},{5,3},{6,0},{7,1},{8,14},{9,15},{10,... | collective-permute-start | bytes 589832 | tf_op jit(solution)/shard_map/ppermute | solution.py:617
  18.0 1.7 %collective-permute-start.26 = (f32[192,256]{1,0:T(8,128)S(1)}, f32[192,256]{1,0:T(8,128)S(1)}, u32[]{:S(2)}, u32[]{:S(2)}) collective-permute-start(f32[192,256]{1,0:T(8,128)S(1)} %get-tuple-element.79), channel_id=1, source_target_pairs={{0,7},{1,6},{2,5},{3,4},{4,3},{5,2},{6,1},{7,0},{8,15},{9,14},{10,... | collective-permute-start | bytes 589832 | tf_op jit(solution)/shard_map/ppermute | solution.py:617
  19.7 3.4 %copy-done.1 = bf16[8,32,2,32,256]{4,3,2,1,0:T(8,128)(2,1)S(1)} copy-done((bf16[8,32,2,32,256]{4,3,2,1,0:T(8,128)(2,1)S(1)}, bf16[8,32,2,32,256]{4,3,2,1,0:T(8,128)(2,1)}, u32[]{:S(2)}) %copy-start.1) | copy-done | bytes 8388632
  23.1 4.3 %rows.2 = (f32[192,256]{1,0:T(8,128)S(1)}, f32[192,256]{1,0:T(8,128)S(1)}, f32[192,256]{1,0:T(8,128)S(1)}, f32[192,256]{1,0:T(8,128)S(1)}, f32[192,256]{1,0:T(8,...) custom-call(s32[1]{0:T(128)} %bitcast.me_ref, ...), custom_call_target="tpu_custom_call" | custom-call | flops 2000000000 | bytes 12582912 | tf_op jit(solution)/shard_map/rows/pallas_call | solution.py:255
  29.3 2.1 %collective-permute-done.24.rest_5_ = f32[192,256]{1,0:T(8,128)S(1)} collective-permute-done((f32[192,256]{1,0:T(8,128)S(1)}, f32[192,256]{1,0:T(8,128)S(1)}, u32[]{:S(2)}, u32[]{:S(2)}) %collective-permute-start.24) | collective-permute-done | bytes 196640 | tf_op jit(solution)/shard_map/ppermute | solution.py:617
  31.3 2.2 %collective-permute-start.2 = (f32[192,256]{1,0:T(8,128)S(1)}, f32[192,256]{1,0:T(8,128)S(1)}, u32[]{:S(2)}, u32[]{:S(2)}) collective-permute-start(f32[192,256]{1,0:T(8,128)S(1)} %get-tuple-element.53), channel_id=1, source_target_pairs={{0,3},{1,2},{2,1},{3,0},{4,7},{5,6},{6,5},{7,4},{8,11},{9,10},{10,... | collective-permute-start | bytes 589832 | tf_op jit(solution)/shard_map/ppermute | solution.py:617
  36.9 1.7 %collective-permute-start.6 = (f32[192,256]{1,0:T(8,128)S(1)}, f32[192,256]{1,0:T(8,128)S(1)}, u32[]{:S(2)}, u32[]{:S(2)}) collective-permute-start(f32[192,256]{1,0:T(8,128)S(1)} %get-tuple-element.57), channel_id=1, source_target_pairs={{0,7},{1,6},{2,5},{3,4},{4,3},{5,2},{6,1},{7,0},{8,15},{9,14},{10,... | collective-permute-start | bytes 589832 | tf_op jit(solution)/shard_map/ppermute | solution.py:617
  39.0 1.6 collective-permute-start.27
  40.6 9.2 %collective-permute-done.3.rest_4_ = f32[192,256]{1,0:T(8,128)S(1)} collective-permute-done((f32[192,256]{1,0:T(8,128)S(1)}, f32[192,256]{1,0:T(8,128)S(1)}, u32[]{:S(2)}, u32[]{:S(2)}) %collective-permute-start.3) | collective-permute-done | bytes 196640 | tf_op jit(solution)/shard_map/ppermute | solution.py:617
  49.8 2.6 %collective-permute-start.28 = (f32[144,256]{1,0:T(8,128)S(1)}, f32[144,256]{1,0:T(8,128)S(1)}, u32[]{:S(2)}, u32[]{:S(2)}) collective-permute-start(f32[144,256]{1,0:T(8,128)S(1)} %get-tuple-element.82), channel_id=1, source_target_pairs={{0,16},{1,17},{2,18},{3,19},{4,20},{5,21},{6,22},{7,23},{8,24},{9,... | collective-permute-start | bytes 442376 | tf_op jit(solution)/shard_map/ppermute | solution.py:617
  52.4 3.1 %collective-permute-start.29 = (f32[144,256]{1,0:T(8,128)S(1)}, f32[144,256]{1,0:T(8,128)S(1)}, u32[]{:S(2)}, u32[]{:S(2)}) collective-permute-start(f32[144,256]{1,0:T(8,128)S(1)} %get-tuple-element.83), channel_id=1, source_target_pairs={{0,24},{1,25},{2,26},{3,27},{4,28},{5,29},{6,30},{7,31},{8,0},{9,1... | collective-permute-start | bytes 442376 | tf_op jit(solution)/shard_map/ppermute | solution.py:617
  55.4 3.4 %copy-done.2 = bf16[8,32,2,32,256]{4,3,2,1,0:T(8,128)(2,1)S(1)} copy-done((bf16[8,32,2,32,256]{4,3,2,1,0:T(8,128)(2,1)S(1)}, bf16[8,32,2,32,256]{4,3,2,1,0:T(8,128)(2,1)}, u32[]{:S(2)}) %copy-start.2) | copy-done | bytes 8388632
  58.8 4.8 %pointwise.1.extra_ref = f32[8,256]{1,0:T(8,128)S(1)} custom-call(bf16[8,32,2,32,256]{4,3,2,1,0:T(8,128)(2,1)S(1)} %copy-done.2, bf16[8,32,2,32,256]{4,3,2,1,0:T(8,128)(2,1)S(1)} %bitcast.9), custom_call_target="tpu_custom_call" | custom-call | flops 4000000000 | bytes 17825792 | tf_op jit(solution)/shard_map/pointwise/pallas_call | solution.py:594
  66.6 2.8 %collective-permute-start.9 = (f32[144,256]{1,0:T(8,128)S(1)}, f32[144,256]{1,0:T(8,128)S(1)}, u32[]{:S(2)}, u32[]{:S(2)}) collective-permute-start(f32[144,256]{1,0:T(8,128)S(1)} %get-tuple-element.61), channel_id=1, source_target_pairs={{0,24},{1,25},{2,26},{3,27},{4,28},{5,29},{6,30},{7,31},{8,0},{9,1... | collective-permute-start | bytes 442376 | tf_op jit(solution)/shard_map/ppermute | solution.py:617
  69.4 3.7 %copy-done.5 = bf16[2,32,32,24,24]{2,4,3,1,0:T(8,128)(2,1)S(1)} copy-done((bf16[2,32,32,24,24]{2,4,3,1,0:T(8,128)(2,1)S(1)}, bf16[2,32,32,24,24]{2,4,3,1,0:T(8,128)(2,1)}, u32[]{:S(2)}) %copy-start.5) | copy-done | bytes 2359320
  73.1 7.9 %adjoint.1 = (f32[144,256]{1,0:T(8,128)S(1)}, f32[24,48,32]{2,1,0:T(8,128)S(1)}) custom-call(bf16[2,32,24,24,32]{4,3,2,1,0:T(8,128)(2,1)S(1)} %bitcast.14, f32[144,256]{1,0:T(8,128)S(1)} %get-tuple-element.80.rest_0_, f32[144,256]{1,0:T(8,128)S(1)} %collective-permute-done.27.rest_1_, f32[144,256]{1,0:T(8,128)S(1)} %collective-permute-done.28.rest_2_, ...), custom_call_target="tpu_custom_call" | custom-call | flops 5000000000 | bytes 12582912 | tf_op jit(solution)/shard_map/adjoint/pallas_call | solution.py:399
  83.2 1.9 %collective-permute-start.32 = (f32[144,256]{1,0:T(8,128)S(1)}, f32[144,256]{1,0:T(8,128)S(1)}, u32[]{:S(2)}, u32[]{:S(2)}) collective-permute-start(f32[144,256]{1,0:T(8,128)S(1)} %get-tuple-element.84.rest_0_), channel_id=1, source_target_pairs={{0,8},{1,9},{2,10},{3,11},{4,12},{5,13},{6,14},{7,15},{8,16},{9,17... | collective-permute-start | bytes 442376 | tf_op jit(solution)/shard_map/ppermute | solution.py:617
  85.1 3.7 %copy-done.6 = bf16[2,32,32,24,24]{2,4,3,1,0:T(8,128)(2,1)S(1)} copy-done((bf16[2,32,32,24,24]{2,4,3,1,0:T(8,128)(2,1)S(1)}, bf16[2,32,32,24,24]{2,4,3,1,0:T(8,128)(2,1)}, u32[]{:S(2)}) %copy-start.6) | copy-done | bytes 2359320
  88.8 9.9 %mix.1 = (f32[152,256]{1,0:T(8,128)}, f32[24,48,32]{2,1,0:T(8,128)S(1)}) custom-call(bf16[2,32,24,24,32]{4,3,2,1,0:T(8,128)(2,1)S(1)} %bitcast.15, f32[8,256]{1,0:T(8,128)S(1)} %pointwise.1.extra_ref, f32[144,256]{1,0:T(8,128)S(1)} %get-tuple-element.58.rest_0_, f32[144,256]{1,0:T(8,128)S(1)} %collective-permute-done.7.rest_1_, ...), custom_call_target="tpu_custom_call" | custom-call | flops 5000000000 | bytes 12582912 | tf_op jit(solution)/shard_map/mix/pallas_call | solution.py:399
  98.7 1.9 %collective-permute-start.10 = (f32[152,256]{1,0:T(8,128)}, f32[152,256]{1,0:T(8,128)S(1)}, u32[]{:S(2)}, u32[]{:S(2)}) collective-permute-start(f32[152,256]{1,0:T(8,128)} %get-tuple-element.62.rest_0_), channel_id=1, source_target_pairs={{0,24},{1,25},{2,26},{3,27},{4,28},{5,29},{6,30},{7,31},{8,0},{9,1... | collective-permute-start | bytes 466952 | tf_op jit(solution)/shard_map/ppermute | solution.py:617
  103.5 1.9 %collective-permute-done.10.rest_1_ = f32[152,256]{1,0:T(8,128)S(1)} collective-permute-done((f32[152,256]{1,0:T(8,128)}, f32[152,256]{1,0:T(8,128)S(1)}, u32[]{:S(2)}, u32[]{:S(2)}) %collective-permute-start.10) | collective-permute-done | bytes 155680 | tf_op jit(solution)/shard_map/ppermute | solution.py:617
  105.4 8.3 %collective-permute-done.11.rest_2_ = f32[152,256]{1,0:T(8,128)S(1)} collective-permute-done((f32[152,256]{1,0:T(8,128)}, f32[152,256]{1,0:T(8,128)S(1)}, u32[]{:S(2)}, u32[]{:S(2)}) %collective-permute-start.11) | collective-permute-done | bytes 155680 | tf_op jit(solution)/shard_map/ppermute | solution.py:617
  125.3 2.2 %collective-permute-start.39 = (f32[192,256]{1,0:T(8,128)S(1)}, f32[192,256]{1,0:T(8,128)S(1)}, u32[]{:S(2)}, u32[]{:S(2)}) collective-permute-start(f32[192,256]{1,0:T(8,128)S(1)} %get-tuple-element.92), channel_id=1, source_target_pairs={{0,7},{1,6},{2,5},{3,4},{4,3},{5,2},{6,1},{7,0},{8,15},{9,14},{10,... | collective-permute-start | bytes 589832 | tf_op jit(solution)/shard_map/ppermute | solution.py:617
  128.3 10.4 %grad_modes.1 = f32[2,32,24,24,32]{4,3,2,1,0:T(8,128)} custom-call(f32[24,48,32]{2,1,0:T(8,128)S(1)} %get-tuple-element.93.f_ref, f32[24,48,32]{2,1,0:T(8,128)S(1)} %get-tuple-element.94.g_ref), custom_call_target="tpu_custom_call" | custom-call | flops 5000000000 | bytes 20971520 | tf_op jit(solution)/shard_map/grad_modes/pallas_call | solution.py:441
  144.1 8.6 %cells.3 = bf16[8,32,2,32,256]{4,3,2,1,0:T(8,128)(2,1)} custom-call(s32[1]{0:T(128)} %bitcast.me_ref, bf16[8,32,2,32,256]{4,3,2,1,0:T(8,128)(2,1)S(1)} %bitcast.11, bf16[2,144,256]{2,1,0:T(8,128)(2,1)S(1)} %copy-done.4, bf16[256,256]{1,0:T(8,128)(2,1)S(1)} %mul.47.w_ref, f32[192,256]{1,0:T(8,128)S(1)} %get-tuple-element.85.rest_0_, ...), custom_call_target="tpu_custom_call" | custom-call | flops 4000000000 | bytes 20971520 | tf_op jit(solution)/shard_map/cells/pallas_call | solution.py:541
  152.7 3.7 %collective-permute-done.16.rest_4_ = f32[200,256]{1,0:T(8,128)S(1)} collective-permute-done((f32[200,256]{1,0:T(8,128)S(1)}, f32[200,256]{1,0:T(8,128)S(1)}, u32[]{:S(2)}, u32[]{:S(2)}) %collective-permute-start.16) | collective-permute-done | bytes 204832 | tf_op jit(solution)/shard_map/ppermute | solution.py:617
  156.4 3.3 %collective-permute-done.17.rest_5_ = f32[200,256]{1,0:T(8,128)S(1)} collective-permute-done((f32[200,256]{1,0:T(8,128)S(1)}, f32[200,256]{1,0:T(8,128)S(1)}, u32[]{:S(2)}, u32[]{:S(2)}) %collective-permute-start.17) | collective-permute-done | bytes 204832 | tf_op jit(solution)/shard_map/ppermute | solution.py:617
  159.7 8.6 %cells.2 = (bf16[8,32,2,32,256]{4,3,2,1,0:T(8,128)(2,1)}, f32[8,256]{1,0:T(8,128)S(1)}) custom-call(s32[1]{0:T(128)} %bitcast.me_ref, bf16[8,32,2,32,256]{4,3,2,1,0:T(8,128)(2,1)S(1)} %bitcast.13, bf16[2,144,256]{2,1,0:T(8,128)(2,1)S(1)} %copy-done.4, bf16[256,256]{1,0:T(8,128)(2,1)S(1)} %mul.44.w_ref, f32[200,256]{1,0:T(8,128)S(1)} %get-tuple-element.63.rest_0_, ...), custom_call_target="tpu_custom_call" | custom-call | flops 4000000000 | bytes 20971520 | tf_op jit(solution)/shard_map/cells/pallas_call | solution.py:541
  (114 shorter events, 34.9 us)
Async XLA Ops:
  12.2 15.2 %collective-permute-start.22 = (f32[192,256]{1,0:T(8,128)S(1)}, f32[192,256]{1,0:T(8,128)S(1)}, u32[]{:S(2)}, u32[]{:S(2)}) collective-permute-start(f32[192,256]{1,0:T(8,128)S(1)} %get-tuple-element.75), channel_id=1, source_target_pairs={{0,3},{1,2},{2,1},{3,0},{4,7},{5,6},{6,5},{7,4},{8,11},{9,10},{10,... | collective-permute-start | bytes 589832 | tf_op jit(solution)/shard_map/ppermute | solution.py:617
  12.3 16.5 %collective-permute-start.23 = (f32[192,256]{1,0:T(8,128)S(1)}, f32[192,256]{1,0:T(8,128)S(1)}, u32[]{:S(2)}, u32[]{:S(2)}) collective-permute-start(f32[192,256]{1,0:T(8,128)S(1)} %get-tuple-element.76), channel_id=1, source_target_pairs={{0,4},{1,5},{2,6},{3,7},{4,0},{5,1},{6,2},{7,3},{8,12},{9,13},{10,... | collective-permute-start | bytes 589832 | tf_op jit(solution)/shard_map/ppermute | solution.py:617
  14.1 17.3 %collective-permute-start.24 = (f32[192,256]{1,0:T(8,128)S(1)}, f32[192,256]{1,0:T(8,128)S(1)}, u32[]{:S(2)}, u32[]{:S(2)}) collective-permute-start(f32[192,256]{1,0:T(8,128)S(1)} %get-tuple-element.77), channel_id=1, source_target_pairs={{0,5},{1,4},{2,7},{3,6},{4,1},{5,0},{6,3},{7,2},{8,13},{9,12},{10,... | collective-permute-start | bytes 589832 | tf_op jit(solution)/shard_map/ppermute | solution.py:617
  14.1 19.5 %collective-permute-start.25 = (f32[192,256]{1,0:T(8,128)S(1)}, f32[192,256]{1,0:T(8,128)S(1)}, u32[]{:S(2)}, u32[]{:S(2)}) collective-permute-start(f32[192,256]{1,0:T(8,128)S(1)} %get-tuple-element.78), channel_id=1, source_target_pairs={{0,6},{1,7},{2,4},{3,5},{4,2},{5,3},{6,0},{7,1},{8,14},{9,15},{10,... | collective-permute-start | bytes 589832 | tf_op jit(solution)/shard_map/ppermute | solution.py:617
  18.0 17.1 %collective-permute-start.26 = (f32[192,256]{1,0:T(8,128)S(1)}, f32[192,256]{1,0:T(8,128)S(1)}, u32[]{:S(2)}, u32[]{:S(2)}) collective-permute-start(f32[192,256]{1,0:T(8,128)S(1)} %get-tuple-element.79), channel_id=1, source_target_pairs={{0,7},{1,6},{2,5},{3,4},{4,3},{5,2},{6,1},{7,0},{8,15},{9,14},{10,... | collective-permute-start | bytes 589832 | tf_op jit(solution)/shard_map/ppermute | solution.py:617
  33.5 16.2 %collective-permute-start.3 = (f32[192,256]{1,0:T(8,128)S(1)}, f32[192,256]{1,0:T(8,128)S(1)}, u32[]{:S(2)}, u32[]{:S(2)}) collective-permute-start(f32[192,256]{1,0:T(8,128)S(1)} %get-tuple-element.54), channel_id=1, source_target_pairs={{0,4},{1,5},{2,6},{3,7},{4,0},{5,1},{6,2},{7,3},{8,12},{9,13},{10,... | collective-permute-start | bytes 589832 | tf_op jit(solution)/shard_map/ppermute | solution.py:617
  35.0 17.3 %collective-permute-start.4 = (f32[192,256]{1,0:T(8,128)S(1)}, f32[192,256]{1,0:T(8,128)S(1)}, u32[]{:S(2)}, u32[]{:S(2)}) collective-permute-start(f32[192,256]{1,0:T(8,128)S(1)} %get-tuple-element.55), channel_id=1, source_target_pairs={{0,5},{1,4},{2,7},{3,6},{4,1},{5,0},{6,3},{7,2},{8,13},{9,12},{10,... | collective-permute-start | bytes 589832 | tf_op jit(solution)/shard_map/ppermute | solution.py:617
  35.6 28.1 %collective-permute-start.5 = (f32[192,256]{1,0:T(8,128)S(1)}, f32[192,256]{1,0:T(8,128)S(1)}, u32[]{:S(2)}, u32[]{:S(2)}) collective-permute-start(f32[192,256]{1,0:T(8,128)S(1)} %get-tuple-element.56), channel_id=1, source_target_pairs={{0,6},{1,7},{2,4},{3,5},{4,2},{5,3},{6,0},{7,1},{8,14},{9,15},{10,... | collective-permute-start | bytes 589832 | tf_op jit(solution)/shard_map/ppermute | solution.py:617
  36.9 26.8 %collective-permute-start.6 = (f32[192,256]{1,0:T(8,128)S(1)}, f32[192,256]{1,0:T(8,128)S(1)}, u32[]{:S(2)}, u32[]{:S(2)}) collective-permute-start(f32[192,256]{1,0:T(8,128)S(1)} %get-tuple-element.57), channel_id=1, source_target_pairs={{0,7},{1,6},{2,5},{3,4},{4,3},{5,2},{6,1},{7,0},{8,15},{9,14},{10,... | collective-permute-start | bytes 589832 | tf_op jit(solution)/shard_map/ppermute | solution.py:617
  39.0 27.6 %collective-permute-start.27 = (f32[144,256]{1,0:T(8,128)S(1)}, f32[144,256]{1,0:T(8,128)S(1)}, u32[]{:S(2)}, u32[]{:S(2)}) collective-permute-start(f32[144,256]{1,0:T(8,128)S(1)} %get-tuple-element.81), channel_id=1, source_target_pairs={{0,8},{1,9},{2,10},{3,11},{4,12},{5,13},{6,14},{7,15},{8,16},{9,17... | collective-permute-start | bytes 442376 | tf_op jit(solution)/shard_map/ppermute | solution.py:617
  49.8 19.6 %collective-permute-start.28 = (f32[144,256]{1,0:T(8,128)S(1)}, f32[144,256]{1,0:T(8,128)S(1)}, u32[]{:S(2)}, u32[]{:S(2)}) collective-permute-start(f32[144,256]{1,0:T(8,128)S(1)} %get-tuple-element.82), channel_id=1, source_target_pairs={{0,16},{1,17},{2,18},{3,19},{4,20},{5,21},{6,22},{7,23},{8,24},{9,... | collective-permute-start | bytes 442376 | tf_op jit(solution)/shard_map/ppermute | solution.py:617
  52.4 17.0 %collective-permute-start.29 = (f32[144,256]{1,0:T(8,128)S(1)}, f32[144,256]{1,0:T(8,128)S(1)}, u32[]{:S(2)}, u32[]{:S(2)}) collective-permute-start(f32[144,256]{1,0:T(8,128)S(1)} %get-tuple-element.83), channel_id=1, source_target_pairs={{0,24},{1,25},{2,26},{3,27},{4,28},{5,29},{6,30},{7,31},{8,0},{9,1... | collective-permute-start | bytes 442376 | tf_op jit(solution)/shard_map/ppermute | solution.py:617
  65.5 17.6 %collective-permute-start.7 = (f32[144,256]{1,0:T(8,128)S(1)}, f32[144,256]{1,0:T(8,128)S(1)}, u32[]{:S(2)}, u32[]{:S(2)}) collective-permute-start(f32[144,256]{1,0:T(8,128)S(1)} %get-tuple-element.59), channel_id=1, source_target_pairs={{0,8},{1,9},{2,10},{3,11},{4,12},{5,13},{6,14},{7,15},{8,16},{9,17... | collective-permute-start | bytes 442376 | tf_op jit(solution)/shard_map/ppermute | solution.py:617
  65.6 19.5 %collective-permute-start.8 = (f32[144,256]{1,0:T(8,128)S(1)}, f32[144,256]{1,0:T(8,128)S(1)}, u32[]{:S(2)}, u32[]{:S(2)}) collective-permute-start(f32[144,256]{1,0:T(8,128)S(1)} %get-tuple-element.60), channel_id=1, source_target_pairs={{0,16},{1,17},{2,18},{3,19},{4,20},{5,21},{6,22},{7,23},{8,24},{9,... | collective-permute-start | bytes 442376 | tf_op jit(solution)/shard_map/ppermute | solution.py:617
  66.6 18.5 %collective-permute-start.9 = (f32[144,256]{1,0:T(8,128)S(1)}, f32[144,256]{1,0:T(8,128)S(1)}, u32[]{:S(2)}, u32[]{:S(2)}) collective-permute-start(f32[144,256]{1,0:T(8,128)S(1)} %get-tuple-element.61), channel_id=1, source_target_pairs={{0,24},{1,25},{2,26},{3,27},{4,28},{5,29},{6,30},{7,31},{8,0},{9,1... | collective-permute-start | bytes 442376 | tf_op jit(solution)/shard_map/ppermute | solution.py:617
  81.0 19.6 %collective-permute-start.30 = (f32[144,256]{1,0:T(8,128)S(1)}, f32[144,256]{1,0:T(8,128)S(1)}, u32[]{:S(2)}, u32[]{:S(2)}) collective-permute-start(f32[144,256]{1,0:T(8,128)S(1)} %get-tuple-element.84.rest_0_), channel_id=1, source_target_pairs={{0,24},{1,25},{2,26},{3,27},{4,28},{5,29},{6,30},{7,31},{8,0},{9,1... | collective-permute-start | bytes 442376 | tf_op jit(solution)/shard_map/ppermute | solution.py:617
  81.7 20.0 %collective-permute-start.31 = (f32[144,256]{1,0:T(8,128)S(1)}, f32[144,256]{1,0:T(8,128)S(1)}, u32[]{:S(2)}, u32[]{:S(2)}) collective-permute-start(f32[144,256]{1,0:T(8,128)S(1)} %get-tuple-element.84.rest_0_), channel_id=1, source_target_pairs={{0,16},{1,17},{2,18},{3,19},{4,20},{5,21},{6,22},{7,23},{8,24},{9,... | collective-permute-start | bytes 442376 | tf_op jit(solution)/shard_map/ppermute | solution.py:617
  83.2 18.5 %collective-permute-start.32 = (f32[144,256]{1,0:T(8,128)S(1)}, f32[144,256]{1,0:T(8,128)S(1)}, u32[]{:S(2)}, u32[]{:S(2)}) collective-permute-start(f32[144,256]{1,0:T(8,128)S(1)} %get-tuple-element.84.rest_0_), channel_id=1, source_target_pairs={{0,8},{1,9},{2,10},{3,11},{4,12},{5,13},{6,14},{7,15},{8,16},{9,17... | collective-permute-start | bytes 442376 | tf_op jit(solution)/shard_map/ppermute | solution.py:617
  100.6 19.1 %collective-permute-start.12 = (f32[152,256]{1,0:T(8,128)}, f32[152,256]{1,0:T(8,128)}, u32[]{:S(2)}, u32[]{:S(2)}) collective-permute-start(f32[152,256]{1,0:T(8,128)} %get-tuple-element.62.rest_0_), channel_id=1, source_target_pairs={{0,8},{1,9},{2,10},{3,11},{4,12},{5,13},{6,14},{7,15},{8,16},{9,17... | collective-permute-start | bytes 466952 | tf_op jit(solution)/shard_map/ppermute | solution.py:617
  102.8 21.6 %collective-permute-start.33 = (f32[192,256]{1,0:T(8,128)}, f32[192,256]{1,0:T(8,128)S(1)}, u32[]{:S(2)}, u32[]{:S(2)}) collective-permute-start(f32[192,256]{1,0:T(8,128)} %get-tuple-element.86), channel_id=1, source_target_pairs={{0,1},{1,0},{2,3},{3,2},{4,5},{5,4},{6,7},{7,6},{8,9},{9,8},{10,11... | collective-permute-start | bytes 589832 | tf_op jit(solution)/shard_map/ppermute | solution.py:617
  102.8 22.5 %collective-permute-start.34 = (f32[192,256]{1,0:T(8,128)}, f32[192,256]{1,0:T(8,128)S(1)}, u32[]{:S(2)}, u32[]{:S(2)}) collective-permute-start(f32[192,256]{1,0:T(8,128)} %get-tuple-element.87), channel_id=1, source_target_pairs={{0,2},{1,3},{2,0},{3,1},{4,6},{5,7},{6,4},{7,5},{8,10},{9,11},{10,... | collective-permute-start | bytes 589832 | tf_op jit(solution)/shard_map/ppermute | solution.py:617
  105.4 22.0 %collective-permute-start.35 = (f32[192,256]{1,0:T(8,128)S(1)}, f32[192,256]{1,0:T(8,128)S(1)}, u32[]{:S(2)}, u32[]{:S(2)}) collective-permute-start(f32[192,256]{1,0:T(8,128)S(1)} %get-tuple-element.88), channel_id=1, source_target_pairs={{0,3},{1,2},{2,1},{3,0},{4,7},{5,6},{6,5},{7,4},{8,11},{9,10},{10,... | collective-permute-start | bytes 589832 | tf_op jit(solution)/shard_map/ppermute | solution.py:617
  119.7 19.0 %collective-permute-start.37 = (f32[192,256]{1,0:T(8,128)S(1)}, f32[192,256]{1,0:T(8,128)S(1)}, u32[]{:S(2)}, u32[]{:S(2)}) collective-permute-start(f32[192,256]{1,0:T(8,128)S(1)} %get-tuple-element.90), channel_id=1, source_target_pairs={{0,5},{1,4},{2,7},{3,6},{4,1},{5,0},{6,3},{7,2},{8,13},{9,12},{10,... | collective-permute-start | bytes 589832 | tf_op jit(solution)/shard_map/ppermute | solution.py:617
  124.3 15.4 %collective-permute-start.38 = (f32[192,256]{1,0:T(8,128)S(1)}, f32[192,256]{1,0:T(8,128)S(1)}, u32[]{:S(2)}, u32[]{:S(2)}) collective-permute-start(f32[192,256]{1,0:T(8,128)S(1)} %get-tuple-element.91), channel_id=1, source_target_pairs={{0,6},{1,7},{2,4},{3,5},{4,2},{5,3},{6,0},{7,1},{8,14},{9,15},{10,... | collective-permute-start | bytes 589832 | tf_op jit(solution)/shard_map/ppermute | solution.py:617
  125.3 15.7 %collective-permute-start.39 = (f32[192,256]{1,0:T(8,128)S(1)}, f32[192,256]{1,0:T(8,128)S(1)}, u32[]{:S(2)}, u32[]{:S(2)}) collective-permute-start(f32[192,256]{1,0:T(8,128)S(1)} %get-tuple-element.92), channel_id=1, source_target_pairs={{0,7},{1,6},{2,5},{3,4},{4,3},{5,2},{6,1},{7,0},{8,15},{9,14},{10,... | collective-permute-start | bytes 589832 | tf_op jit(solution)/shard_map/ppermute | solution.py:617
  127.5 13.9 %collective-permute-start.13 = (f32[200,256]{1,0:T(8,128)S(1)}, f32[200,256]{1,0:T(8,128)S(1)}, u32[]{:S(2)}, u32[]{:S(2)}) collective-permute-start(f32[200,256]{1,0:T(8,128)S(1)} %get-tuple-element.64), channel_id=1, source_target_pairs={{0,1},{1,0},{2,3},{3,2},{4,5},{5,4},{6,7},{7,6},{8,9},{9,8},{10,11... | collective-permute-start | bytes 614408 | tf_op jit(solution)/shard_map/ppermute | solution.py:617
  127.5 15.3 %collective-permute-start.14 = (f32[200,256]{1,0:T(8,128)S(1)}, f32[200,256]{1,0:T(8,128)S(1)}, u32[]{:S(2)}, u32[]{:S(2)}) collective-permute-start(f32[200,256]{1,0:T(8,128)S(1)} %get-tuple-element.65), channel_id=1, source_target_pairs={{0,2},{1,3},{2,0},{3,1},{4,6},{5,7},{6,4},{7,5},{8,10},{9,11},{10,... | collective-permute-start | bytes 614408 | tf_op jit(solution)/shard_map/ppermute | solution.py:617
  138.7 14.0 %collective-permute-start.15 = (f32[200,256]{1,0:T(8,128)S(1)}, f32[200,256]{1,0:T(8,128)S(1)}, u32[]{:S(2)}, u32[]{:S(2)}) collective-permute-start(f32[200,256]{1,0:T(8,128)S(1)} %get-tuple-element.66), channel_id=1, source_target_pairs={{0,3},{1,2},{2,1},{3,0},{4,7},{5,6},{6,5},{7,4},{8,11},{9,10},{10,... | collective-permute-start | bytes 614408 | tf_op jit(solution)/shard_map/ppermute | solution.py:617
  139.7 16.7 %collective-permute-start.16 = (f32[200,256]{1,0:T(8,128)S(1)}, f32[200,256]{1,0:T(8,128)S(1)}, u32[]{:S(2)}, u32[]{:S(2)}) collective-permute-start(f32[200,256]{1,0:T(8,128)S(1)} %get-tuple-element.67), channel_id=1, source_target_pairs={{0,4},{1,5},{2,6},{3,7},{4,0},{5,1},{6,2},{7,3},{8,12},{9,13},{10,... | collective-permute-start | bytes 614408 | tf_op jit(solution)/shard_map/ppermute | solution.py:617
  141.0 18.6 %collective-permute-start.17 = (f32[200,256]{1,0:T(8,128)S(1)}, f32[200,256]{1,0:T(8,128)S(1)}, u32[]{:S(2)}, u32[]{:S(2)}) collective-permute-start(f32[200,256]{1,0:T(8,128)S(1)} %get-tuple-element.68), channel_id=1, source_target_pairs={{0,5},{1,4},{2,7},{3,6},{4,1},{5,0},{6,3},{7,2},{8,13},{9,12},{10,... | collective-permute-start | bytes 614408 | tf_op jit(solution)/shard_map/ppermute | solution.py:617
  141.4 18.2 %collective-permute-start.18 = (f32[200,256]{1,0:T(8,128)S(1)}, f32[200,256]{1,0:T(8,128)S(1)}, u32[]{:S(2)}, u32[]{:S(2)}) collective-permute-start(f32[200,256]{1,0:T(8,128)S(1)} %get-tuple-element.69), channel_id=1, source_target_pairs={{0,6},{1,7},{2,4},{3,5},{4,2},{5,3},{6,0},{7,1},{8,14},{9,15},{10,... | collective-permute-start | bytes 614408 | tf_op jit(solution)/shard_map/ppermute | solution.py:617
  142.8 16.8 %collective-permute-start.19 = (f32[200,256]{1,0:T(8,128)S(1)}, f32[200,256]{1,0:T(8,128)S(1)}, u32[]{:S(2)}, u32[]{:S(2)}) collective-permute-start(f32[200,256]{1,0:T(8,128)S(1)} %get-tuple-element.70), channel_id=1, source_target_pairs={{0,7},{1,6},{2,5},{3,4},{4,3},{5,2},{6,1},{7,0},{8,15},{9,14},{10,... | collective-permute-start | bytes 614408 | tf_op jit(solution)/shard_map/ppermute | solution.py:617
  (30 other events, 361.8 us)

commit v2 on v0

--- a/solution.py
+++ b/solution.py
@@ -1,14 +1,22 @@
+import functools
 import math
+
+import numpy as np
 
 import jax
 import jax.numpy as jnp
 from jax import lax
+from jax.experimental import pallas as pl
+from jax.experimental.pallas import tpu as pltpu
 from jax.sharding import PartitionSpec as P
 
 NX = 256
 NY = 256
 KY = 24
 PAIRS = 32
+
+F32 = jnp.float32
+BF16 = jnp.bfloat16
 
 
 def phases(length, kept):
@@ -95,7 +103,7 @@
     return jnp.stack([out_re, out_im], axis=2)
 
 
-def local(field, cotangent, spectral_weight, local_weight):
+def local_plain(field, cotangent, spectral_weight, local_weight):
     cosines_y, sines_y = phases(field.shape[4], KY)
     low_cosines = cosines_y.astype(jnp.bfloat16)
     low_sines = sines_y.astype(jnp.bfloat16)
@@ -127,7 +135,641 @@
     return (output, grad_field, grad_spectral, grad_local)
 
 
+LANES = 256
+PER = 8
+SLOTS = 3
+NEAR = 8
+G = 4
+K2 = 48
+CHUNK = SLOTS * K2
+EXTRA = 8
+MIB = 2**20
+VMEM = pl.BlockSpec(memory_space=pltpu.VMEM)
+SMEM = pl.BlockSpec(memory_space=pltpu.SMEM)
+HBM = pl.BlockSpec(memory_space=pltpu.HBM)
+
+
+def far(me, s):
+    return me ^ (NEAR * s)
+
+
+def np_tables(length, kept):
+    rows = np.arange(length)[:, None]
+    cols = np.arange(kept)[None, :]
+    freqs = np.where(cols < kept // 2, cols, cols - kept)
+    angles = ((rows * freqs) % length) * (2.0 * np.pi / length)
+    return (
+        (np.cos(angles) / np.sqrt(length)).astype(np.float32),
+        (-np.sin(angles) / np.sqrt(length)).astype(np.float32),
+    )
+
+
+def complex_rows(cos, sin):
+    return np.concatenate(
+        [
+            np.concatenate([cos.T, -sin.T], axis=1),
+            np.concatenate([sin.T, cos.T], axis=1),
+        ],
+        axis=0,
+    )
+
+
+def high_low(array):
+    high = array.astype(jnp.bfloat16)
+    low = (array - high.astype(np.float32)).astype(jnp.bfloat16)
+    return high, low
+
+
+def x_tables(n, cells):
+    cos, sin = np_tables(n * cells, 24)
+    forward, backward = [], []
+    for me in range(n):
+        blocks = []
+        for m in range(NEAR):
+            source = me // NEAR * NEAR + m
+            at = slice(source * cells, (source + 1) * cells)
+            blocks.append(complex_rows(cos[at], sin[at]))
+        table = np.concatenate(blocks, axis=1)
+        high, low = high_low(table)
+        forward.append(np.concatenate([high, low, high], axis=1))
+        backward.append(np.concatenate([high.T, low.T], axis=1))
+    return jnp.asarray(np.stack(forward)), jnp.asarray(np.stack(backward))
+
+
+def nt(a, b):
+    return lax.dot_general(a, b, (((1,), (1,)), ((), ())), preferred_element_type=F32)
+
+
+def tn(a, b):
+    return lax.dot_general(a, b, (((0,), (0,)), ((), ())), preferred_element_type=F32)
+
+
+def nn(a, b):
+    return lax.dot_general(a, b, (((1,), (0,)), ((), ())), preferred_element_type=F32)
+
+
+def nn_full(a, b):
+    return lax.dot_general(
+        a, b, (((1,), (0,)), ((), ())), precision=lax.Precision.HIGHEST, preferred_element_type=F32
+    )
+
+
+def iota(shape, dim):
+    return lax.broadcasted_iota(jnp.int32, shape, dim)
+
+
+def whole(a):
+    return pl.BlockSpec(a.shape, lambda *i: (0,) * a.ndim)
+
+
+def params(mib):
+    return pltpu.CompilerParams(vmem_limit_bytes=mib * MIB)
+
+
+def cost(flops, mib):
+    return pl.CostEstimate(flops=int(flops), bytes_accessed=int(mib * 2**20), transcendentals=0)
+
+
+def piece_places(me, cells, n):
+    for m in range(NEAR):
+        for s in range(G):
+            owner = far((me & -NEAR) + m, s)
+            for slot in range(SLOTS):
+                q = owner * SLOTS + slot
+                yield m, (s * SLOTS + slot) * 2 * cells, q >> 2, q & 3
+
+
+def message_shape(cells, extra=0):
+    return jax.ShapeDtypeStruct((NEAR * (G * SLOTS * 2 * cells + extra), LANES), F32)
+
+
+def messages(ref):
+    rows = ref.shape[0] // NEAR
+    return [ref.at[pl.ds(m * rows, rows)] for m in range(NEAR)]
+
+
+def fetch(src_ref, buffer, sems):
+    def copy(x):
+        return pltpu.make_async_copy(src_ref.at[x], buffer.at[x], sems.at[x])
+
+    for x in range(src_ref.shape[0]):
+        copy(x).start()
+    return copy
+
+
+def rows_kernel(n, me_ref, src_ref, tab_ref, *rest):
+    out_ref, hold, buffer, sems = rest
+    outs = messages(out_ref)
+    cells, pairs, _, _, length = src_ref.shape
+    copy = fetch(src_ref, buffer, sems)
+
+    def body(x, carry):
+        copy(x).wait()
+        at = pl.ds(pl.multiple_of(x * K2, 8), K2)
+        for g in range(pairs // PER):
+            total = None
+            for r in range(2):
+                tile = buffer[x, g * PER : (g + 1) * PER, r].reshape(LANES, length)
+                part = nt(tab_ref[r], tile)
+                total = part if total is None else total + part
+            hold[2 * g, at, :] = total[:, :128]
+            hold[2 * g + 1, at, :] = total[:, 128:]
+        return carry
+
+    lax.fori_loop(0, cells, body, 0)
+    for index, row, k, g in piece_places(me_ref[0], cells, n):
+        for r in range(2):
+            at = row + r * cells
+            for half in range(2):
+                outs[index][at : at + cells, half * 128 : (half + 1) * 128] = hold[
+                    2 * g + half, pl.ds(k + r * KY, cells, stride=K2), :
+                ]
+
+
+def rows_call(n, me, src, tab):
+    cells, pairs = src.shape[:2]
+    return pl.pallas_call(
+        functools.partial(rows_kernel, n),
+        in_specs=[SMEM, HBM, VMEM],
+        out_specs=VMEM,
+        out_shape=message_shape(cells),
+        scratch_shapes=[
+            pltpu.VMEM((pairs // PER * 2, cells * K2, 128), F32),
+            pltpu.VMEM(src.shape, BF16),
+            pltpu.SemaphoreType.DMA((cells,)),
+        ],
+        compiler_params=params(56),
+        cost_estimate=cost(6e9, 14),
+        name="rows",
+    )(me, src, tab)
+
+
+def partial_kernel(cells, tab_ref, in_ref, *outs):
+    ins = messages(in_ref)
+    table = tab_ref[...]
+    step = 2 * cells
+    for s in range(G):
+        for slot in range(SLOTS):
+            at = (s * SLOTS + slot) * step
+            data = jnp.concatenate([ref[at : at + step, :] for ref in ins], axis=0)
+            high = data.astype(BF16)
+            low = (data - high.astype(F32)).astype(BF16)
+            outs[s][slot * K2 : (slot + 1) * K2, :] = nn(
+                table, jnp.concatenate([high, high, low], axis=0)
+            )
+
+
+def partial_call(cells, tab, rows):
+    out = [jax.ShapeDtypeStruct((CHUNK, LANES), F32)] * G
+    return pl.pallas_call(
+        functools.partial(partial_kernel, cells),
+        in_specs=[VMEM] * 2,
+        out_specs=[VMEM] * G,
+        out_shape=out,
+        compiler_params=params(16),
+        cost_estimate=cost(1e9, 2),
+        name="partial_modes",
+    )(tab, rows)
+
+
+def pack_kernel(block, w_ref, out_ref, buffer, sems):
+    _, channels, modes, _, _ = w_ref.shape
+
+    def copy(i):
+        at = pl.ds(i * block, block)
+        return pltpu.make_async_copy(w_ref.at[:, :, at], buffer.at[:, :, at], sems.at[i])
+
+    for i in range(modes // block):
+        copy(i).start()
+
+    def body(i, carry):
+        copy(i).wait()
+        for j in range(block):
+            for r in range(2):
+                out_ref[r, i * block + j] = jnp.concatenate(
+                    [buffer[r, c, i * block + j].astype(F32) for c in range(channels)], axis=1
+                )
+        return carry
+
+    lax.fori_loop(0, modes // block, body, 0)
+
+
+def pack_call(weight):
+    _, channels, modes, kx, _ = weight.shape
+    block = 2
+    return pl.pallas_call(
+        functools.partial(pack_kernel, block),
+        in_specs=[HBM],
+        out_specs=VMEM,
+        out_shape=jax.ShapeDtypeStruct((2, modes, kx, channels * channels), F32),
+        scratch_shapes=[
+            pltpu.VMEM(weight.shape, BF16),
+            pltpu.SemaphoreType.DMA((modes // block,)),
+        ],
+        compiler_params=params(55),
+        cost_estimate=cost(6e9, 16),
+        name="pack_weight",
+    )(weight)
+
+
+def load_hat(parts, hat_ref, channels):
+    for slot in range(SLOTS):
+        at = slice(slot * K2, (slot + 1) * K2)
+        total = parts[0][at, :]
+        for part in parts[1:]:
+            total = total + part[at, :]
+        total = total.astype(BF16).astype(F32)
+        for p in range(PER):
+            hat_ref[slot * PER + p] = total[:, p * channels : (p + 1) * channels]
+
+
+def store_modes(hold, out_ref):
+    for slot in range(SLOTS):
+        out_ref[slot * K2 : (slot + 1) * K2, :] = jnp.concatenate(
+            [hold[slot * PER + p] for p in range(PER)], axis=1
+        )
+
+
+BLOCK = 4
+
+
+def mode_blocks(w_ref, hat_ref, spread_ref, write):
+    _, modes, kx, _ = w_ref.shape
+    channels = hat_ref.shape[2]
+
+    def body(i, carry):
+        at = pl.ds(i * BLOCK, BLOCK)
+        hats = hat_ref[at].reshape(BLOCK * 2 * kx, channels).astype(BF16)
+        wide = nn(hats, spread_ref[...])
+        pieces = []
+        for j in range(BLOCK):
+            re = wide[2 * j * kx : (2 * j + 1) * kx]
+            im = wide[(2 * j + 1) * kx : (2 * j + 2) * kx]
+            pieces.append((w_ref[0, i * BLOCK + j], w_ref[1, i * BLOCK + j], re, im))
+        write(i, pieces)
+        return carry
+
+    lax.fori_loop(0, modes // BLOCK, body, 0)
+
+
+def mix_kernel(w_ref, spread_ref, extra_ref, *rest):
+    parts, (out_ref, hat_ref, hold) = rest[:G], rest[G:]
+    channels = hat_ref.shape[2]
+    kx = w_ref.shape[2]
+    load_hat(parts, hat_ref, channels)
+
+    def fold(value):
+        total = value[:, :128]
+        for t in range(1, value.shape[1] // 128):
+            total = total + value[:, t * 128 : (t + 1) * 128]
+        out = total[:, :channels]
+        for t in range(1, 128 // channels):
+            out = out + total[:, t * channels : (t + 1) * channels]
+        return out.astype(BF16).astype(F32)
+
+    def write(i, pieces):
+        for j, (w_re, w_im, f_re, f_im) in enumerate(pieces):
+            hold[i * BLOCK + j, 0:kx, :] = fold(f_re * w_re - f_im * w_im)
+            hold[i * BLOCK + j, kx : 2 * kx, :] = fold(f_re * w_im + f_im * w_re)
+
+    mode_blocks(w_ref, hat_ref, spread_ref, write)
+    store_modes(hold, out_ref)
+    out_ref[CHUNK:, :] = extra_ref[...]
+
+
+def adjoint_kernel(w_ref, spread_ref, gather_ref, *rest):
+    parts, (out_ref, hat_ref, hold) = rest[:G], rest[G:]
+    channels = hat_ref.shape[2]
+    kx = w_ref.shape[2]
+    load_hat(parts, hat_ref, channels)
+
+    def write(i, pieces):
+        both = []
+        for w_re, w_im, g_re, g_im in pieces:
+            both += [w_re * g_re + w_im * g_im, w_re * g_im - w_im * g_re]
+        both = jnp.concatenate(both, axis=0)
+        high = both.astype(BF16)
+        low = (both - high.astype(F32)).astype(BF16)
+        total = nn(high, gather_ref[...]) + nn(low, gather_ref[...])
+        hold[pl.ds(i * BLOCK, BLOCK)] = (
+            total.astype(BF16).astype(F32).reshape(BLOCK, 2 * kx, channels)
+        )
+
+    mode_blocks(w_ref, hat_ref, spread_ref, write)
+    store_modes(hold, out_ref)
+
+
+def mode_call(kernel, name, channels, packed, more, extra, parts):
+    _, modes, kx, width = packed.shape
+    shape = (modes, 2 * kx, channels)
+    return pl.pallas_call(
+        kernel,
+        in_specs=[VMEM] * (1 + len(more) + len(parts)),
+        out_specs=[VMEM] * 2,
+        out_shape=[
+            jax.ShapeDtypeStruct((CHUNK + extra, LANES), F32),
+            jax.ShapeDtypeStruct(shape, F32),
+        ],
+        scratch_shapes=[pltpu.VMEM(shape, F32)],
+        compiler_params=params(16),
+        cost_estimate=cost(4e9, 6),
+        name=name,
+    )(packed, *more, *parts)
+
+
+def outer_kernel(f_ref, g_ref, out_ref, buffer, sems):
+    modes, two_kx, channels = f_ref.shape
+    kx = two_kx // 2
+
+    def copy(j):
+        return pltpu.make_async_copy(buffer.at[:, :, j], out_ref.at[:, :, j], sems.at[j])
+
+    def body(j, carry):
+        f_re = f_ref[j, 0:kx, :]
+        f_im = f_ref[j, kx : 2 * kx, :]
+        g_re = g_ref[j, 0:kx, :]
+        g_im = g_ref[j, kx : 2 * kx, :]
+        for c in range(channels):
+            a = f_re[:, c : c + 1]
+            b = f_im[:, c : c + 1]
+            buffer[0, c, j] = a * g_re + b * g_im
+            buffer[1, c, j] = a * g_im - b * g_re
+        copy(j).start()
+        return carry
+
+    def finish(j, carry):
+        copy(j).wait()
+        return carry
+
+    lax.fori_loop(0, modes, body, 0)
+    lax.fori_loop(0, modes, finish, 0)
+
+
+def outer_call(f_hat, g_hat):
+    modes, two_kx, channels = f_hat.shape
+    kx = two_kx // 2
+    shape = (2, channels, modes, kx, channels)
+    return pl.pallas_call(
+        outer_kernel,
+        in_specs=[VMEM] * 2,
+        out_specs=HBM,
+        out_shape=jax.ShapeDtypeStruct(shape, F32),
+        scratch_shapes=[pltpu.VMEM(shape, F32), pltpu.SemaphoreType.DMA((modes,))],
+        compiler_params=params(28),
+        cost_estimate=cost(11e9, 34),
+        name="grad_modes",
+    )(f_hat, g_hat)
+
+
+def expand_kernel(cells, extra, tab_ref, *rest):
+    ins, outs = rest[:G], messages(rest[G])
+    table = tab_ref[...]
+    step = 2 * cells
+    for s in range(G):
+        for slot in range(SLOTS):
+            data = ins[s][slot * K2 : (slot + 1) * K2, :].astype(BF16)
+            full = nn(table, jnp.concatenate([data, data], axis=0))
+            at = (s * SLOTS + slot) * step
+            for m in range(NEAR):
+                outs[m][at : at + step, :] = full[m * step : (m + 1) * step]
+    if extra:
+        total = ins[0][CHUNK:, :]
+        for ref in ins[1:]:
+            total = total + ref[CHUNK:, :]
+        for m in range(NEAR):
+            outs[m][G * SLOTS * step :, :] = total
+
+
+def expand_call(cells, tab, parts):
+    extra = parts[0].shape[0] - CHUNK
+    return pl.pallas_call(
+        functools.partial(expand_kernel, cells, extra),
+        in_specs=[VMEM] * (1 + len(parts)),
+        out_specs=VMEM,
+        out_shape=message_shape(cells, extra),
+        compiler_params=params(16),
+        cost_estimate=cost(1e9, 2),
+        name="expand_cells",
+    )(tab, *parts)
+
+
+def cells_kernel(n, extra, flip, me_ref, src_ref, tab_ref, w_ref, *rest):
+    ins = messages(rest[0])
+    out_ref = rest[1]
+    hold, mixer, buffer, tiles, in_sems, out_sems = rest[-6:]
+    cells, pairs, _, channels, length = src_ref.shape
+    copy = fetch(src_ref, buffer, in_sems)
+
+    for index, row, k, g in piece_places(me_ref[0], cells, n):
+        for r in range(2):
+            at = row + r * cells
+            for half in range(2):
+                hold[2 * g + half, pl.ds(k + r * KY, cells, stride=K2), :] = ins[index][
+                    at : at + cells, half * 128 : (half + 1) * 128
+                ]
+    if extra:
+        at = slice(ins[0].shape[0] - extra, ins[0].shape[0])
+        total = ins[0][at, :]
+        for ref in ins[1:]:
+            total = total + ref[at, :]
+        rest[2][...] = total
+    tall = (iota((LANES, channels), 0) % channels == iota((LANES, channels), 1)).astype(BF16)
+    rows = (nt if flip else nn)(tall, w_ref[...]).astype(BF16)
+    same = iota((LANES, LANES), 0) // channels == iota((LANES, LANES), 1) // channels
+    mixer[...] = jnp.where(same, nt(rows, tall), 0.0).astype(BF16)
+
+    def copy_out(x):
+        return pltpu.make_async_copy(tiles.at[x], out_ref.at[x], out_sems.at[x])
+
+    def body(x, carry):
+        copy(x).wait()
+        at = pl.ds(pl.multiple_of(x * K2, 8), K2)
+        for g in range(pairs // PER):
+            data = jnp.concatenate([hold[2 * g, at, :], hold[2 * g + 1, at, :]], axis=1)
+            high = data.astype(BF16)
+            low = (data - high.astype(F32)).astype(BF16)
+            stack = jnp.concatenate([high, high, low], axis=0)
+            for r in range(2):
+                tile = buffer[x, g * PER : (g + 1) * PER, r].reshape(LANES, length)
+                total = tn(stack, tab_ref[r]) + nn(mixer[...], tile)
+                tiles[x, g * PER : (g + 1) * PER, r] = total.astype(BF16).reshape(
+                    PER, channels, length
+                )
+        copy_out(x).start()
+        return carry
+
+    lax.fori_loop(0, cells, body, 0)
+    for x in range(cells):
+        copy_out(x).wait()
+
+
+def cells_call(n, extra, flip, me, src, tab, weight, rows):
+    cells, pairs = src.shape[:2]
+    out_shape = [jax.ShapeDtypeStruct(src.shape, BF16)]
+    if extra:
+        out_shape.append(jax.ShapeDtypeStruct((extra, LANES), F32))
+    return pl.pallas_call(
+        functools.partial(cells_kernel, n, extra, flip),
+        in_specs=[SMEM, HBM, VMEM, VMEM, VMEM],
+        out_specs=[HBM] + [VMEM] * (len(out_shape) - 1),
+        out_shape=out_shape,
+        scratch_shapes=[
+            pltpu.VMEM((pairs // PER * 2, cells * K2, 128), F32),
+            pltpu.VMEM((LANES, LANES), BF16),
+            pltpu.VMEM(src.shape, BF16),
+            pltpu.VMEM(src.shape, BF16),
+            pltpu.SemaphoreType.DMA((cells,)),
+            pltpu.SemaphoreType.DMA((cells,)),
+        ],
+        compiler_params=params(56),
+        cost_estimate=cost(9e9, 28),
+        name="cells",
+    )(me, src, tab, weight, rows)
+
+
+def pointwise_kernel(norm, f_ref, g_ref, out_ref, f_buffer, g_buffer, hold, f_sems, g_sems):
+    cells, pairs, _, channels, length = f_ref.shape
+    f_copy = fetch(f_ref, f_buffer, f_sems)
+    g_copy = fetch(g_ref, g_buffer, g_sems)
+    square = (LANES, LANES)
+    hold[...] = jnp.zeros(square, F32)
+
+    def body(x, carry):
+        f_copy(x).wait()
+        g_copy(x).wait()
+        total = hold[...]
+        for g in range(pairs // PER):
+            at = slice(g * PER, (g + 1) * PER)
+            for r in range(2):
+                left = f_buffer[x, at, r].reshape(LANES, length)
+                right = g_buffer[x, at, r].reshape(LANES, length)
+                total = total + nt(left, right)
+        hold[...] = total
+        return carry
+
+    lax.fori_loop(0, cells, body, 0)
+    same = iota(square, 0) // channels == iota(square, 1) // channels
+    diagonal = jnp.where(same, hold[...], 0.0)
+    fold = (iota((channels, LANES), 1) % channels == iota((channels, LANES), 0)).astype(F32)
+    rows = nn_full(fold, diagonal)
+    spread = (iota(square, 0) % channels == iota(square, 1) % channels).astype(F32)
+    full = nn_full(rows, spread)
+    keep = iota((channels, LANES), 0) % PER == iota((channels, LANES), 1) // channels
+    full = jnp.where(keep, full, 0.0)
+    pick = (iota((EXTRA, channels), 1) // PER == iota((EXTRA, channels), 0)).astype(F32)
+    out_ref[...] = nn_full(pick, full) * norm
+
+
+def pointwise_call(field, cotangent, norm):
+    cells = field.shape[0]
+    return pl.pallas_call(
+        functools.partial(pointwise_kernel, norm),
+        in_specs=[HBM] * 2,
+        out_specs=VMEM,
+        out_shape=jax.ShapeDtypeStruct((EXTRA, LANES), F32),
+        scratch_shapes=[
+            pltpu.VMEM(field.shape, BF16),
+            pltpu.VMEM(field.shape, BF16),
+            pltpu.VMEM((LANES, LANES), F32),
+            pltpu.SemaphoreType.DMA((cells,)),
+            pltpu.SemaphoreType.DMA((cells,)),
+        ],
+        compiler_params=params(56),
+        cost_estimate=cost(8e9, 20),
+        name="pointwise",
+    )(field, cotangent)
+
+
+def local_kernels(n, field, cotangent, spectral_weight, local_weight):
+    cells = field.shape[0]
+    channels = field.shape[3]
+    me = lax.axis_index("gx").astype(jnp.int32)[None]
+
+    def permute(array, hop):
+        return lax.ppermute(array, "gx", [(i, hop(i)) for i in range(n)])
+
+    planes = [list(range(first, first + NEAR)) for first in range(0, n, NEAR)]
+
+    def near_exchange(rows):
+        stacked = rows.reshape(NEAR, rows.shape[0] // NEAR, LANES)
+        moved = lax.all_to_all(stacked, "gx", 0, 0, axis_index_groups=planes, tiled=True)
+        return moved.reshape(rows.shape)
+
+    def hop(array, s):
+        return permute(array, lambda i: far(i, s))
+
+    def far_scatter(parts):
+        return [parts[0]] + [hop(parts[s], s) for s in (1, 2, 3)]
+
+    def far_gather(chunk):
+        got = hop(chunk, 2)
+        return [chunk, hop(chunk, 1), got, hop(got, 1)]
+
+    cos_y, sin_y = np_tables(field.shape[4], KY)
+    split_y = np.stack(np.split(complex_rows(cos_y, sin_y), 2, axis=1))
+    rows_table = jnp.asarray(split_y.astype(BF16))
+    high, low = high_low(split_y)
+    cells_table = jnp.asarray(np.concatenate([high, low, high], axis=1))
+    def own(table):
+        return lax.dynamic_index_in_dim(table, me[0], 0, keepdims=False)
+
+    forward, backward = map(own, x_tables(n, cells))
+    lanes = np.arange(channels * channels)
+    index = np.arange(channels)[:, None]
+    by_c = jnp.asarray((lanes // channels == index).astype(np.float32).astype(BF16))
+    by_d = jnp.asarray((lanes % channels == index).astype(np.float32).astype(BF16))
+    gather_c = jnp.asarray((lanes // channels == index).astype(np.float32).T.astype(BF16))
+    weight = jnp.transpose(spectral_weight, (0, 1, 3, 4, 2))
+    norm = 1.0 / math.sqrt(NX * NY * PAIRS * 2.0)
+
+    def after(arrays, *others):
+        return lax.optimization_barrier((arrays, others))[0]
+
+    field_rows = near_exchange(rows_call(n, me, field, rows_table))
+    cot_out = rows_call(n, me, cotangent, rows_table)
+    grad_part = pointwise_call(after(field, cot_out), cotangent, norm)
+    packed = pack_call(after(weight, grad_part))
+
+    field_sums = partial_call(cells, forward, after(field_rows, packed))
+    field_parts = far_scatter(field_sums)
+    cot_rows = near_exchange(after(cot_out, field_sums))
+    mixed, field_hat = mode_call(
+        mix_kernel, "mix", channels, packed, [by_c, grad_part], EXTRA, field_parts
+    )
+    cot_sums = partial_call(cells, forward, after(cot_rows, mixed))
+    cot_parts = far_scatter(cot_sums)
+    mixed_parts = after(far_gather(mixed), cot_parts)
+    mixed_rows = near_exchange(expand_call(cells, backward, mixed_parts))
+    back, cot_hat = mode_call(
+        adjoint_kernel, "adjoint", channels, packed, [by_d, gather_c], 0, cot_parts
+    )
+    outer = outer_call(field_hat, after(cot_hat, back))
+    grad_spectral = jnp.transpose(outer, (0, 1, 4, 2, 3))
+    back_parts = far_gather(back)
+    back_rows = near_exchange(expand_call(cells, backward, back_parts))
+    output, grad_rows = cells_call(
+        n, EXTRA, True, me, field, cells_table, local_weight, mixed_rows
+    )
+    (grad_field,) = cells_call(
+        n, 0, False, me, cotangent, cells_table, local_weight, back_rows
+    )
+    grad_local = grad_rows[: channels // PER].reshape(channels, channels)
+    return (output, grad_field, grad_spectral, grad_local)
+
+
 def solution(mesh):
+    n = mesh.shape["gx"]
+
+    def local(field, cotangent, spectral_weight, local_weight):
+        tiled = (
+            n == 32
+            and field.shape == (8, PAIRS, 2, 32, NY)
+            and spectral_weight.shape == (2, 32, 32, SLOTS * PER, 24)
+        )
+        if tiled:
+            return local_kernels(n, field, cotangent, spectral_weight, local_weight)
+        return local_plain(field, cotangent, spectral_weight, local_weight)
+
     return jax.shard_map(
         local,
         mesh=mesh,

time: 517 us -> 151 us (0.29); the launches traced: 508 us -> 151 us
  matrix products: 191 us -> 0 us
  local copies, waits for them, and re-layouts: 168 us -> 7.61 us
  other arithmetic: 81.5 us -> 0 us
  Pallas kernels: 0 us -> 68.1 us
  blocking collectives: 41.1 us -> 0 us
  waiting for transfers between devices: 0.01 us -> 40.5 us
  starting transfers between devices: 24.8 us -> 33.6 us
    dot_general x39 -> x0, matrix products: 191 us -> none  [the longest x8 76.1 us: product(): jnp.einsum('xckp,nk->xpcn', operand, matrix, precision=lax.Precision.HIGH...]
    unnamed x62 -> x12, local copies, waits for them, and re-layouts: 86.6 us -> 4.68 us
    pallas_call x0 -> x13, Pallas kernels: none -> 68.1 us  [the longest x2 20.9 us: cells_call(): pl.pallas_call(functools.partial(cells_kernel, n, extra, flip), in_specs=...]
    psum x1 -> x0, blocking collectives: 41.1 us -> none  [local(): grad_local = lax.psum(partial_grad, 'gx') * norm_factor]
    ppermute x0 -> x12, waiting for transfers between devices: none -> 40.4 us  [permute(): return lax.ppermute(array, 'gx', [(i, hop(i)) for i in range(n)])]
    another operation x10 -> x0, local copies, waits for them, and re-layouts: 32.2 us -> none  [the longest x6 20.8 us: spectral_rows(): stacked = jnp.stack([out_re, out_im], axis=1)]
    convert_element_type x2 -> x0, other arithmetic: 25.8 us -> none  [the longest x1 13 us: local(): (spatial_y(mixed_rows, cosines_y, sines_y, KY) + local_term).astype(jnp.b...]
    all_to_all x4 -> x0, other arithmetic: 23.9 us -> none  [the longest x1 5.98 us: local(): lax.all_to_all(mixed_cols, 'gx', split_axis=0, concat_axis=3, tiled=True)]
  transfers between devices with their start and end apart: 4 -> 16, of which waited for: 0 -> 9; matrix products, arithmetic and copies ran while one was open for 52% -> 2% of each run, Pallas kernels for 0% -> 32%
where the time goes in v2:
time: 151 us
  Pallas kernels  68.1 us (45%)
  waiting for transfers between devices  40.5 us (27%)
  starting transfers between devices  33.6 us (22%)
  local copies, waits for them, and re-layouts  7.61 us (5%)
    ppermute x12, waiting for transfers between devices, permute(): return lax.ppermute(array, 'gx', [(i, hop(i)) for i in range(n)])  40.4 us
    pallas_call x2, Pallas kernels, cells_call(): pl.pallas_call(functools.partial(cells_kernel, n, extra, flip), in_specs=...  20.9 us
    all_to_all x4, starting transfers between devices, near_exchange(): lax.all_to_all(stacked, 'gx', 0, 0, axis_index_groups=planes, tiled=True)  18.3 us
    ppermute x12, starting transfers between devices, permute(): return lax.ppermute(array, 'gx', [(i, hop(i)) for i in range(n)])  15.3 us
    pallas_call x2, Pallas kernels, rows_call(): pl.pallas_call(functools.partial(rows_kernel, n), in_specs=[SMEM, HBM, VM...  14.2 us
    pallas_call x1, Pallas kernels, outer_call(): pl.pallas_call(outer_kernel, in_specs=[VMEM] * 2, out_specs=HBM, out_shap...  8.81 us
    pallas_call x1, Pallas kernels, pointwise_call(): pl.pallas_call(functools.partial(pointwise_kernel, norm), in_specs=[HBM]...  7.75 us
    pallas_call x1, Pallas kernels, pack_call(): pl.pallas_call(functools.partial(pack_kernel, block), in_specs=[HBM], out...  6.24 us
  transfers between devices with their start and end apart: 16, of which 9 were waited for; matrix products, arithmetic and copies ran while one was open for 2% of the time, Pallas kernels for 32%

profile of v2, /device:TPU:0, one launch (start us, length us, event | category | flops | bytes accessed | tf_op | source)
XLA Modules:
  0.0 150.6 jit_solution(1282690394582032566)
XLA Ops:
  0.6 7.1 %rows.3 = f32[1536,256]{1,0:T(8,128)} custom-call(s32[1]{0:T(128)} %bitcast.me_ref, bf16[8,32,2,32,256]{4,3,2,1,0:T(8,128)(2,1)} %src_ref.6, bf16[2,48,256]{2,1,0:T(8,128)(2,1)} %constant.28.clone.tab_ref), custom_call_target="tpu_custom_call" | custom-call | flops 6000000000 | bytes 14680064 | tf_op jit(solution)/shard_map/rows/pallas_call | solution.py:291
  7.7 5.2 %all-to-all-start = ((f32[8,192,256]{2,1,0:T(8,128)}), f32[8,192,256]{2,1,0:T(8,128)S(1)}, u32[]{:S(2)}, u32[]{:S(2)}) async-start(f32[8,192,256]{2,1,0:T(8,128)} %bitcast.18), calls=%async_computation | async-start | bytes 3145728 | tf_op jit(solution)/shard_map/all_to_all | solution.py:695
  12.9 7.1 %rows.2 = f32[1536,256]{1,0:T(8,128)} custom-call(s32[1]{0:T(128)} %bitcast.me_ref, bf16[8,32,2,32,256]{4,3,2,1,0:T(8,128)(2,1)} %src_ref.7, bf16[2,48,256]{2,1,0:T(8,128)(2,1)} %constant.28.clone.tab_ref), custom_call_target="tpu_custom_call" | custom-call | flops 6000000000 | bytes 14680064 | tf_op jit(solution)/shard_map/rows/pallas_call | solution.py:291
  20.0 7.8 %pointwise.1.extra_ref = f32[8,256]{1,0:T(8,128)} custom-call(bf16[8,32,2,32,256]{4,3,2,1,0:T(8,128)(2,1)} %src_ref.6, bf16[8,32,2,32,256]{4,3,2,1,0:T(8,128)(2,1)} %src_ref.7), custom_call_target="tpu_custom_call" | custom-call | flops 8000000000 | bytes 20971520 | tf_op jit(solution)/shard_map/pointwise/pallas_call | solution.py:665
  28.6 6.2 %pack_weight.1.w_ref = f32[2,24,24,1024]{3,2,1,0:T(8,128)} custom-call(bf16[2,32,24,24,32]{4,3,2,1,0:T(8,128)(2,1)} %bitcast.19), custom_call_target="tpu_custom_call" | custom-call | flops 6000000000 | bytes 16777216 | tf_op jit(solution)/shard_map/pack_weight/pallas_call | solution.py:360
  35.4 4.3 %all-to-all-start.1 = ((f32[8,192,256]{2,1,0:T(8,128)}), f32[8,192,256]{2,1,0:T(8,128)S(1)}, u32[]{:S(2)}, u32[]{:S(2)}) async-start(f32[8,192,256]{2,1,0:T(8,128)} %bitcast.17), calls=%async_computation.1 | async-start | bytes 3145728 | tf_op jit(solution)/shard_map/all_to_all | solution.py:695
  39.7 1.6 %collective-permute-start = (f32[144,256]{1,0:T(8,128)S(1)}, f32[144,256]{1,0:T(8,128)S(1)}, u32[]{:S(2)}, u32[]{:S(2)}) collective-permute-start(f32[144,256]{1,0:T(8,128)S(1)} %get-tuple-element.32), channel_id=1, source_target_pairs={{0,8},{1,9},{2,10},{3,11},{4,12},{5,13},{6,14},{7,15},{8,0},{9,1},... | collective-permute-start | bytes 442376 | tf_op jit(solution)/shard_map/ppermute | solution.py:689
  41.3 2.6 %collective-permute-start.1 = (f32[144,256]{1,0:T(8,128)S(1)}, f32[144,256]{1,0:T(8,128)S(1)}, u32[]{:S(2)}, u32[]{:S(2)}) collective-permute-start(f32[144,256]{1,0:T(8,128)S(1)} %get-tuple-element.33), channel_id=1, source_target_pairs={{0,16},{1,17},{2,18},{3,19},{4,20},{5,21},{6,22},{7,23},{8,24},{9,... | collective-permute-start | bytes 442376 | tf_op jit(solution)/shard_map/ppermute | solution.py:689
  44.1 4.6 %collective-permute-done.rest_1_ = f32[144,256]{1,0:T(8,128)S(1)} collective-permute-done((f32[144,256]{1,0:T(8,128)S(1)}, f32[144,256]{1,0:T(8,128)S(1)}, u32[]{:S(2)}, u32[]{:S(2)}) %collective-permute-start) | collective-permute-done | bytes 147488 | tf_op jit(solution)/shard_map/ppermute | solution.py:689
  48.7 6.5 %collective-permute-done.1.rest_2_ = f32[144,256]{1,0:T(8,128)S(1)} collective-permute-done((f32[144,256]{1,0:T(8,128)S(1)}, f32[144,256]{1,0:T(8,128)S(1)}, u32[]{:S(2)}, u32[]{:S(2)}) %collective-permute-start.1) | collective-permute-done | bytes 147488 | tf_op jit(solution)/shard_map/ppermute | solution.py:689
  55.3 2.3 %copy-done.3 = f32[2,24,24,1024]{3,2,1,0:T(8,128)S(1)} copy-done((f32[2,24,24,1024]{3,2,1,0:T(8,128)S(1)}, f32[2,24,24,1024]{3,2,1,0:T(8,128)}, u32[]{:S(2)}) %copy-start.3) | copy-done | bytes 4718616
  57.6 2.4 %mix.1 = (f32[152,256]{1,0:T(8,128)S(1)}, f32[24,48,32]{2,1,0:T(8,128)S(1)}) custom-call(f32[2,24,24,1024]{3,2,1,0:T(8,128)S(1)} %copy-done.3, bf16[32,1024]{1,0:T(8,128)(2,1)S(1)} %copy-done.2, f32[8,256]{1,0:T(8,128)S(1)} %copy-done.5, f32[144,256]{1,0:T(8,128)S(1)} %get-tuple-element.31.rest_0_, f32[144,256]{1,0:T(8,128)S(1)} %collective-permute-done.rest_1_, ...), custom_call_target="tpu_custom_call" | custom-call | flops 4000000000 | bytes 6291456 | tf_op jit(solution)/shard_map/mix/pallas_call | solution.py:465
  60.0 4.1 %collective-permute-start.4 = (f32[152,256]{1,0:T(8,128)S(1)}, f32[152,256]{1,0:T(8,128)S(1)}, u32[]{:S(2)}, u32[]{:S(2)}) collective-permute-start(f32[152,256]{1,0:T(8,128)S(1)} %get-tuple-element.42.rest_0_), channel_id=1, source_target_pairs={{0,16},{1,17},{2,18},{3,19},{4,20},{5,21},{6,22},{7,23},{8,24},{9,... | collective-permute-start | bytes 466952 | tf_op jit(solution)/shard_map/ppermute | solution.py:689
  64.1 7.0 %collective-permute-done.4.rest_2_ = f32[152,256]{1,0:T(8,128)S(1)} collective-permute-done((f32[152,256]{1,0:T(8,128)S(1)}, f32[152,256]{1,0:T(8,128)S(1)}, u32[]{:S(2)}, u32[]{:S(2)}) %collective-permute-start.4) | collective-permute-done | bytes 155680 | tf_op jit(solution)/shard_map/ppermute | solution.py:689
  71.7 2.1 %collective-permute-start.6 = (f32[144,256]{1,0:T(8,128)S(1)}, f32[144,256]{1,0:T(8,128)S(1)}, u32[]{:S(2)}, u32[]{:S(2)}) collective-permute-start(f32[144,256]{1,0:T(8,128)S(1)} %get-tuple-element.39), channel_id=1, source_target_pairs={{0,8},{1,9},{2,10},{3,11},{4,12},{5,13},{6,14},{7,15},{8,0},{9,1},... | collective-permute-start | bytes 442376 | tf_op jit(solution)/shard_map/ppermute | solution.py:689
  73.8 0.8 collective-permute-start.7
  74.6 1.6 %collective-permute-start.8 = (f32[144,256]{1,0:T(8,128)S(1)}, f32[144,256]{1,0:T(8,128)S(1)}, u32[]{:S(2)}, u32[]{:S(2)}) collective-permute-start(f32[144,256]{1,0:T(8,128)S(1)} %get-tuple-element.41), channel_id=1, source_target_pairs={{0,24},{1,25},{2,26},{3,27},{4,28},{5,29},{6,30},{7,31},{8,16},{9,... | collective-permute-start | bytes 442376 | tf_op jit(solution)/shard_map/ppermute | solution.py:689
  77.0 1.5 collective-permute-done.5.rest_3_
  78.4 4.0 %collective-permute-done.6.rest_1_ = f32[144,256]{1,0:T(8,128)S(1)} collective-permute-done((f32[144,256]{1,0:T(8,128)S(1)}, f32[144,256]{1,0:T(8,128)S(1)}, u32[]{:S(2)}, u32[]{:S(2)}) %collective-permute-start.6) | collective-permute-done | bytes 147488 | tf_op jit(solution)/shard_map/ppermute | solution.py:689
  82.4 3.5 %collective-permute-done.7.rest_2_ = f32[144,256]{1,0:T(8,128)S(1)} collective-permute-done((f32[144,256]{1,0:T(8,128)S(1)}, f32[144,256]{1,0:T(8,128)S(1)}, u32[]{:S(2)}, u32[]{:S(2)}) %collective-permute-start.7) | collective-permute-done | bytes 147488 | tf_op jit(solution)/shard_map/ppermute | solution.py:689
  86.0 1.5 %expand_cells.2 = f32[1600,256]{1,0:T(8,128)} custom-call(bf16[128,96]{1,0:T(8,128)(2,1)S(1)} %dynamic-slice_bitcast_fusion.1.tab_ref, f32[152,256]{1,0:T(8,128)S(1)} %get-tuple-element.42.rest_0_, f32[152,256]{1,0:T(8,128)S(1)} %collective-permute-done.3.rest_1_, f32[152,256]{1,0:T(8,128)S(1)} %collective-permute-done.4.rest_2_, ...), custom_call_target="tpu_custom_call" | custom-call | flops 1000000000 | bytes 2097152 | tf_op jit(solution)/shard_map/expand_cells/pallas_call | solution.py:545
  87.5 4.4 %all-to-all-start.2 = ((f32[8,200,256]{2,1,0:T(8,128)}), f32[8,200,256]{2,1,0:T(8,128)}, u32[]{:S(2)}, u32[]{:S(2)}) async-start(f32[8,200,256]{2,1,0:T(8,128)} %bitcast.8), calls=%async_computation.2 | async-start | bytes 3276800 | tf_op jit(solution)/shard_map/all_to_all | solution.py:695
  92.0 2.3 %copy-done.4 = f32[2,24,24,1024]{3,2,1,0:T(8,128)S(1)} copy-done((f32[2,24,24,1024]{3,2,1,0:T(8,128)S(1)}, f32[2,24,24,1024]{3,2,1,0:T(8,128)}, u32[]{:S(2)}) %copy-start.4) | copy-done | bytes 4718616
  94.3 3.8 %adjoint.1 = (f32[144,256]{1,0:T(8,128)S(1)}, f32[24,48,32]{2,1,0:T(8,128)S(1)}) custom-call(f32[2,24,24,1024]{3,2,1,0:T(8,128)S(1)} %copy-done.4, bf16[32,1024]{1,0:T(8,128)(2,1)S(1)} %copy-done.1, bf16[1024,32]{1,0:T(8,128)(2,1)S(1)} %copy-done, f32[144,256]{1,0:T(8,128)S(1)} %get-tuple-element.38.rest_0_, f32[144,256]{1,0:T(8,128)S(1)} %collective-permute-done.6.rest_1_, ...), custom_call_target="tpu_custom_call" | custom-call | flops 4000000000 | bytes 6291456 | tf_op jit(solution)/shard_map/adjoint/pallas_call | solution.py:465
  98.1 1.8 %collective-permute-start.10 = (f32[144,256]{1,0:T(8,128)S(1)}, f32[144,256]{1,0:T(8,128)S(1)}, u32[]{:S(2)}, u32[]{:S(2)}) collective-permute-start(f32[144,256]{1,0:T(8,128)S(1)} %get-tuple-element.47.rest_0_), channel_id=1, source_target_pairs={{0,16},{1,17},{2,18},{3,19},{4,20},{5,21},{6,22},{7,23},{8,24},{9,... | collective-permute-start | bytes 442376 | tf_op jit(solution)/shard_map/ppermute | solution.py:689
  100.4 7.9 %collective-permute-done.10.rest_2_ = f32[144,256]{1,0:T(8,128)S(1)} collective-permute-done((f32[144,256]{1,0:T(8,128)S(1)}, f32[144,256]{1,0:T(8,128)S(1)}, u32[]{:S(2)}, u32[]{:S(2)}) %collective-permute-start.10) | collective-permute-done | bytes 147488 | tf_op jit(solution)/shard_map/ppermute | solution.py:689
  108.3 5.3 %collective-permute-done.11.rest_3_ = f32[144,256]{1,0:T(8,128)S(1)} collective-permute-done((f32[144,256]{1,0:T(8,128)S(1)}, f32[144,256]{1,0:T(8,128)S(1)}, u32[]{:S(2)}, u32[]{:S(2)}) %collective-permute-start.11) | collective-permute-done | bytes 147488 | tf_op jit(solution)/shard_map/ppermute | solution.py:689
  113.6 1.5 expand_cells.3
  115.1 4.3 %all-to-all-start.3 = ((f32[8,192,256]{2,1,0:T(8,128)}), f32[8,192,256]{2,1,0:T(8,128)}, u32[]{:S(2)}, u32[]{:S(2)}) async-start(f32[8,192,256]{2,1,0:T(8,128)} %bitcast.10), calls=%async_computation.3 | async-start | bytes 3145728 | tf_op jit(solution)/shard_map/all_to_all | solution.py:695
  119.4 8.8 %grad_modes.1 = f32[2,32,24,24,32]{4,3,2,1,0:T(8,128)} custom-call(f32[24,48,32]{2,1,0:T(8,128)S(1)} %get-tuple-element.48.f_ref, f32[24,48,32]{2,1,0:T(8,128)S(1)} %get-tuple-element.50.g_ref), custom_call_target="tpu_custom_call" | custom-call | flops 11000000512 | bytes 35651584 | tf_op jit(solution)/shard_map/grad_modes/pallas_call | solution.py:512
  128.3 10.8 %cells.2 = (bf16[8,32,2,32,256]{4,3,2,1,0:T(8,128)(2,1)}, f32[8,256]{1,0:T(8,128)}) custom-call(s32[1]{0:T(128)} %bitcast.me_ref, bf16[8,32,2,32,256]{4,3,2,1,0:T(8,128)(2,1)} %src_ref.6, bf16[2,144,256]{2,1,0:T(8,128)(2,1)} %constant.29.clone.tab_ref, bf16[32,32]{1,0:T(8,128)(2,1)} %w_ref.3, f32[1600,256]{1,0:T(8,128)} %bitcast.9.rest_0_), custom_call_target="tpu_custom_call" | custom-call | flops 8999999488 | bytes 29360128 | tf_op jit(solution)/shard_map/cells/pallas_call | solution.py:611
  140.5 10.1 %cells.3 = bf16[8,32,2,32,256]{4,3,2,1,0:T(8,128)(2,1)} custom-call(s32[1]{0:T(128)} %bitcast.me_ref, bf16[8,32,2,32,256]{4,3,2,1,0:T(8,128)(2,1)} %src_ref.7, bf16[2,144,256]{2,1,0:T(8,128)(2,1)} %constant.29.clone.tab_ref, bf16[32,32]{1,0:T(8,128)(2,1)} %w_ref.3, f32[1536,256]{1,0:T(8,128)} %bitcast.11.rest_0_), custom_call_target="tpu_custom_call" | custom-call | flops 8999999488 | bytes 29360128 | tf_op jit(solution)/shard_map/cells/pallas_call | solution.py:611
  (29 shorter events, 4.8 us)
Async XLA Ops:
  7.7 27.1 %all-to-all-start = ((f32[8,192,256]{2,1,0:T(8,128)}), f32[8,192,256]{2,1,0:T(8,128)S(1)}, u32[]{:S(2)}, u32[]{:S(2)}) async-start(f32[8,192,256]{2,1,0:T(8,128)} %bitcast.18), calls=%async_computation | async-start | bytes 3145728 | tf_op jit(solution)/shard_map/all_to_all | solution.py:695
  35.4 19.9 %copy-start.2 = (bf16[32,1024]{1,0:T(8,128)(2,1)S(1)}, bf16[32,1024]{1,0:T(8,128)(2,1)}, u32[]{:S(2)}) copy-start(bf16[32,1024]{1,0:T(8,128)(2,1)} %constant.32.clone.spread_ref) | copy-start | bytes 196612
  35.4 19.9 %copy-start.5 = (f32[8,256]{1,0:T(8,128)S(1)}, f32[8,256]{1,0:T(8,128)}, u32[]{:S(2)}) copy-start(f32[8,256]{1,0:T(8,128)} %pointwise.1.extra_ref) | copy-start | bytes 24580
  35.4 35.7 %all-to-all-start.1 = ((f32[8,192,256]{2,1,0:T(8,128)}), f32[8,192,256]{2,1,0:T(8,128)S(1)}, u32[]{:S(2)}, u32[]{:S(2)}) async-start(f32[8,192,256]{2,1,0:T(8,128)} %bitcast.17), calls=%async_computation.1 | async-start | bytes 3145728 | tf_op jit(solution)/shard_map/all_to_all | solution.py:695
  39.7 9.0 %collective-permute-start = (f32[144,256]{1,0:T(8,128)S(1)}, f32[144,256]{1,0:T(8,128)S(1)}, u32[]{:S(2)}, u32[]{:S(2)}) collective-permute-start(f32[144,256]{1,0:T(8,128)S(1)} %get-tuple-element.32), channel_id=1, source_target_pairs={{0,8},{1,9},{2,10},{3,11},{4,12},{5,13},{6,14},{7,15},{8,0},{9,1},... | collective-permute-start | bytes 442376 | tf_op jit(solution)/shard_map/ppermute | solution.py:689
  41.3 13.9 %collective-permute-start.1 = (f32[144,256]{1,0:T(8,128)S(1)}, f32[144,256]{1,0:T(8,128)S(1)}, u32[]{:S(2)}, u32[]{:S(2)}) collective-permute-start(f32[144,256]{1,0:T(8,128)S(1)} %get-tuple-element.33), channel_id=1, source_target_pairs={{0,16},{1,17},{2,18},{3,19},{4,20},{5,21},{6,22},{7,23},{8,24},{9,... | collective-permute-start | bytes 442376 | tf_op jit(solution)/shard_map/ppermute | solution.py:689
  43.9 11.4 %collective-permute-start.2 = (f32[144,256]{1,0:T(8,128)S(1)}, f32[144,256]{1,0:T(8,128)S(1)}, u32[]{:S(2)}, u32[]{:S(2)}) collective-permute-start(f32[144,256]{1,0:T(8,128)S(1)} %get-tuple-element.34), channel_id=1, source_target_pairs={{0,24},{1,25},{2,26},{3,27},{4,28},{5,29},{6,30},{7,31},{8,16},{9,... | collective-permute-start | bytes 442376 | tf_op jit(solution)/shard_map/ppermute | solution.py:689
  55.3 2.3 %copy-start.3 = (f32[2,24,24,1024]{3,2,1,0:T(8,128)S(1)}, f32[2,24,24,1024]{3,2,1,0:T(8,128)}, u32[]{:S(2)}) copy-start(f32[2,24,24,1024]{3,2,1,0:T(8,128)} %pack_weight.1.w_ref) | copy-start | bytes 14155780
  60.0 11.1 %collective-permute-start.4 = (f32[152,256]{1,0:T(8,128)S(1)}, f32[152,256]{1,0:T(8,128)S(1)}, u32[]{:S(2)}, u32[]{:S(2)}) collective-permute-start(f32[152,256]{1,0:T(8,128)S(1)} %get-tuple-element.42.rest_0_), channel_id=1, source_target_pairs={{0,16},{1,17},{2,18},{3,19},{4,20},{5,21},{6,22},{7,23},{8,24},{9,... | collective-permute-start | bytes 466952 | tf_op jit(solution)/shard_map/ppermute | solution.py:689
  64.1 12.9 %collective-permute-start.3 = (f32[152,256]{1,0:T(8,128)S(1)}, f32[152,256]{1,0:T(8,128)S(1)}, u32[]{:S(2)}, u32[]{:S(2)}) collective-permute-start(f32[152,256]{1,0:T(8,128)S(1)} %get-tuple-element.42.rest_0_), channel_id=1, source_target_pairs={{0,8},{1,9},{2,10},{3,11},{4,12},{5,13},{6,14},{7,15},{8,0},{9,1},... | collective-permute-start | bytes 466952 | tf_op jit(solution)/shard_map/ppermute | solution.py:689
  71.1 7.3 %collective-permute-start.5 = (f32[152,256]{1,0:T(8,128)S(1)}, f32[152,256]{1,0:T(8,128)S(1)}, u32[]{:S(2)}, u32[]{:S(2)}) collective-permute-start(f32[152,256]{1,0:T(8,128)S(1)} %collective-permute-done.4.rest_2_), channel_id=1, source_target_pairs={{0,8},{1,9},{2,10},{3,11},{4,12},{5,13},{6,14},{7,15},{8,0},{9,1},... | collective-permute-start | bytes 466952 | tf_op jit(solution)/shard_map/ppermute | solution.py:689
  71.7 10.7 %collective-permute-start.6 = (f32[144,256]{1,0:T(8,128)S(1)}, f32[144,256]{1,0:T(8,128)S(1)}, u32[]{:S(2)}, u32[]{:S(2)}) collective-permute-start(f32[144,256]{1,0:T(8,128)S(1)} %get-tuple-element.39), channel_id=1, source_target_pairs={{0,8},{1,9},{2,10},{3,11},{4,12},{5,13},{6,14},{7,15},{8,0},{9,1},... | collective-permute-start | bytes 442376 | tf_op jit(solution)/shard_map/ppermute | solution.py:689
  73.8 12.2 %collective-permute-start.7 = (f32[144,256]{1,0:T(8,128)S(1)}, f32[144,256]{1,0:T(8,128)S(1)}, u32[]{:S(2)}, u32[]{:S(2)}) collective-permute-start(f32[144,256]{1,0:T(8,128)S(1)} %get-tuple-element.40), channel_id=1, source_target_pairs={{0,16},{1,17},{2,18},{3,19},{4,20},{5,21},{6,22},{7,23},{8,24},{9,... | collective-permute-start | bytes 442376 | tf_op jit(solution)/shard_map/ppermute | solution.py:689
  74.6 11.4 %collective-permute-start.8 = (f32[144,256]{1,0:T(8,128)S(1)}, f32[144,256]{1,0:T(8,128)S(1)}, u32[]{:S(2)}, u32[]{:S(2)}) collective-permute-start(f32[144,256]{1,0:T(8,128)S(1)} %get-tuple-element.41), channel_id=1, source_target_pairs={{0,24},{1,25},{2,26},{3,27},{4,28},{5,29},{6,30},{7,31},{8,16},{9,... | collective-permute-start | bytes 442376 | tf_op jit(solution)/shard_map/ppermute | solution.py:689
  87.5 4.5 %copy-start = (bf16[1024,32]{1,0:T(8,128)(2,1)S(1)}, bf16[1024,32]{1,0:T(8,128)(2,1)}, u32[]{:S(2)}) copy-start(bf16[1024,32]{1,0:T(8,128)(2,1)} %constant.34.clone.gather_ref) | copy-start | bytes 196612
  87.5 4.5 %copy-start.1 = (bf16[32,1024]{1,0:T(8,128)(2,1)S(1)}, bf16[32,1024]{1,0:T(8,128)(2,1)}, u32[]{:S(2)}) copy-start(bf16[32,1024]{1,0:T(8,128)(2,1)} %constant.33.clone.spread_ref) | copy-start | bytes 196612
  87.5 27.6 %all-to-all-start.2 = ((f32[8,200,256]{2,1,0:T(8,128)}), f32[8,200,256]{2,1,0:T(8,128)}, u32[]{:S(2)}, u32[]{:S(2)}) async-start(f32[8,200,256]{2,1,0:T(8,128)} %bitcast.8), calls=%async_computation.2 | async-start | bytes 3276800 | tf_op jit(solution)/shard_map/all_to_all | solution.py:695
  92.0 2.3 %copy-start.4 = (f32[2,24,24,1024]{3,2,1,0:T(8,128)S(1)}, f32[2,24,24,1024]{3,2,1,0:T(8,128)}, u32[]{:S(2)}) copy-start(f32[2,24,24,1024]{3,2,1,0:T(8,128)} %pack_weight.1.w_ref) | copy-start | bytes 14155780
  98.1 10.2 %collective-permute-start.10 = (f32[144,256]{1,0:T(8,128)S(1)}, f32[144,256]{1,0:T(8,128)S(1)}, u32[]{:S(2)}, u32[]{:S(2)}) collective-permute-start(f32[144,256]{1,0:T(8,128)S(1)} %get-tuple-element.47.rest_0_), channel_id=1, source_target_pairs={{0,16},{1,17},{2,18},{3,19},{4,20},{5,21},{6,22},{7,23},{8,24},{9,... | collective-permute-start | bytes 442376 | tf_op jit(solution)/shard_map/ppermute | solution.py:689
  99.9 8.4 %collective-permute-start.9 = (f32[144,256]{1,0:T(8,128)S(1)}, f32[144,256]{1,0:T(8,128)S(1)}, u32[]{:S(2)}, u32[]{:S(2)}) collective-permute-start(f32[144,256]{1,0:T(8,128)S(1)} %get-tuple-element.47.rest_0_), channel_id=1, source_target_pairs={{0,8},{1,9},{2,10},{3,11},{4,12},{5,13},{6,14},{7,15},{8,0},{9,1},... | collective-permute-start | bytes 442376 | tf_op jit(solution)/shard_map/ppermute | solution.py:689
  108.3 5.3 %collective-permute-start.11 = (f32[144,256]{1,0:T(8,128)S(1)}, f32[144,256]{1,0:T(8,128)S(1)}, u32[]{:S(2)}, u32[]{:S(2)}) collective-permute-start(f32[144,256]{1,0:T(8,128)S(1)} %collective-permute-done.10.rest_2_), channel_id=1, source_target_pairs={{0,8},{1,9},{2,10},{3,11},{4,12},{5,13},{6,14},{7,15},{8,0},{9,1},... | collective-permute-start | bytes 442376 | tf_op jit(solution)/shard_map/ppermute | solution.py:689
  115.1 25.4 %all-to-all-start.3 = ((f32[8,192,256]{2,1,0:T(8,128)}), f32[8,192,256]{2,1,0:T(8,128)}, u32[]{:S(2)}, u32[]{:S(2)}) async-start(f32[8,192,256]{2,1,0:T(8,128)} %bitcast.10), calls=%async_computation.3 | async-start | bytes 3145728 | tf_op jit(solution)/shard_map/all_to_all | solution.py:695

commit v3 on v2

--- a/solution.py
+++ b/solution.py
@@ -348,7 +348,7 @@
             for r in range(2):
                 out_ref[r, i * block + j] = jnp.concatenate(
                     [buffer[r, c, i * block + j].astype(F32) for c in range(channels)], axis=1
-                )
+                ).astype(BF16)
         return carry
 
     lax.fori_loop(0, modes // block, body, 0)
@@ -361,7 +361,7 @@
         functools.partial(pack_kernel, block),
         in_specs=[HBM],
         out_specs=VMEM,
-        out_shape=jax.ShapeDtypeStruct((2, modes, kx, channels * channels), F32),
+        out_shape=jax.ShapeDtypeStruct((2, modes, kx, channels * channels), BF16),
         scratch_shapes=[
             pltpu.VMEM(weight.shape, BF16),
             pltpu.SemaphoreType.DMA((modes // block,)),
@@ -405,7 +405,8 @@
         for j in range(BLOCK):
             re = wide[2 * j * kx : (2 * j + 1) * kx]
             im = wide[(2 * j + 1) * kx : (2 * j + 2) * kx]
-            pieces.append((w_ref[0, i * BLOCK + j], w_ref[1, i * BLOCK + j], re, im))
+            mode = i * BLOCK + j
+            pieces.append((w_ref[0, mode].astype(F32), w_ref[1, mode].astype(F32), re, im))
         write(i, pieces)
         return carry
 
@@ -572,7 +573,9 @@
         total = ins[0][at, :]
         for ref in ins[1:]:
             total = total + ref[at, :]
-        rest[2][...] = total
+        for c in range(channels):
+            lanes = slice(c % PER * channels, (c % PER + 1) * channels)
+            rest[2][c : c + 1, :] = total[c // PER : c // PER + 1, lanes]
     tall = (iota((LANES, channels), 0) % channels == iota((LANES, channels), 1)).astype(BF16)
     rows = (nt if flip else nn)(tall, w_ref[...]).astype(BF16)
     same = iota((LANES, LANES), 0) // channels == iota((LANES, LANES), 1) // channels
@@ -607,7 +610,7 @@
     cells, pairs = src.shape[:2]
     out_shape = [jax.ShapeDtypeStruct(src.shape, BF16)]
     if extra:
-        out_shape.append(jax.ShapeDtypeStruct((extra, LANES), F32))
+        out_shape.append(jax.ShapeDtypeStruct(weight.shape, F32))
     return pl.pallas_call(
         functools.partial(cells_kernel, n, extra, flip),
         in_specs=[SMEM, HBM, VMEM, VMEM, VMEM],
@@ -627,57 +630,72 @@
     )(me, src, tab, weight, rows)
 
 
-def pointwise_kernel(norm, f_ref, g_ref, out_ref, f_buffer, g_buffer, hold, f_sems, g_sems):
-    cells, pairs, _, channels, length = f_ref.shape
-    f_copy = fetch(f_ref, f_buffer, f_sems)
-    g_copy = fetch(g_ref, g_buffer, g_sems)
-    square = (LANES, LANES)
-    hold[...] = jnp.zeros(square, F32)
+def rows_pointwise_kernel(n, norm, me_ref, field_ref, src_ref, tab_ref, *rest):
+    out_ref, grad_ref, hold, square, f_buffer, buffer, f_sems, sems = rest
+    outs = messages(out_ref)
+    cells, pairs, _, channels, length = src_ref.shape
+    copy = fetch(src_ref, buffer, sems)
+    f_copy = fetch(field_ref, f_buffer, f_sems)
+    square[...] = jnp.zeros(square.shape, F32)
 
     def body(x, carry):
+        copy(x).wait()
         f_copy(x).wait()
-        g_copy(x).wait()
-        total = hold[...]
+        at = pl.ds(pl.multiple_of(x * K2, 8), K2)
+        products = square[...]
         for g in range(pairs // PER):
-            at = slice(g * PER, (g + 1) * PER)
+            total = None
             for r in range(2):
-                left = f_buffer[x, at, r].reshape(LANES, length)
-                right = g_buffer[x, at, r].reshape(LANES, length)
-                total = total + nt(left, right)
-        hold[...] = total
+                tile = buffer[x, g * PER : (g + 1) * PER, r].reshape(LANES, length)
+                left = f_buffer[x, g * PER : (g + 1) * PER, r].reshape(LANES, length)
+                products = products + nt(left, tile)
+                part = nt(tab_ref[r], tile)
+                total = part if total is None else total + part
+            hold[2 * g, at, :] = total[:, :128]
+            hold[2 * g + 1, at, :] = total[:, 128:]
+        square[...] = products
         return carry
 
     lax.fori_loop(0, cells, body, 0)
-    same = iota(square, 0) // channels == iota(square, 1) // channels
-    diagonal = jnp.where(same, hold[...], 0.0)
+    for index, row, k, g in piece_places(me_ref[0], cells, n):
+        for r in range(2):
+            at = row + r * cells
+            for half in range(2):
+                outs[index][at : at + cells, half * 128 : (half + 1) * 128] = hold[
+                    2 * g + half, pl.ds(k + r * KY, cells, stride=K2), :
+                ]
+    shape = (LANES, LANES)
+    same = iota(shape, 0) // channels == iota(shape, 1) // channels
+    diagonal = jnp.where(same, square[...], 0.0)
     fold = (iota((channels, LANES), 1) % channels == iota((channels, LANES), 0)).astype(F32)
     rows = nn_full(fold, diagonal)
-    spread = (iota(square, 0) % channels == iota(square, 1) % channels).astype(F32)
+    spread = (iota(shape, 0) % channels == iota(shape, 1) % channels).astype(F32)
     full = nn_full(rows, spread)
     keep = iota((channels, LANES), 0) % PER == iota((channels, LANES), 1) // channels
     full = jnp.where(keep, full, 0.0)
     pick = (iota((EXTRA, channels), 1) // PER == iota((EXTRA, channels), 0)).astype(F32)
-    out_ref[...] = nn_full(pick, full) * norm
-
-
-def pointwise_call(field, cotangent, norm):
-    cells = field.shape[0]
+    grad_ref[...] = nn_full(pick, full) * norm
+
+
+def rows_pointwise_call(n, norm, me, field, src, tab):
+    cells, pairs = src.shape[:2]
     return pl.pallas_call(
-        functools.partial(pointwise_kernel, norm),
-        in_specs=[HBM] * 2,
-        out_specs=VMEM,
-        out_shape=jax.ShapeDtypeStruct((EXTRA, LANES), F32),
+        functools.partial(rows_pointwise_kernel, n, norm),
+        in_specs=[SMEM, HBM, HBM, VMEM],
+        out_specs=[VMEM] * 2,
+        out_shape=[message_shape(cells), jax.ShapeDtypeStruct((EXTRA, LANES), F32)],
         scratch_shapes=[
-            pltpu.VMEM(field.shape, BF16),
-            pltpu.VMEM(field.shape, BF16),
+            pltpu.VMEM((pairs // PER * 2, cells * K2, 128), F32),
             pltpu.VMEM((LANES, LANES), F32),
+            pltpu.VMEM(src.shape, BF16),
+            pltpu.VMEM(src.shape, BF16),
             pltpu.SemaphoreType.DMA((cells,)),
             pltpu.SemaphoreType.DMA((cells,)),
         ],
         compiler_params=params(56),
-        cost_estimate=cost(8e9, 20),
-        name="pointwise",
-    )(field, cotangent)
+        cost_estimate=cost(14e9, 34),
+        name="rows_pointwise",
+    )(me, field, src, tab)
 
 
 def local_kernels(n, field, cotangent, spectral_weight, local_weight):
@@ -725,9 +743,11 @@
     def after(arrays, *others):
         return lax.optimization_barrier((arrays, others))[0]
 
-    field_rows = near_exchange(rows_call(n, me, field, rows_table))
-    cot_out = rows_call(n, me, cotangent, rows_table)
-    grad_part = pointwise_call(after(field, cot_out), cotangent, norm)
+    field_out = rows_call(n, me, field, rows_table)
+    field_rows = near_exchange(field_out)
+    cot_out, grad_part = rows_pointwise_call(
+        n, norm, me, after(field, field_out), cotangent, rows_table
+    )
     packed = pack_call(after(weight, grad_part))
 
     field_sums = partial_call(cells, forward, after(field_rows, packed))
@@ -747,13 +767,12 @@
     grad_spectral = jnp.transpose(outer, (0, 1, 4, 2, 3))
     back_parts = far_gather(back)
     back_rows = near_exchange(expand_call(cells, backward, back_parts))
-    output, grad_rows = cells_call(
+    output, grad_local = cells_call(
         n, EXTRA, True, me, field, cells_table, local_weight, mixed_rows
     )
     (grad_field,) = cells_call(
         n, 0, False, me, cotangent, cells_table, local_weight, back_rows
     )
-    grad_local = grad_rows[: channels // PER].reshape(channels, channels)
     return (output, grad_field, grad_spectral, grad_local)
 
 

time: 151 us -> 148 us (0.980)
  waiting for transfers between devices: 40.5 us -> 45.5 us
  Pallas kernels: 68.1 us -> 63.6 us
  local copies, waits for them, and re-layouts: 7.61 us -> 4.88 us
    pallas_call x2 -> x1, Pallas kernels: 14.2 us -> 7.1 us  [rows_call(): pl.pallas_call(functools.partial(rows_kernel, n), in_specs=[SMEM, HBM, VM...]
    all_to_all x4, waiting for transfers between devices: 0.06 us -> 5.53 us  [near_exchange(): lax.all_to_all(stacked, 'gx', 0, 0, axis_index_groups=planes, tiled=True)]
    pallas_call x1, Pallas kernels: 7.75 us -> 10.7 us  [rows_pointwise_call(): pl.pallas_call(functools.partial(rows_pointwise_kernel, n, norm), in_spec...]
  transfers between devices with their start and end apart: 16 -> 16, of which waited for: 9 -> 10; matrix products, arithmetic and copies ran while one was open for 2% -> 1% of each run, Pallas kernels for 32% -> 30%
where the time goes in v3:
time: 148 us
  Pallas kernels  63.6 us (43%)
  waiting for transfers between devices  45.5 us (31%)
  starting transfers between devices  32.9 us (22%)
  local copies, waits for them, and re-layouts  4.88 us (3%)
    ppermute x12, waiting for transfers between devices, permute(): return lax.ppermute(array, 'gx', [(i, hop(i)) for i in range(n)])  39.9 us
    pallas_call x2, Pallas kernels, cells_call(): pl.pallas_call(functools.partial(cells_kernel, n, extra, flip), in_specs=...  20.9 us
    all_to_all x4, starting transfers between devices, near_exchange(): lax.all_to_all(stacked, 'gx', 0, 0, axis_index_groups=planes, tiled=True)  17.6 us
    ppermute x12, starting transfers between devices, permute(): return lax.ppermute(array, 'gx', [(i, hop(i)) for i in range(n)])  15.3 us
    pallas_call x1, Pallas kernels, rows_pointwise_call(): pl.pallas_call(functools.partial(rows_pointwise_kernel, n, norm), in_spec...  10.7 us
    pallas_call x1, Pallas kernels, outer_call(): pl.pallas_call(outer_kernel, in_specs=[VMEM] * 2, out_specs=HBM, out_shap...  8.81 us
    pallas_call x1, Pallas kernels, rows_call(): pl.pallas_call(functools.partial(rows_kernel, n), in_specs=[SMEM, HBM, VM...  7.1 us
    pallas_call x2, Pallas kernels, mode_call(): pl.pallas_call(kernel, in_specs=[VMEM] * (1 + len(more) + len(parts)), ou...  6.51 us
  transfers between devices with their start and end apart: 16, of which 10 were waited for; matrix products, arithmetic and copies ran while one was open for 1% of the time, Pallas kernels for 30%

profile of v3, /device:TPU:0, one launch (start us, length us, event | category | flops | bytes accessed | tf_op | source)
XLA Modules:
  0.0 147.7 jit_solution(7637366184611371915)
XLA Ops:
  0.6 7.1 %rows.1 = f32[1536,256]{1,0:T(8,128)} custom-call(s32[1]{0:T(128)} %bitcast.me_ref, bf16[8,32,2,32,256]{4,3,2,1,0:T(8,128)(2,1)} %src_ref.6, bf16[2,48,256]{2,1,0:T(8,128)(2,1)} %constant.28.clone.tab_ref), custom_call_target="tpu_custom_call" | custom-call | flops 6000000000 | bytes 14680064 | tf_op jit(solution)/shard_map/rows/pallas_call | solution.py:291
  7.7 5.2 %all-to-all-start = ((f32[8,192,256]{2,1,0:T(8,128)}), f32[8,192,256]{2,1,0:T(8,128)S(1)}, u32[]{:S(2)}, u32[]{:S(2)}) async-start(f32[8,192,256]{2,1,0:T(8,128)} %bitcast.18), calls=%async_computation | async-start | bytes 3145728 | tf_op jit(solution)/shard_map/all_to_all | solution.py:713
  12.9 10.7 %rows_pointwise.1 = (f32[1536,256]{1,0:T(8,128)}, f32[8,256]{1,0:T(8,128)}) custom-call(s32[1]{0:T(128)} %bitcast.me_ref, bf16[8,32,2,32,256]{4,3,2,1,0:T(8,128)(2,1)} %src_ref.6, bf16[8,32,2,32,256]{4,3,2,1,0:T(8,128)(2,1)} %src_ref.7, bf16[2,48,256]{2,1,0:T(8,128)(2,1)} %constant.28.clone.tab_ref), custom_call_target="tpu_custom_call" | custom-call | flops 14000000000 | bytes 35651584 | tf_op jit(solution)/shard_map/rows_pointwise/pallas_call | solution.py:682
  24.4 5.5 %pack_weight.1.w_ref = bf16[2,24,24,1024]{3,2,1,0:T(8,128)(2,1)} custom-call(bf16[2,32,24,24,32]{4,3,2,1,0:T(8,128)(2,1)} %bitcast.19), custom_call_target="tpu_custom_call" | custom-call | flops 6000000000 | bytes 16777216 | tf_op jit(solution)/shard_map/pack_weight/pallas_call | solution.py:360
  29.9 4.1 %all-to-all-done = f32[8,192,256]{2,1,0:T(8,128)S(1)} async-done(((f32[8,192,256]{2,1,0:T(8,128)}), f32[8,192,256]{2,1,0:T(8,128)S(1)}, u32[]{:S(2)}, u32[]{:S(2)}) %all-to-all-start) | async-done | bytes 1572896 | tf_op jit(solution)/shard_map/all_to_all | solution.py:713
  34.5 3.7 %all-to-all-start.1 = ((f32[8,192,256]{2,1,0:T(8,128)}), f32[8,192,256]{2,1,0:T(8,128)S(1)}, u32[]{:S(2)}, u32[]{:S(2)}) async-start(f32[8,192,256]{2,1,0:T(8,128)} %bitcast.17), calls=%async_computation.1 | async-start | bytes 3145728 | tf_op jit(solution)/shard_map/all_to_all | solution.py:713
  38.3 1.6 %collective-permute-start = (f32[144,256]{1,0:T(8,128)S(1)}, f32[144,256]{1,0:T(8,128)S(1)}, u32[]{:S(2)}, u32[]{:S(2)}) collective-permute-start(f32[144,256]{1,0:T(8,128)S(1)} %get-tuple-element.35), channel_id=1, source_target_pairs={{0,8},{1,9},{2,10},{3,11},{4,12},{5,13},{6,14},{7,15},{8,0},{9,1},... | collective-permute-start | bytes 442376 | tf_op jit(solution)/shard_map/ppermute | solution.py:707
  39.9 2.6 %collective-permute-start.1 = (f32[144,256]{1,0:T(8,128)S(1)}, f32[144,256]{1,0:T(8,128)S(1)}, u32[]{:S(2)}, u32[]{:S(2)}) collective-permute-start(f32[144,256]{1,0:T(8,128)S(1)} %get-tuple-element.36), channel_id=1, source_target_pairs={{0,16},{1,17},{2,18},{3,19},{4,20},{5,21},{6,22},{7,23},{8,24},{9,... | collective-permute-start | bytes 442376 | tf_op jit(solution)/shard_map/ppermute | solution.py:707
  42.7 4.3 %collective-permute-done.rest_1_ = f32[144,256]{1,0:T(8,128)S(1)} collective-permute-done((f32[144,256]{1,0:T(8,128)S(1)}, f32[144,256]{1,0:T(8,128)S(1)}, u32[]{:S(2)}, u32[]{:S(2)}) %collective-permute-start) | collective-permute-done | bytes 147488 | tf_op jit(solution)/shard_map/ppermute | solution.py:707
  47.0 6.9 %collective-permute-done.1.rest_2_ = f32[144,256]{1,0:T(8,128)S(1)} collective-permute-done((f32[144,256]{1,0:T(8,128)S(1)}, f32[144,256]{1,0:T(8,128)S(1)}, u32[]{:S(2)}, u32[]{:S(2)}) %collective-permute-start.1) | collective-permute-done | bytes 147488 | tf_op jit(solution)/shard_map/ppermute | solution.py:707
  53.9 1.7 %copy-done.3 = bf16[2,24,24,1024]{3,2,1,0:T(8,128)(2,1)S(1)} copy-done((bf16[2,24,24,1024]{3,2,1,0:T(8,128)(2,1)S(1)}, bf16[2,24,24,1024]{3,2,1,0:T(8,128)(2,1)}, u32[]{:S(2)}) %copy-start.3) | copy-done | bytes 2359320
  55.6 2.5 %mix.1 = (f32[152,256]{1,0:T(8,128)S(1)}, f32[24,48,32]{2,1,0:T(8,128)S(1)}) custom-call(bf16[2,24,24,1024]{3,2,1,0:T(8,128)(2,1)S(1)} %copy-done.3, bf16[32,1024]{1,0:T(8,128)(2,1)S(1)} %copy-done.2, f32[8,256]{1,0:T(8,128)S(1)} %copy-done.5, f32[144,256]{1,0:T(8,128)S(1)} %get-tuple-element.34.rest_0_, f32[144,256]{1,0:T(8,128)S(1)} %collective-permute-done.rest_1_, ...), custom_call_target="tpu_custom_call" | custom-call | flops 4000000000 | bytes 6291456 | tf_op jit(solution)/shard_map/mix/pallas_call | solution.py:466
  58.0 3.9 %collective-permute-start.4 = (f32[152,256]{1,0:T(8,128)S(1)}, f32[152,256]{1,0:T(8,128)S(1)}, u32[]{:S(2)}, u32[]{:S(2)}) collective-permute-start(f32[152,256]{1,0:T(8,128)S(1)} %get-tuple-element.46.rest_0_), channel_id=1, source_target_pairs={{0,16},{1,17},{2,18},{3,19},{4,20},{5,21},{6,22},{7,23},{8,24},{9,... | collective-permute-start | bytes 466952 | tf_op jit(solution)/shard_map/ppermute | solution.py:707
  62.0 6.8 %collective-permute-done.4.rest_2_ = f32[152,256]{1,0:T(8,128)S(1)} collective-permute-done((f32[152,256]{1,0:T(8,128)S(1)}, f32[152,256]{1,0:T(8,128)S(1)}, u32[]{:S(2)}, u32[]{:S(2)}) %collective-permute-start.4) | collective-permute-done | bytes 155680 | tf_op jit(solution)/shard_map/ppermute | solution.py:707
  69.3 2.1 %collective-permute-start.6 = (f32[144,256]{1,0:T(8,128)S(1)}, f32[144,256]{1,0:T(8,128)S(1)}, u32[]{:S(2)}, u32[]{:S(2)}) collective-permute-start(f32[144,256]{1,0:T(8,128)S(1)} %get-tuple-element.43), channel_id=1, source_target_pairs={{0,8},{1,9},{2,10},{3,11},{4,12},{5,13},{6,14},{7,15},{8,0},{9,1},... | collective-permute-start | bytes 442376 | tf_op jit(solution)/shard_map/ppermute | solution.py:707
  72.4 1.5 %collective-permute-start.8 = (f32[144,256]{1,0:T(8,128)S(1)}, f32[144,256]{1,0:T(8,128)S(1)}, u32[]{:S(2)}, u32[]{:S(2)}) collective-permute-start(f32[144,256]{1,0:T(8,128)S(1)} %get-tuple-element.45), channel_id=1, source_target_pairs={{0,24},{1,25},{2,26},{3,27},{4,28},{5,29},{6,30},{7,31},{8,16},{9,... | collective-permute-start | bytes 442376 | tf_op jit(solution)/shard_map/ppermute | solution.py:707
  74.6 1.3 collective-permute-done.5.rest_3_
  75.9 4.0 %collective-permute-done.6.rest_1_ = f32[144,256]{1,0:T(8,128)S(1)} collective-permute-done((f32[144,256]{1,0:T(8,128)S(1)}, f32[144,256]{1,0:T(8,128)S(1)}, u32[]{:S(2)}, u32[]{:S(2)}) %collective-permute-start.6) | collective-permute-done | bytes 147488 | tf_op jit(solution)/shard_map/ppermute | solution.py:707
  79.9 3.6 %collective-permute-done.7.rest_2_ = f32[144,256]{1,0:T(8,128)S(1)} collective-permute-done((f32[144,256]{1,0:T(8,128)S(1)}, f32[144,256]{1,0:T(8,128)S(1)}, u32[]{:S(2)}, u32[]{:S(2)}) %collective-permute-start.7) | collective-permute-done | bytes 147488 | tf_op jit(solution)/shard_map/ppermute | solution.py:707
  83.4 1.5 %expand_cells.2 = f32[1600,256]{1,0:T(8,128)} custom-call(bf16[128,96]{1,0:T(8,128)(2,1)S(1)} %dynamic-slice_bitcast_fusion.1.tab_ref, f32[152,256]{1,0:T(8,128)S(1)} %get-tuple-element.46.rest_0_, f32[152,256]{1,0:T(8,128)S(1)} %collective-permute-done.3.rest_1_, f32[152,256]{1,0:T(8,128)S(1)} %collective-permute-done.4.rest_2_, ...), custom_call_target="tpu_custom_call" | custom-call | flops 1000000000 | bytes 2097152 | tf_op jit(solution)/shard_map/expand_cells/pallas_call | solution.py:546
  85.0 4.4 %all-to-all-start.2 = ((f32[8,200,256]{2,1,0:T(8,128)}), f32[8,200,256]{2,1,0:T(8,128)}, u32[]{:S(2)}, u32[]{:S(2)}) async-start(f32[8,200,256]{2,1,0:T(8,128)} %bitcast.8), calls=%async_computation.2 | async-start | bytes 3276800 | tf_op jit(solution)/shard_map/all_to_all | solution.py:713
  89.4 1.7 %copy-done.4 = bf16[2,24,24,1024]{3,2,1,0:T(8,128)(2,1)S(1)} copy-done((bf16[2,24,24,1024]{3,2,1,0:T(8,128)(2,1)S(1)}, bf16[2,24,24,1024]{3,2,1,0:T(8,128)(2,1)}, u32[]{:S(2)}) %copy-start.4) | copy-done | bytes 2359320
  91.1 4.0 %adjoint.1 = (f32[144,256]{1,0:T(8,128)S(1)}, f32[24,48,32]{2,1,0:T(8,128)S(1)}) custom-call(bf16[2,24,24,1024]{3,2,1,0:T(8,128)(2,1)S(1)} %copy-done.4, bf16[32,1024]{1,0:T(8,128)(2,1)S(1)} %copy-done.1, bf16[1024,32]{1,0:T(8,128)(2,1)S(1)} %copy-done, f32[144,256]{1,0:T(8,128)S(1)} %get-tuple-element.42.rest_0_, ...), custom_call_target="tpu_custom_call" | custom-call | flops 4000000000 | bytes 6291456 | tf_op jit(solution)/shard_map/adjoint/pallas_call | solution.py:466
  95.1 1.8 %collective-permute-start.10 = (f32[144,256]{1,0:T(8,128)S(1)}, f32[144,256]{1,0:T(8,128)S(1)}, u32[]{:S(2)}, u32[]{:S(2)}) collective-permute-start(f32[144,256]{1,0:T(8,128)S(1)} %get-tuple-element.51.rest_0_), channel_id=1, source_target_pairs={{0,16},{1,17},{2,18},{3,19},{4,20},{5,21},{6,22},{7,23},{8,24},{9,... | collective-permute-start | bytes 442376 | tf_op jit(solution)/shard_map/ppermute | solution.py:707
  97.5 7.8 %collective-permute-done.10.rest_2_ = f32[144,256]{1,0:T(8,128)S(1)} collective-permute-done((f32[144,256]{1,0:T(8,128)S(1)}, f32[144,256]{1,0:T(8,128)S(1)}, u32[]{:S(2)}, u32[]{:S(2)}) %collective-permute-start.10) | collective-permute-done | bytes 147488 | tf_op jit(solution)/shard_map/ppermute | solution.py:707
  105.4 5.3 %collective-permute-done.11.rest_3_ = f32[144,256]{1,0:T(8,128)S(1)} collective-permute-done((f32[144,256]{1,0:T(8,128)S(1)}, f32[144,256]{1,0:T(8,128)S(1)}, u32[]{:S(2)}, u32[]{:S(2)}) %collective-permute-start.11) | collective-permute-done | bytes 147488 | tf_op jit(solution)/shard_map/ppermute | solution.py:707
  110.7 1.5 %expand_cells.3 = f32[1536,256]{1,0:T(8,128)} custom-call(bf16[128,96]{1,0:T(8,128)(2,1)S(1)} %dynamic-slice_bitcast_fusion.1.tab_ref, f32[144,256]{1,0:T(8,128)S(1)} %get-tuple-element.51.rest_0_, f32[144,256]{1,0:T(8,128)S(1)} %collective-permute-done.9.rest_1_, f32[144,256]{1,0:T(8,128)S(1)} %collective-permute-done.10.rest_2_, ...), custom_call_target="tpu_custom_call" | custom-call | flops 1000000000 | bytes 2097152 | tf_op jit(solution)/shard_map/expand_cells/pallas_call | solution.py:546
  112.2 4.3 %all-to-all-start.3 = ((f32[8,192,256]{2,1,0:T(8,128)}), f32[8,192,256]{2,1,0:T(8,128)}, u32[]{:S(2)}, u32[]{:S(2)}) async-start(f32[8,192,256]{2,1,0:T(8,128)} %bitcast.10), calls=%async_computation.3 | async-start | bytes 3145728 | tf_op jit(solution)/shard_map/all_to_all | solution.py:713
  116.5 8.8 %grad_modes.1 = f32[2,32,24,24,32]{4,3,2,1,0:T(8,128)} custom-call(f32[24,48,32]{2,1,0:T(8,128)S(1)} %get-tuple-element.52.f_ref, f32[24,48,32]{2,1,0:T(8,128)S(1)} %get-tuple-element.54.g_ref), custom_call_target="tpu_custom_call" | custom-call | flops 11000000512 | bytes 35651584 | tf_op jit(solution)/shard_map/grad_modes/pallas_call | solution.py:513
  125.3 10.8 %cells.2 = (bf16[8,32,2,32,256]{4,3,2,1,0:T(8,128)(2,1)}, f32[32,32]{1,0:T(8,128)}) custom-call(s32[1]{0:T(128)} %bitcast.me_ref, bf16[8,32,2,32,256]{4,3,2,1,0:T(8,128)(2,1)} %src_ref.6, bf16[2,144,256]{2,1,0:T(8,128)(2,1)} %constant.29.clone.tab_ref, bf16[32,32]{1,0:T(8,128)(2,1)} %w_ref.3, f32[1600,256]{1,0:T(8,128)} %bitcast.9.rest_0_), custom_call_target="tpu_custom_call" | custom-call | flops 8999999488 | bytes 29360128 | tf_op jit(solution)/shard_map/cells/pallas_call | solution.py:614
  136.1 1.4 all-to-all-done.3
  137.5 10.1 %cells.3 = bf16[8,32,2,32,256]{4,3,2,1,0:T(8,128)(2,1)} custom-call(s32[1]{0:T(128)} %bitcast.me_ref, bf16[8,32,2,32,256]{4,3,2,1,0:T(8,128)(2,1)} %src_ref.7, bf16[2,144,256]{2,1,0:T(8,128)(2,1)} %constant.29.clone.tab_ref, bf16[32,32]{1,0:T(8,128)(2,1)} %w_ref.3, f32[1536,256]{1,0:T(8,128)} %bitcast.11.rest_0_), custom_call_target="tpu_custom_call" | custom-call | flops 8999999488 | bytes 29360128 | tf_op jit(solution)/shard_map/cells/pallas_call | solution.py:614
  (26 shorter events, 4.5 us)
Async XLA Ops:
  7.7 26.2 %all-to-all-start = ((f32[8,192,256]{2,1,0:T(8,128)}), f32[8,192,256]{2,1,0:T(8,128)S(1)}, u32[]{:S(2)}, u32[]{:S(2)}) async-start(f32[8,192,256]{2,1,0:T(8,128)} %bitcast.18), calls=%async_computation | async-start | bytes 3145728 | tf_op jit(solution)/shard_map/all_to_all | solution.py:713
  34.5 19.4 %copy-start.2 = (bf16[32,1024]{1,0:T(8,128)(2,1)S(1)}, bf16[32,1024]{1,0:T(8,128)(2,1)}, u32[]{:S(2)}) copy-start(bf16[32,1024]{1,0:T(8,128)(2,1)} %constant.32.clone.spread_ref) | copy-start | bytes 196612
  34.5 19.4 %copy-start.5 = (f32[8,256]{1,0:T(8,128)S(1)}, f32[8,256]{1,0:T(8,128)}, u32[]{:S(2)}) copy-start(f32[8,256]{1,0:T(8,128)} %get-tuple-element.31.extra_ref) | copy-start | bytes 24580
  34.5 34.2 %all-to-all-start.1 = ((f32[8,192,256]{2,1,0:T(8,128)}), f32[8,192,256]{2,1,0:T(8,128)S(1)}, u32[]{:S(2)}, u32[]{:S(2)}) async-start(f32[8,192,256]{2,1,0:T(8,128)} %bitcast.17), calls=%async_computation.1 | async-start | bytes 3145728 | tf_op jit(solution)/shard_map/all_to_all | solution.py:713
  38.3 8.8 %collective-permute-start = (f32[144,256]{1,0:T(8,128)S(1)}, f32[144,256]{1,0:T(8,128)S(1)}, u32[]{:S(2)}, u32[]{:S(2)}) collective-permute-start(f32[144,256]{1,0:T(8,128)S(1)} %get-tuple-element.35), channel_id=1, source_target_pairs={{0,8},{1,9},{2,10},{3,11},{4,12},{5,13},{6,14},{7,15},{8,0},{9,1},... | collective-permute-start | bytes 442376 | tf_op jit(solution)/shard_map/ppermute | solution.py:707
  39.9 14.0 %collective-permute-start.1 = (f32[144,256]{1,0:T(8,128)S(1)}, f32[144,256]{1,0:T(8,128)S(1)}, u32[]{:S(2)}, u32[]{:S(2)}) collective-permute-start(f32[144,256]{1,0:T(8,128)S(1)} %get-tuple-element.36), channel_id=1, source_target_pairs={{0,16},{1,17},{2,18},{3,19},{4,20},{5,21},{6,22},{7,23},{8,24},{9,... | collective-permute-start | bytes 442376 | tf_op jit(solution)/shard_map/ppermute | solution.py:707
  42.5 11.4 %collective-permute-start.2 = (f32[144,256]{1,0:T(8,128)S(1)}, f32[144,256]{1,0:T(8,128)S(1)}, u32[]{:S(2)}, u32[]{:S(2)}) collective-permute-start(f32[144,256]{1,0:T(8,128)S(1)} %get-tuple-element.37), channel_id=1, source_target_pairs={{0,24},{1,25},{2,26},{3,27},{4,28},{5,29},{6,30},{7,31},{8,16},{9,... | collective-permute-start | bytes 442376 | tf_op jit(solution)/shard_map/ppermute | solution.py:707
  53.9 1.7 %copy-start.3 = (bf16[2,24,24,1024]{3,2,1,0:T(8,128)(2,1)S(1)}, bf16[2,24,24,1024]{3,2,1,0:T(8,128)(2,1)}, u32[]{:S(2)}) copy-start(bf16[2,24,24,1024]{3,2,1,0:T(8,128)(2,1)} %pack_weight.1.w_ref) | copy-start | bytes 7077892
  58.0 10.7 %collective-permute-start.4 = (f32[152,256]{1,0:T(8,128)S(1)}, f32[152,256]{1,0:T(8,128)S(1)}, u32[]{:S(2)}, u32[]{:S(2)}) collective-permute-start(f32[152,256]{1,0:T(8,128)S(1)} %get-tuple-element.46.rest_0_), channel_id=1, source_target_pairs={{0,16},{1,17},{2,18},{3,19},{4,20},{5,21},{6,22},{7,23},{8,24},{9,... | collective-permute-start | bytes 466952 | tf_op jit(solution)/shard_map/ppermute | solution.py:707
  61.9 12.6 %collective-permute-start.3 = (f32[152,256]{1,0:T(8,128)S(1)}, f32[152,256]{1,0:T(8,128)S(1)}, u32[]{:S(2)}, u32[]{:S(2)}) collective-permute-start(f32[152,256]{1,0:T(8,128)S(1)} %get-tuple-element.46.rest_0_), channel_id=1, source_target_pairs={{0,8},{1,9},{2,10},{3,11},{4,12},{5,13},{6,14},{7,15},{8,0},{9,1},... | collective-permute-start | bytes 466952 | tf_op jit(solution)/shard_map/ppermute | solution.py:707
  68.7 7.1 %collective-permute-start.5 = (f32[152,256]{1,0:T(8,128)S(1)}, f32[152,256]{1,0:T(8,128)S(1)}, u32[]{:S(2)}, u32[]{:S(2)}) collective-permute-start(f32[152,256]{1,0:T(8,128)S(1)} %collective-permute-done.4.rest_2_), channel_id=1, source_target_pairs={{0,8},{1,9},{2,10},{3,11},{4,12},{5,13},{6,14},{7,15},{8,0},{9,1},... | collective-permute-start | bytes 466952 | tf_op jit(solution)/shard_map/ppermute | solution.py:707
  69.3 10.6 %collective-permute-start.6 = (f32[144,256]{1,0:T(8,128)S(1)}, f32[144,256]{1,0:T(8,128)S(1)}, u32[]{:S(2)}, u32[]{:S(2)}) collective-permute-start(f32[144,256]{1,0:T(8,128)S(1)} %get-tuple-element.43), channel_id=1, source_target_pairs={{0,8},{1,9},{2,10},{3,11},{4,12},{5,13},{6,14},{7,15},{8,0},{9,1},... | collective-permute-start | bytes 442376 | tf_op jit(solution)/shard_map/ppermute | solution.py:707
  71.4 12.1 %collective-permute-start.7 = (f32[144,256]{1,0:T(8,128)S(1)}, f32[144,256]{1,0:T(8,128)S(1)}, u32[]{:S(2)}, u32[]{:S(2)}) collective-permute-start(f32[144,256]{1,0:T(8,128)S(1)} %get-tuple-element.44), channel_id=1, source_target_pairs={{0,16},{1,17},{2,18},{3,19},{4,20},{5,21},{6,22},{7,23},{8,24},{9,... | collective-permute-start | bytes 442376 | tf_op jit(solution)/shard_map/ppermute | solution.py:707
  72.4 11.1 %collective-permute-start.8 = (f32[144,256]{1,0:T(8,128)S(1)}, f32[144,256]{1,0:T(8,128)S(1)}, u32[]{:S(2)}, u32[]{:S(2)}) collective-permute-start(f32[144,256]{1,0:T(8,128)S(1)} %get-tuple-element.45), channel_id=1, source_target_pairs={{0,24},{1,25},{2,26},{3,27},{4,28},{5,29},{6,30},{7,31},{8,16},{9,... | collective-permute-start | bytes 442376 | tf_op jit(solution)/shard_map/ppermute | solution.py:707
  85.0 4.4 %copy-start = (bf16[1024,32]{1,0:T(8,128)(2,1)S(1)}, bf16[1024,32]{1,0:T(8,128)(2,1)}, u32[]{:S(2)}) copy-start(bf16[1024,32]{1,0:T(8,128)(2,1)} %constant.34.clone.gather_ref) | copy-start | bytes 196612
  85.0 4.5 %copy-start.1 = (bf16[32,1024]{1,0:T(8,128)(2,1)S(1)}, bf16[32,1024]{1,0:T(8,128)(2,1)}, u32[]{:S(2)}) copy-start(bf16[32,1024]{1,0:T(8,128)(2,1)} %constant.33.clone.spread_ref) | copy-start | bytes 196612
  85.0 27.2 %all-to-all-start.2 = ((f32[8,200,256]{2,1,0:T(8,128)}), f32[8,200,256]{2,1,0:T(8,128)}, u32[]{:S(2)}, u32[]{:S(2)}) async-start(f32[8,200,256]{2,1,0:T(8,128)} %bitcast.8), calls=%async_computation.2 | async-start | bytes 3276800 | tf_op jit(solution)/shard_map/all_to_all | solution.py:713
  89.4 1.7 %copy-start.4 = (bf16[2,24,24,1024]{3,2,1,0:T(8,128)(2,1)S(1)}, bf16[2,24,24,1024]{3,2,1,0:T(8,128)(2,1)}, u32[]{:S(2)}) copy-start(bf16[2,24,24,1024]{3,2,1,0:T(8,128)(2,1)} %pack_weight.1.w_ref) | copy-start | bytes 7077892
  95.1 10.2 %collective-permute-start.10 = (f32[144,256]{1,0:T(8,128)S(1)}, f32[144,256]{1,0:T(8,128)S(1)}, u32[]{:S(2)}, u32[]{:S(2)}) collective-permute-start(f32[144,256]{1,0:T(8,128)S(1)} %get-tuple-element.51.rest_0_), channel_id=1, source_target_pairs={{0,16},{1,17},{2,18},{3,19},{4,20},{5,21},{6,22},{7,23},{8,24},{9,... | collective-permute-start | bytes 442376 | tf_op jit(solution)/shard_map/ppermute | solution.py:707
  96.9 8.4 %collective-permute-start.9 = (f32[144,256]{1,0:T(8,128)S(1)}, f32[144,256]{1,0:T(8,128)S(1)}, u32[]{:S(2)}, u32[]{:S(2)}) collective-permute-start(f32[144,256]{1,0:T(8,128)S(1)} %get-tuple-element.51.rest_0_), channel_id=1, source_target_pairs={{0,8},{1,9},{2,10},{3,11},{4,12},{5,13},{6,14},{7,15},{8,0},{9,1},... | collective-permute-start | bytes 442376 | tf_op jit(solution)/shard_map/ppermute | solution.py:707
  105.4 5.3 %collective-permute-start.11 = (f32[144,256]{1,0:T(8,128)S(1)}, f32[144,256]{1,0:T(8,128)S(1)}, u32[]{:S(2)}, u32[]{:S(2)}) collective-permute-start(f32[144,256]{1,0:T(8,128)S(1)} %collective-permute-done.10.rest_2_), channel_id=1, source_target_pairs={{0,8},{1,9},{2,10},{3,11},{4,12},{5,13},{6,14},{7,15},{8,0},{9,1},... | collective-permute-start | bytes 442376 | tf_op jit(solution)/shard_map/ppermute | solution.py:707
  112.2 25.3 %all-to-all-start.3 = ((f32[8,192,256]{2,1,0:T(8,128)}), f32[8,192,256]{2,1,0:T(8,128)}, u32[]{:S(2)}, u32[]{:S(2)}) async-start(f32[8,192,256]{2,1,0:T(8,128)} %bitcast.10), calls=%async_computation.3 | async-start | bytes 3145728 | tf_op jit(solution)/shard_map/all_to_all | solution.py:713

commit v4 on v3

--- a/solution.py
+++ b/solution.py
@@ -257,9 +257,15 @@
     return copy
 
 
+def departures(stage, out_ref, sems):
+    pairs = zip(messages(stage), messages(out_ref))
+    return [pltpu.make_async_copy(a, b, sems.at[m]) for m, (a, b) in enumerate(pairs)]
+
+
 def rows_kernel(n, me_ref, src_ref, tab_ref, *rest):
-    out_ref, hold, buffer, sems = rest
-    outs = messages(out_ref)
+    out_ref, hold, buffer, sems, stage, out_sems = rest
+    outs = messages(stage)
+    leave = departures(stage, out_ref, out_sems)
     cells, pairs, _, _, length = src_ref.shape
     copy = fetch(src_ref, buffer, sems)
 
@@ -278,12 +284,17 @@
 
     lax.fori_loop(0, cells, body, 0)
     for index, row, k, g in piece_places(me_ref[0], cells, n):
+        if row == 0 and index > 0:
+            leave[index - 1].start()
         for r in range(2):
             at = row + r * cells
             for half in range(2):
                 outs[index][at : at + cells, half * 128 : (half + 1) * 128] = hold[
                     2 * g + half, pl.ds(k + r * KY, cells, stride=K2), :
                 ]
+    leave[-1].start()
+    for copy in leave:
+        copy.wait()
 
 
 def rows_call(n, me, src, tab):
@@ -291,12 +302,14 @@
     return pl.pallas_call(
         functools.partial(rows_kernel, n),
         in_specs=[SMEM, HBM, VMEM],
-        out_specs=VMEM,
+        out_specs=HBM,
         out_shape=message_shape(cells),
         scratch_shapes=[
             pltpu.VMEM((pairs // PER * 2, cells * K2, 128), F32),
             pltpu.VMEM(src.shape, BF16),
             pltpu.SemaphoreType.DMA((cells,)),
+            pltpu.VMEM(message_shape(cells).shape, F32),
+            pltpu.SemaphoreType.DMA((NEAR,)),
         ],
         compiler_params=params(56),
         cost_estimate=cost(6e9, 14),
@@ -523,7 +536,9 @@
 
 
 def expand_kernel(cells, extra, tab_ref, *rest):
-    ins, outs = rest[:G], messages(rest[G])
+    ins, (out_ref, stage, out_sems) = rest[:G], rest[G:]
+    outs = messages(stage)
+    leave = departures(stage, out_ref, out_sems)
     table = tab_ref[...]
     step = 2 * cells
     for s in range(G):
@@ -539,6 +554,10 @@
             total = total + ref[CHUNK:, :]
         for m in range(NEAR):
             outs[m][G * SLOTS * step :, :] = total
+    for copy in leave:
+        copy.start()
+    for copy in leave:
+        copy.wait()
 
 
 def expand_call(cells, tab, parts):
@@ -546,8 +565,12 @@
     return pl.pallas_call(
         functools.partial(expand_kernel, cells, extra),
         in_specs=[VMEM] * (1 + len(parts)),
-        out_specs=VMEM,
+        out_specs=HBM,
         out_shape=message_shape(cells, extra),
+        scratch_shapes=[
+            pltpu.VMEM(message_shape(cells, extra).shape, F32),
+            pltpu.SemaphoreType.DMA((NEAR,)),
+        ],
         compiler_params=params(16),
         cost_estimate=cost(1e9, 2),
         name="expand_cells",

time: 148 us -> 148 us (level)
  no operation moved by 1% of the time
where the time goes in v4:
time: 148 us; the launch traced here: 147 us
  Pallas kernels  63.3 us (43%)
  waiting for transfers between devices  45.5 us (31%)
  starting transfers between devices  32.9 us (22%)
  local copies, waits for them, and re-layouts  4.89 us (3%)
    ppermute x12, waiting for transfers between devices, permute(): return lax.ppermute(array, 'gx', [(i, hop(i)) for i in range(n)])  40 us
    pallas_call x2, Pallas kernels, cells_call(): pl.pallas_call(functools.partial(cells_kernel, n, extra, flip), in_specs=...  20.9 us
    all_to_all x4, starting transfers between devices, near_exchange(): lax.all_to_all(stacked, 'gx', 0, 0, axis_index_groups=planes, tiled=True)  17.7 us
    ppermute x12, starting transfers between devices, permute(): return lax.ppermute(array, 'gx', [(i, hop(i)) for i in range(n)])  15.3 us
    pallas_call x1, Pallas kernels, rows_pointwise_call(): pl.pallas_call(functools.partial(rows_pointwise_kernel, n, norm), in_spec...  10.7 us
    pallas_call x1, Pallas kernels, outer_call(): pl.pallas_call(outer_kernel, in_specs=[VMEM] * 2, out_specs=HBM, out_shap...  8.81 us
    pallas_call x1, Pallas kernels, rows_call(): pl.pallas_call(functools.partial(rows_kernel, n), in_specs=[SMEM, HBM, VM...  6.73 us
    pallas_call x2, Pallas kernels, mode_call(): pl.pallas_call(kernel, in_specs=[VMEM] * (1 + len(more) + len(parts)), ou...  6.51 us
  transfers between devices with their start and end apart: 16, of which 10 were waited for; matrix products, arithmetic and copies ran while one was open for 1% of the time, Pallas kernels for 30%

profile of v4, /device:TPU:0, one launch (start us, length us, event | category | flops | bytes accessed | tf_op | source)
XLA Modules:
  0.0 147.5 jit_solution(7427629672079306718)
XLA Ops:
  0.6 6.7 %rows.1 = f32[1536,256]{1,0:T(8,128)} custom-call(s32[1]{0:T(128)} %bitcast.me_ref, bf16[8,32,2,32,256]{4,3,2,1,0:T(8,128)(2,1)} %src_ref.6, bf16[2,48,256]{2,1,0:T(8,128)(2,1)} %constant.28.clone.tab_ref), custom_call_target="tpu_custom_call" | custom-call | flops 6000000000 | bytes 14680064 | tf_op jit(solution)/shard_map/rows/pallas_call | solution.py:302
  7.4 5.2 %all-to-all-start = ((f32[8,192,256]{2,1,0:T(8,128)}), f32[8,192,256]{2,1,0:T(8,128)S(1)}, u32[]{:S(2)}, u32[]{:S(2)}) async-start(f32[8,192,256]{2,1,0:T(8,128)} %bitcast.18), calls=%async_computation | async-start | bytes 3145728 | tf_op jit(solution)/shard_map/all_to_all | solution.py:736
  12.6 10.7 %rows_pointwise.1 = (f32[1536,256]{1,0:T(8,128)}, f32[8,256]{1,0:T(8,128)}) custom-call(s32[1]{0:T(128)} %bitcast.me_ref, bf16[8,32,2,32,256]{4,3,2,1,0:T(8,128)(2,1)} %src_ref.6, bf16[8,32,2,32,256]{4,3,2,1,0:T(8,128)(2,1)} %src_ref.7, bf16[2,48,256]{2,1,0:T(8,128)(2,1)} %constant.28.clone.tab_ref), custom_call_target="tpu_custom_call" | custom-call | flops 14000000000 | bytes 35651584 | tf_op jit(solution)/shard_map/rows_pointwise/pallas_call | solution.py:705
  24.0 5.5 %pack_weight.1.w_ref = bf16[2,24,24,1024]{3,2,1,0:T(8,128)(2,1)} custom-call(bf16[2,32,24,24,32]{4,3,2,1,0:T(8,128)(2,1)} %bitcast.19), custom_call_target="tpu_custom_call" | custom-call | flops 6000000000 | bytes 16777216 | tf_op jit(solution)/shard_map/pack_weight/pallas_call | solution.py:373
  29.5 4.1 %all-to-all-done = f32[8,192,256]{2,1,0:T(8,128)S(1)} async-done(((f32[8,192,256]{2,1,0:T(8,128)}), f32[8,192,256]{2,1,0:T(8,128)S(1)}, u32[]{:S(2)}, u32[]{:S(2)}) %all-to-all-start) | async-done | bytes 1572896 | tf_op jit(solution)/shard_map/all_to_all | solution.py:736
  34.2 3.7 %all-to-all-start.1 = ((f32[8,192,256]{2,1,0:T(8,128)}), f32[8,192,256]{2,1,0:T(8,128)S(1)}, u32[]{:S(2)}, u32[]{:S(2)}) async-start(f32[8,192,256]{2,1,0:T(8,128)} %bitcast.17), calls=%async_computation.1 | async-start | bytes 3145728 | tf_op jit(solution)/shard_map/all_to_all | solution.py:736
  37.9 1.6 %collective-permute-start = (f32[144,256]{1,0:T(8,128)S(1)}, f32[144,256]{1,0:T(8,128)S(1)}, u32[]{:S(2)}, u32[]{:S(2)}) collective-permute-start(f32[144,256]{1,0:T(8,128)S(1)} %get-tuple-element.35), channel_id=1, source_target_pairs={{0,8},{1,9},{2,10},{3,11},{4,12},{5,13},{6,14},{7,15},{8,0},{9,1},... | collective-permute-start | bytes 442376 | tf_op jit(solution)/shard_map/ppermute | solution.py:730
  39.5 2.6 %collective-permute-start.1 = (f32[144,256]{1,0:T(8,128)S(1)}, f32[144,256]{1,0:T(8,128)S(1)}, u32[]{:S(2)}, u32[]{:S(2)}) collective-permute-start(f32[144,256]{1,0:T(8,128)S(1)} %get-tuple-element.36), channel_id=1, source_target_pairs={{0,16},{1,17},{2,18},{3,19},{4,20},{5,21},{6,22},{7,23},{8,24},{9,... | collective-permute-start | bytes 442376 | tf_op jit(solution)/shard_map/ppermute | solution.py:730
  42.3 4.3 %collective-permute-done.rest_1_ = f32[144,256]{1,0:T(8,128)S(1)} collective-permute-done((f32[144,256]{1,0:T(8,128)S(1)}, f32[144,256]{1,0:T(8,128)S(1)}, u32[]{:S(2)}, u32[]{:S(2)}) %collective-permute-start) | collective-permute-done | bytes 147488 | tf_op jit(solution)/shard_map/ppermute | solution.py:730
  46.6 6.9 %collective-permute-done.1.rest_2_ = f32[144,256]{1,0:T(8,128)S(1)} collective-permute-done((f32[144,256]{1,0:T(8,128)S(1)}, f32[144,256]{1,0:T(8,128)S(1)}, u32[]{:S(2)}, u32[]{:S(2)}) %collective-permute-start.1) | collective-permute-done | bytes 147488 | tf_op jit(solution)/shard_map/ppermute | solution.py:730
  53.5 1.7 %copy-done.3 = bf16[2,24,24,1024]{3,2,1,0:T(8,128)(2,1)S(1)} copy-done((bf16[2,24,24,1024]{3,2,1,0:T(8,128)(2,1)S(1)}, bf16[2,24,24,1024]{3,2,1,0:T(8,128)(2,1)}, u32[]{:S(2)}) %copy-start.3) | copy-done | bytes 2359320
  55.2 2.5 %mix.1 = (f32[152,256]{1,0:T(8,128)S(1)}, f32[24,48,32]{2,1,0:T(8,128)S(1)}) custom-call(bf16[2,24,24,1024]{3,2,1,0:T(8,128)(2,1)S(1)} %copy-done.3, bf16[32,1024]{1,0:T(8,128)(2,1)S(1)} %copy-done.2, f32[8,256]{1,0:T(8,128)S(1)} %copy-done.5, f32[144,256]{1,0:T(8,128)S(1)} %get-tuple-element.34.rest_0_, f32[144,256]{1,0:T(8,128)S(1)} %collective-permute-done.rest_1_, ...), custom_call_target="tpu_custom_call" | custom-call | flops 4000000000 | bytes 6291456 | tf_op jit(solution)/shard_map/mix/pallas_call | solution.py:479
  57.7 3.9 %collective-permute-start.4 = (f32[152,256]{1,0:T(8,128)S(1)}, f32[152,256]{1,0:T(8,128)S(1)}, u32[]{:S(2)}, u32[]{:S(2)}) collective-permute-start(f32[152,256]{1,0:T(8,128)S(1)} %get-tuple-element.46.rest_0_), channel_id=1, source_target_pairs={{0,16},{1,17},{2,18},{3,19},{4,20},{5,21},{6,22},{7,23},{8,24},{9,... | collective-permute-start | bytes 466952 | tf_op jit(solution)/shard_map/ppermute | solution.py:730
  61.6 6.8 %collective-permute-done.4.rest_2_ = f32[152,256]{1,0:T(8,128)S(1)} collective-permute-done((f32[152,256]{1,0:T(8,128)S(1)}, f32[152,256]{1,0:T(8,128)S(1)}, u32[]{:S(2)}, u32[]{:S(2)}) %collective-permute-start.4) | collective-permute-done | bytes 155680 | tf_op jit(solution)/shard_map/ppermute | solution.py:730
  68.9 2.1 %collective-permute-start.6 = (f32[144,256]{1,0:T(8,128)S(1)}, f32[144,256]{1,0:T(8,128)S(1)}, u32[]{:S(2)}, u32[]{:S(2)}) collective-permute-start(f32[144,256]{1,0:T(8,128)S(1)} %get-tuple-element.43), channel_id=1, source_target_pairs={{0,8},{1,9},{2,10},{3,11},{4,12},{5,13},{6,14},{7,15},{8,0},{9,1},... | collective-permute-start | bytes 442376 | tf_op jit(solution)/shard_map/ppermute | solution.py:730
  72.0 1.5 %collective-permute-start.8 = (f32[144,256]{1,0:T(8,128)S(1)}, f32[144,256]{1,0:T(8,128)S(1)}, u32[]{:S(2)}, u32[]{:S(2)}) collective-permute-start(f32[144,256]{1,0:T(8,128)S(1)} %get-tuple-element.45), channel_id=1, source_target_pairs={{0,24},{1,25},{2,26},{3,27},{4,28},{5,29},{6,30},{7,31},{8,16},{9,... | collective-permute-start | bytes 442376 | tf_op jit(solution)/shard_map/ppermute | solution.py:730
  74.2 1.3 collective-permute-done.5.rest_3_
  75.5 4.0 %collective-permute-done.6.rest_1_ = f32[144,256]{1,0:T(8,128)S(1)} collective-permute-done((f32[144,256]{1,0:T(8,128)S(1)}, f32[144,256]{1,0:T(8,128)S(1)}, u32[]{:S(2)}, u32[]{:S(2)}) %collective-permute-start.6) | collective-permute-done | bytes 147488 | tf_op jit(solution)/shard_map/ppermute | solution.py:730
  79.5 3.6 %collective-permute-done.7.rest_2_ = f32[144,256]{1,0:T(8,128)S(1)} collective-permute-done((f32[144,256]{1,0:T(8,128)S(1)}, f32[144,256]{1,0:T(8,128)S(1)}, u32[]{:S(2)}, u32[]{:S(2)}) %collective-permute-start.7) | collective-permute-done | bytes 147488 | tf_op jit(solution)/shard_map/ppermute | solution.py:730
  83.1 1.6 %expand_cells.2 = f32[1600,256]{1,0:T(8,128)} custom-call(bf16[128,96]{1,0:T(8,128)(2,1)S(1)} %dynamic-slice_bitcast_fusion.1.tab_ref, f32[152,256]{1,0:T(8,128)S(1)} %get-tuple-element.46.rest_0_, f32[152,256]{1,0:T(8,128)S(1)} %collective-permute-done.3.rest_1_, f32[152,256]{1,0:T(8,128)S(1)} %collective-permute-done.4.rest_2_, ...), custom_call_target="tpu_custom_call" | custom-call | flops 1000000000 | bytes 2097152 | tf_op jit(solution)/shard_map/expand_cells/pallas_call | solution.py:565
  84.7 4.4 %all-to-all-start.2 = ((f32[8,200,256]{2,1,0:T(8,128)}), f32[8,200,256]{2,1,0:T(8,128)}, u32[]{:S(2)}, u32[]{:S(2)}) async-start(f32[8,200,256]{2,1,0:T(8,128)} %bitcast.8), calls=%async_computation.2 | async-start | bytes 3276800 | tf_op jit(solution)/shard_map/all_to_all | solution.py:736
  89.2 1.7 %copy-done.4 = bf16[2,24,24,1024]{3,2,1,0:T(8,128)(2,1)S(1)} copy-done((bf16[2,24,24,1024]{3,2,1,0:T(8,128)(2,1)S(1)}, bf16[2,24,24,1024]{3,2,1,0:T(8,128)(2,1)}, u32[]{:S(2)}) %copy-start.4) | copy-done | bytes 2359320
  90.8 4.0 %adjoint.1 = (f32[144,256]{1,0:T(8,128)S(1)}, f32[24,48,32]{2,1,0:T(8,128)S(1)}) custom-call(bf16[2,24,24,1024]{3,2,1,0:T(8,128)(2,1)S(1)} %copy-done.4, bf16[32,1024]{1,0:T(8,128)(2,1)S(1)} %copy-done.1, bf16[1024,32]{1,0:T(8,128)(2,1)S(1)} %copy-done, f32[144,256]{1,0:T(8,128)S(1)} %get-tuple-element.42.rest_0_, ...), custom_call_target="tpu_custom_call" | custom-call | flops 4000000000 | bytes 6291456 | tf_op jit(solution)/shard_map/adjoint/pallas_call | solution.py:479
  94.9 1.8 %collective-permute-start.10 = (f32[144,256]{1,0:T(8,128)S(1)}, f32[144,256]{1,0:T(8,128)S(1)}, u32[]{:S(2)}, u32[]{:S(2)}) collective-permute-start(f32[144,256]{1,0:T(8,128)S(1)} %get-tuple-element.51.rest_0_), channel_id=1, source_target_pairs={{0,16},{1,17},{2,18},{3,19},{4,20},{5,21},{6,22},{7,23},{8,24},{9,... | collective-permute-start | bytes 442376 | tf_op jit(solution)/shard_map/ppermute | solution.py:730
  97.2 7.9 %collective-permute-done.10.rest_2_ = f32[144,256]{1,0:T(8,128)S(1)} collective-permute-done((f32[144,256]{1,0:T(8,128)S(1)}, f32[144,256]{1,0:T(8,128)S(1)}, u32[]{:S(2)}, u32[]{:S(2)}) %collective-permute-start.10) | collective-permute-done | bytes 147488 | tf_op jit(solution)/shard_map/ppermute | solution.py:730
  105.1 5.3 %collective-permute-done.11.rest_3_ = f32[144,256]{1,0:T(8,128)S(1)} collective-permute-done((f32[144,256]{1,0:T(8,128)S(1)}, f32[144,256]{1,0:T(8,128)S(1)}, u32[]{:S(2)}, u32[]{:S(2)}) %collective-permute-start.11) | collective-permute-done | bytes 147488 | tf_op jit(solution)/shard_map/ppermute | solution.py:730
  110.4 1.6 %expand_cells.3 = f32[1536,256]{1,0:T(8,128)} custom-call(bf16[128,96]{1,0:T(8,128)(2,1)S(1)} %dynamic-slice_bitcast_fusion.1.tab_ref, f32[144,256]{1,0:T(8,128)S(1)} %get-tuple-element.51.rest_0_, f32[144,256]{1,0:T(8,128)S(1)} %collective-permute-done.9.rest_1_, f32[144,256]{1,0:T(8,128)S(1)} %collective-permute-done.10.rest_2_, ...), custom_call_target="tpu_custom_call" | custom-call | flops 1000000000 | bytes 2097152 | tf_op jit(solution)/shard_map/expand_cells/pallas_call | solution.py:565
  112.0 4.3 %all-to-all-start.3 = ((f32[8,192,256]{2,1,0:T(8,128)}), f32[8,192,256]{2,1,0:T(8,128)}, u32[]{:S(2)}, u32[]{:S(2)}) async-start(f32[8,192,256]{2,1,0:T(8,128)} %bitcast.10), calls=%async_computation.3 | async-start | bytes 3145728 | tf_op jit(solution)/shard_map/all_to_all | solution.py:736
  116.3 8.8 %grad_modes.1 = f32[2,32,24,24,32]{4,3,2,1,0:T(8,128)} custom-call(f32[24,48,32]{2,1,0:T(8,128)S(1)} %get-tuple-element.52.f_ref, f32[24,48,32]{2,1,0:T(8,128)S(1)} %get-tuple-element.54.g_ref), custom_call_target="tpu_custom_call" | custom-call | flops 11000000512 | bytes 35651584 | tf_op jit(solution)/shard_map/grad_modes/pallas_call | solution.py:526
  125.1 10.8 %cells.2 = (bf16[8,32,2,32,256]{4,3,2,1,0:T(8,128)(2,1)}, f32[32,32]{1,0:T(8,128)}) custom-call(s32[1]{0:T(128)} %bitcast.me_ref, bf16[8,32,2,32,256]{4,3,2,1,0:T(8,128)(2,1)} %src_ref.6, bf16[2,144,256]{2,1,0:T(8,128)(2,1)} %constant.29.clone.tab_ref, bf16[32,32]{1,0:T(8,128)(2,1)} %w_ref.3, f32[1600,256]{1,0:T(8,128)} %bitcast.9.rest_0_), custom_call_target="tpu_custom_call" | custom-call | flops 8999999488 | bytes 29360128 | tf_op jit(solution)/shard_map/cells/pallas_call | solution.py:637
  135.9 1.4 all-to-all-done.3
  137.3 10.1 %cells.3 = bf16[8,32,2,32,256]{4,3,2,1,0:T(8,128)(2,1)} custom-call(s32[1]{0:T(128)} %bitcast.me_ref, bf16[8,32,2,32,256]{4,3,2,1,0:T(8,128)(2,1)} %src_ref.7, bf16[2,144,256]{2,1,0:T(8,128)(2,1)} %constant.29.clone.tab_ref, bf16[32,32]{1,0:T(8,128)(2,1)} %w_ref.3, f32[1536,256]{1,0:T(8,128)} %bitcast.11.rest_0_), custom_call_target="tpu_custom_call" | custom-call | flops 8999999488 | bytes 29360128 | tf_op jit(solution)/shard_map/cells/pallas_call | solution.py:637
  (26 shorter events, 4.4 us)
Async XLA Ops:
  7.4 26.2 %all-to-all-start = ((f32[8,192,256]{2,1,0:T(8,128)}), f32[8,192,256]{2,1,0:T(8,128)S(1)}, u32[]{:S(2)}, u32[]{:S(2)}) async-start(f32[8,192,256]{2,1,0:T(8,128)} %bitcast.18), calls=%async_computation | async-start | bytes 3145728 | tf_op jit(solution)/shard_map/all_to_all | solution.py:736
  34.1 19.4 %copy-start.2 = (bf16[32,1024]{1,0:T(8,128)(2,1)S(1)}, bf16[32,1024]{1,0:T(8,128)(2,1)}, u32[]{:S(2)}) copy-start(bf16[32,1024]{1,0:T(8,128)(2,1)} %constant.32.clone.spread_ref) | copy-start | bytes 196612
  34.1 19.4 %copy-start.5 = (f32[8,256]{1,0:T(8,128)S(1)}, f32[8,256]{1,0:T(8,128)}, u32[]{:S(2)}) copy-start(f32[8,256]{1,0:T(8,128)} %get-tuple-element.31.extra_ref) | copy-start | bytes 24580
  34.2 34.2 %all-to-all-start.1 = ((f32[8,192,256]{2,1,0:T(8,128)}), f32[8,192,256]{2,1,0:T(8,128)S(1)}, u32[]{:S(2)}, u32[]{:S(2)}) async-start(f32[8,192,256]{2,1,0:T(8,128)} %bitcast.17), calls=%async_computation.1 | async-start | bytes 3145728 | tf_op jit(solution)/shard_map/all_to_all | solution.py:736
  37.9 8.8 %collective-permute-start = (f32[144,256]{1,0:T(8,128)S(1)}, f32[144,256]{1,0:T(8,128)S(1)}, u32[]{:S(2)}, u32[]{:S(2)}) collective-permute-start(f32[144,256]{1,0:T(8,128)S(1)} %get-tuple-element.35), channel_id=1, source_target_pairs={{0,8},{1,9},{2,10},{3,11},{4,12},{5,13},{6,14},{7,15},{8,0},{9,1},... | collective-permute-start | bytes 442376 | tf_op jit(solution)/shard_map/ppermute | solution.py:730
  39.5 14.0 %collective-permute-start.1 = (f32[144,256]{1,0:T(8,128)S(1)}, f32[144,256]{1,0:T(8,128)S(1)}, u32[]{:S(2)}, u32[]{:S(2)}) collective-permute-start(f32[144,256]{1,0:T(8,128)S(1)} %get-tuple-element.36), channel_id=1, source_target_pairs={{0,16},{1,17},{2,18},{3,19},{4,20},{5,21},{6,22},{7,23},{8,24},{9,... | collective-permute-start | bytes 442376 | tf_op jit(solution)/shard_map/ppermute | solution.py:730
  42.1 11.4 %collective-permute-start.2 = (f32[144,256]{1,0:T(8,128)S(1)}, f32[144,256]{1,0:T(8,128)S(1)}, u32[]{:S(2)}, u32[]{:S(2)}) collective-permute-start(f32[144,256]{1,0:T(8,128)S(1)} %get-tuple-element.37), channel_id=1, source_target_pairs={{0,24},{1,25},{2,26},{3,27},{4,28},{5,29},{6,30},{7,31},{8,16},{9,... | collective-permute-start | bytes 442376 | tf_op jit(solution)/shard_map/ppermute | solution.py:730
  53.5 1.7 %copy-start.3 = (bf16[2,24,24,1024]{3,2,1,0:T(8,128)(2,1)S(1)}, bf16[2,24,24,1024]{3,2,1,0:T(8,128)(2,1)}, u32[]{:S(2)}) copy-start(bf16[2,24,24,1024]{3,2,1,0:T(8,128)(2,1)} %pack_weight.1.w_ref) | copy-start | bytes 7077892
  57.7 10.7 %collective-permute-start.4 = (f32[152,256]{1,0:T(8,128)S(1)}, f32[152,256]{1,0:T(8,128)S(1)}, u32[]{:S(2)}, u32[]{:S(2)}) collective-permute-start(f32[152,256]{1,0:T(8,128)S(1)} %get-tuple-element.46.rest_0_), channel_id=1, source_target_pairs={{0,16},{1,17},{2,18},{3,19},{4,20},{5,21},{6,22},{7,23},{8,24},{9,... | collective-permute-start | bytes 466952 | tf_op jit(solution)/shard_map/ppermute | solution.py:730
  61.6 12.6 %collective-permute-start.3 = (f32[152,256]{1,0:T(8,128)S(1)}, f32[152,256]{1,0:T(8,128)S(1)}, u32[]{:S(2)}, u32[]{:S(2)}) collective-permute-start(f32[152,256]{1,0:T(8,128)S(1)} %get-tuple-element.46.rest_0_), channel_id=1, source_target_pairs={{0,8},{1,9},{2,10},{3,11},{4,12},{5,13},{6,14},{7,15},{8,0},{9,1},... | collective-permute-start | bytes 466952 | tf_op jit(solution)/shard_map/ppermute | solution.py:730
  68.4 7.1 %collective-permute-start.5 = (f32[152,256]{1,0:T(8,128)S(1)}, f32[152,256]{1,0:T(8,128)S(1)}, u32[]{:S(2)}, u32[]{:S(2)}) collective-permute-start(f32[152,256]{1,0:T(8,128)S(1)} %collective-permute-done.4.rest_2_), channel_id=1, source_target_pairs={{0,8},{1,9},{2,10},{3,11},{4,12},{5,13},{6,14},{7,15},{8,0},{9,1},... | collective-permute-start | bytes 466952 | tf_op jit(solution)/shard_map/ppermute | solution.py:730
  68.9 10.6 %collective-permute-start.6 = (f32[144,256]{1,0:T(8,128)S(1)}, f32[144,256]{1,0:T(8,128)S(1)}, u32[]{:S(2)}, u32[]{:S(2)}) collective-permute-start(f32[144,256]{1,0:T(8,128)S(1)} %get-tuple-element.43), channel_id=1, source_target_pairs={{0,8},{1,9},{2,10},{3,11},{4,12},{5,13},{6,14},{7,15},{8,0},{9,1},... | collective-permute-start | bytes 442376 | tf_op jit(solution)/shard_map/ppermute | solution.py:730
  71.0 12.1 %collective-permute-start.7 = (f32[144,256]{1,0:T(8,128)S(1)}, f32[144,256]{1,0:T(8,128)S(1)}, u32[]{:S(2)}, u32[]{:S(2)}) collective-permute-start(f32[144,256]{1,0:T(8,128)S(1)} %get-tuple-element.44), channel_id=1, source_target_pairs={{0,16},{1,17},{2,18},{3,19},{4,20},{5,21},{6,22},{7,23},{8,24},{9,... | collective-permute-start | bytes 442376 | tf_op jit(solution)/shard_map/ppermute | solution.py:730
  72.0 11.1 %collective-permute-start.8 = (f32[144,256]{1,0:T(8,128)S(1)}, f32[144,256]{1,0:T(8,128)S(1)}, u32[]{:S(2)}, u32[]{:S(2)}) collective-permute-start(f32[144,256]{1,0:T(8,128)S(1)} %get-tuple-element.45), channel_id=1, source_target_pairs={{0,24},{1,25},{2,26},{3,27},{4,28},{5,29},{6,30},{7,31},{8,16},{9,... | collective-permute-start | bytes 442376 | tf_op jit(solution)/shard_map/ppermute | solution.py:730
  84.7 4.5 %copy-start = (bf16[1024,32]{1,0:T(8,128)(2,1)S(1)}, bf16[1024,32]{1,0:T(8,128)(2,1)}, u32[]{:S(2)}) copy-start(bf16[1024,32]{1,0:T(8,128)(2,1)} %constant.34.clone.gather_ref) | copy-start | bytes 196612
  84.7 4.5 %copy-start.1 = (bf16[32,1024]{1,0:T(8,128)(2,1)S(1)}, bf16[32,1024]{1,0:T(8,128)(2,1)}, u32[]{:S(2)}) copy-start(bf16[32,1024]{1,0:T(8,128)(2,1)} %constant.33.clone.spread_ref) | copy-start | bytes 196612
  84.7 27.3 %all-to-all-start.2 = ((f32[8,200,256]{2,1,0:T(8,128)}), f32[8,200,256]{2,1,0:T(8,128)}, u32[]{:S(2)}, u32[]{:S(2)}) async-start(f32[8,200,256]{2,1,0:T(8,128)} %bitcast.8), calls=%async_computation.2 | async-start | bytes 3276800 | tf_op jit(solution)/shard_map/all_to_all | solution.py:736
  89.2 1.7 %copy-start.4 = (bf16[2,24,24,1024]{3,2,1,0:T(8,128)(2,1)S(1)}, bf16[2,24,24,1024]{3,2,1,0:T(8,128)(2,1)}, u32[]{:S(2)}) copy-start(bf16[2,24,24,1024]{3,2,1,0:T(8,128)(2,1)} %pack_weight.1.w_ref) | copy-start | bytes 7077892
  94.9 10.2 %collective-permute-start.10 = (f32[144,256]{1,0:T(8,128)S(1)}, f32[144,256]{1,0:T(8,128)S(1)}, u32[]{:S(2)}, u32[]{:S(2)}) collective-permute-start(f32[144,256]{1,0:T(8,128)S(1)} %get-tuple-element.51.rest_0_), channel_id=1, source_target_pairs={{0,16},{1,17},{2,18},{3,19},{4,20},{5,21},{6,22},{7,23},{8,24},{9,... | collective-permute-start | bytes 442376 | tf_op jit(solution)/shard_map/ppermute | solution.py:730
  96.7 8.4 %collective-permute-start.9 = (f32[144,256]{1,0:T(8,128)S(1)}, f32[144,256]{1,0:T(8,128)S(1)}, u32[]{:S(2)}, u32[]{:S(2)}) collective-permute-start(f32[144,256]{1,0:T(8,128)S(1)} %get-tuple-element.51.rest_0_), channel_id=1, source_target_pairs={{0,8},{1,9},{2,10},{3,11},{4,12},{5,13},{6,14},{7,15},{8,0},{9,1},... | collective-permute-start | bytes 442376 | tf_op jit(solution)/shard_map/ppermute | solution.py:730
  105.1 5.3 %collective-permute-start.11 = (f32[144,256]{1,0:T(8,128)S(1)}, f32[144,256]{1,0:T(8,128)S(1)}, u32[]{:S(2)}, u32[]{:S(2)}) collective-permute-start(f32[144,256]{1,0:T(8,128)S(1)} %collective-permute-done.10.rest_2_), channel_id=1, source_target_pairs={{0,8},{1,9},{2,10},{3,11},{4,12},{5,13},{6,14},{7,15},{8,0},{9,1},... | collective-permute-start | bytes 442376 | tf_op jit(solution)/shard_map/ppermute | solution.py:730
  112.0 25.4 %all-to-all-start.3 = ((f32[8,192,256]{2,1,0:T(8,128)}), f32[8,192,256]{2,1,0:T(8,128)}, u32[]{:S(2)}, u32[]{:S(2)}) async-start(f32[8,192,256]{2,1,0:T(8,128)} %bitcast.10), calls=%async_computation.3 | async-start | bytes 3145728 | tf_op jit(solution)/shard_map/all_to_all | solution.py:736
